TPU v7x, 32 devices: a whole 2x2x4 slice. The times are simulated.
32 devices in a mesh: seq: 4 (over z), batch: 4 (over y, x), mp: 2 (over core).
Axes of the slice: x: 2, y: 2, z: 4, core: 2. Of those that a mesh axis runs over, the one named last changes fastest.
Arguments:
- tokens_in: bfloat16 [8, 1024, 2048], P('batch', 'seq'), may hold values from -6 to 6
- grad_out: bfloat16 [8, 1024, 2048], P('batch', 'seq'), may hold values from -6 to 6
- w_input: bfloat16 [2048, 2048], P(('seq', 'batch'), 'mp'), may hold values from -0.125 to 0.125
- w_forget: bfloat16 [2048, 2048], P(('seq', 'batch'), 'mp'), may hold values from -0.125 to 0.125
- w_outgate: bfloat16 [2048, 2048], P(('seq', 'batch'), 'mp'), may hold values from -0.125 to 0.125
- w_out: bfloat16 [2048, 2048], P('mp', ('seq', 'batch')), may hold values from -0.25 to 0.25
- mlp_gate: bfloat16 [2048, 5632], P(('seq', 'batch'), 'mp'), may hold values from -0.125 to 0.125
- mlp_up: bfloat16 [2048, 5632], P(('seq', 'batch'), 'mp'), may hold values from -0.125 to 0.125
- mlp_down: bfloat16 [5632, 2048], P('mp', ('seq', 'batch')), may hold values from -0.15625 to 0.15625
- gain_mixer: bfloat16 [2048], replicated, may hold values from 0.25 to 1.75
- gain_mlp: bfloat16 [2048], replicated, may hold values from 0.25 to 1.75
- gain_state: bfloat16 [2048], P('mp'), may hold values from 0.25 to 1.75
- bound_param: float32 [24, 2048], P(None, 'mp'), may hold values from -12 to 2
- layer_index: int32 [1], replicated, may hold values from 18 to 23
- doc_lengths: int32 [8, 4], P('batch'), may hold values from 1 to 1024, as said below
Outputs:
- tokens_out: bfloat16 [8, 1024, 2048], P('batch', 'seq', 'mp')
- grad_in: float32 [8, 1024, 2048], P('batch', 'seq')
- grad_w_input: float32 [2048, 2048], P(('seq', 'batch'), 'mp')
- grad_w_forget: float32 [2048, 2048], P(('seq', 'batch'), 'mp')
- grad_w_outgate: float32 [2048, 2048], P(('seq', 'batch'), 'mp')
- grad_w_out: float32 [2048, 2048], P('mp', ('seq', 'batch'))
- grad_mlp_gate: float32 [2048, 5632], P(('seq', 'batch'), 'mp')
- grad_mlp_up: float32 [2048, 5632], P(('seq', 'batch'), 'mp')
- grad_mlp_down: float32 [5632, 2048], P('mp', ('seq', 'batch'))
- grad_gain_mixer: float32 [2048], P('mp')
- grad_gain_mlp: float32 [2048], P('mp')
- grad_gain_state: float32 [2048], P('mp')
- grad_bound_param: float32 [24, 2048], P(None, 'mp')
Inputs may be any that keep to these rules, and one draw needn't show every extreme that they name: `doc_lengths`: each row's lengths sum to 1024; in every row one document starts within the row's first 256 tokens and ends within its last 256.
All inputs are finite; a program needn't handle non-finite values.
Results may differ from a plain program's by a relative error of at most 0.013.
Values may be sent and summed in bfloat16 or wider, within the bound.
No kernel may reach another device: no remote copies, remote signals or barrier semaphores. Data moves between devices by JAX's collectives and lax.ppermute only.
A program may use at most 256 MiB of HBM per device.

v0:
```python
import jax
import jax.numpy as jnp
from jax import lax
from jax.sharding import PartitionSpec as P

EPSILON = 1e-06


def entering(x, axis, combine, identity, reverse):
    peers, place = (lax.axis_size(axis), lax.axis_index(axis))
    everything = jax.tree.map(lambda part: lax.all_gather(part, axis), x)
    start = jax.tree.map(
        lambda part, zero: jnp.broadcast_to(jnp.asarray(zero, part.dtype), part.shape), x, identity
    )

    def lap(k, before):
        at = peers - 1 - k if reverse else k
        reached = at > place if reverse else at < place
        new = combine(before, jax.tree.map(lambda part: part[at], everything))
        return jax.tree.map(lambda a, b: jnp.where(reached, a, b), new, before)

    return lax.fori_loop(0, peers, lap, start)


def lower_bound(bound_param, layer_index):
    weights = jax.nn.softmax(bound_param, axis=0)
    running = jnp.cumsum(weights, axis=0)
    return lax.dynamic_index_in_dim(running, layer_index[0], 0, keepdims=False) - weights[0]


def link(earlier, later):
    return (earlier[0] * later[0], later[0] * earlier[1] + later[1])


def plain_dot(left, right):
    return jnp.dot(left, right, preferred_element_type=jnp.float32)


def left_dot(left, right):
    return lax.dot_general(
        left, right, (((0,), (0,)), ((), ())), preferred_element_type=jnp.float32
    )


def right_dot(left, right):
    return lax.dot_general(
        left, right, (((1,), (1,)), ((), ())), preferred_element_type=jnp.float32
    )


def norm_back(upstream, values, scale, inverse):
    weighted = upstream * scale
    return inverse * weighted - values * inverse**3 * jnp.mean(
        weighted * values, axis=-1, keepdims=True
    )


def shards(
    tokens_in,
    grad_out,
    w_input,
    w_forget,
    w_outgate,
    w_out,
    mlp_gate,
    mlp_up,
    mlp_down,
    gain_mixer,
    gain_mlp,
    gain_state,
    bound_param,
    layer_index,
    doc_lengths,
):
    rows, seg, width = tokens_in.shape
    count = rows * seg
    half = gain_state.shape[0]
    own_part = lax.axis_index("mp")
    seq_place = lax.axis_index("seq")
    w_in_all, w_forget_all, w_gate_all, w_out_all, gate_all, up_all, down_all = (
        lax.all_gather(w_input, ("seq", "batch"), axis=0, tiled=True),
        lax.all_gather(w_forget, ("seq", "batch"), axis=0, tiled=True),
        lax.all_gather(w_outgate, ("seq", "batch"), axis=0, tiled=True),
        lax.all_gather(w_out, ("seq", "batch"), axis=1, tiled=True),
        lax.all_gather(mlp_gate, ("seq", "batch"), axis=0, tiled=True),
        lax.all_gather(mlp_up, ("seq", "batch"), axis=0, tiled=True),
        lax.all_gather(mlp_down, ("seq", "batch"), axis=1, tiled=True),
    )
    bound = lower_bound(bound_param, layer_index)
    gain_one = gain_mixer.astype(jnp.float32)
    gain_two = gain_mlp.astype(jnp.float32)
    gain_three = gain_state.astype(jnp.float32)
    starts = jnp.cumsum(doc_lengths, axis=1) - doc_lengths
    places = seq_place * seg + jnp.arange(seg, dtype=jnp.int32)
    resets = jnp.any(places[None, :, None] == starts[:, None, :], axis=2).astype(jnp.float32)
    keep_mask = (1.0 - resets)[:, :, None]
    tok_float = tokens_in.reshape(count, width).astype(jnp.float32)
    inv_one = lax.rsqrt(jnp.mean(tok_float * tok_float, axis=-1, keepdims=True) + EPSILON)
    normed_in = (tok_float * inv_one * gain_one).astype(jnp.bfloat16)
    proj_in = plain_dot(normed_in, w_in_all).reshape(rows, seg, half)
    proj_forget = plain_dot(normed_in, w_forget_all).reshape(rows, seg, half)
    proj_gate = plain_dot(normed_in, w_gate_all).reshape(rows, seg, half)
    sig_forget = jax.nn.sigmoid(proj_forget)
    forget = bound + (1.0 - bound) * sig_forget
    sig_in = jax.nn.sigmoid(proj_in)
    act_in = proj_in * sig_in
    inputs = act_in * (1.0 - forget)
    decay = forget * keep_mask
    cum_decay, local_state = lax.associative_scan(link, (decay, inputs), axis=1)
    unity = jnp.ones((rows, half), jnp.float32)
    nothing = jnp.zeros((rows, half), jnp.float32)
    carried = entering((cum_decay[:, -1], local_state[:, -1]), "seq", link, (unity, nothing), False)
    carry_in = carried[1]
    state = local_state + cum_decay * carry_in[:, None, :]
    square_total = lax.psum(jnp.sum(state * state, axis=-1), "mp")
    inv_state = lax.rsqrt(square_total / width + EPSILON)[:, :, None]
    sig_gate = jax.nn.sigmoid(proj_gate)
    act_gate = proj_gate * sig_gate
    state_normed = state * inv_state
    gated = (state_normed * gain_three * act_gate).astype(jnp.bfloat16).reshape(count, half)
    mixed = lax.psum(plain_dot(gated, w_out_all), "mp")
    resid = tok_float + mixed
    inv_two = lax.rsqrt(jnp.mean(resid * resid, axis=-1, keepdims=True) + EPSILON)
    normed_mlp = (resid * inv_two * gain_two).astype(jnp.bfloat16)
    gate_act = plain_dot(normed_mlp, gate_all)
    up_act = plain_dot(normed_mlp, up_all)
    sig_act = jax.nn.sigmoid(gate_act)
    silu_act = gate_act * sig_act
    hidden = (silu_act * up_act).astype(jnp.bfloat16)
    mlp_term = plain_dot(hidden, down_all).reshape(rows, seg, width)
    mlp_share = lax.psum_scatter(
        mlp_term.astype(jnp.bfloat16), "mp", scatter_dimension=2, tiled=True
    ).astype(jnp.float32)
    resid_own = lax.dynamic_slice_in_dim(resid.reshape(rows, seg, width), own_part * half, half, 2)
    tokens_out = (resid_own + mlp_share).astype(jnp.bfloat16)
    cot_rows = grad_out.reshape(count, width)
    grad_down = left_dot(hidden, cot_rows)
    d_hidden = right_dot(cot_rows, down_all)
    d_gate = (d_hidden * up_act * sig_act * (1.0 + gate_act * (1.0 - sig_act))).astype(jnp.bfloat16)
    d_up = (d_hidden * silu_act).astype(jnp.bfloat16)
    grad_gate = left_dot(normed_mlp, d_gate)
    grad_up = left_dot(normed_mlp, d_up)
    d_normed_mlp = lax.psum(right_dot(d_gate, gate_all) + right_dot(d_up, up_all), "mp")
    gain_two_full = jnp.sum(d_normed_mlp * resid * inv_two, axis=0)
    d_resid = cot_rows.astype(jnp.float32) + norm_back(d_normed_mlp, resid, gain_two, inv_two)
    d_resid_low = d_resid.astype(jnp.bfloat16)
    grad_wout = left_dot(gated, d_resid_low)
    d_gated = right_dot(d_resid_low, w_out_all).reshape(rows, seg, half)
    gain_three_grad = jnp.sum(d_gated * state_normed * act_gate, axis=(0, 1))
    d_proj_gate = (
        d_gated * state_normed * gain_three * sig_gate * (1.0 + proj_gate * (1.0 - sig_gate))
    ).astype(jnp.bfloat16)
    d_normed_state = d_gated * gain_three * act_gate
    dot_total = lax.psum(jnp.sum(d_normed_state * state, axis=-1), "mp")
    d_state = inv_state * d_normed_state - state * inv_state**3 * (dot_total / width)[:, :, None]
    next_decay = jnp.concatenate([decay[:, 1:], jnp.ones((rows, 1, half), jnp.float32)], axis=1)
    back_prod, back_local = lax.associative_scan(
        link, (jnp.flip(next_decay, 1), jnp.flip(d_state, 1)), axis=1
    )
    back_prod = jnp.flip(back_prod, 1)
    back_local = jnp.flip(back_local, 1)
    first_decay = decay[:, 0]
    returned = entering(
        (first_decay * back_prod[:, 0], first_decay * back_local[:, 0]),
        "seq",
        link,
        (unity, nothing),
        True,
    )
    lam = back_local + back_prod * returned[1][:, None, :]
    previous = jnp.concatenate([carry_in[:, None, :], state[:, :-1]], axis=1)
    d_forget = lam * (previous * keep_mask - act_in)
    d_proj_in = (lam * (1.0 - forget) * sig_in * (1.0 + proj_in * (1.0 - sig_in))).astype(
        jnp.bfloat16
    )
    d_proj_forget = (d_forget * (1.0 - bound) * sig_forget * (1.0 - sig_forget)).astype(
        jnp.bfloat16
    )
    bound_grad = jnp.sum(d_forget * (1.0 - sig_forget), axis=(0, 1))
    d_proj_in = d_proj_in.reshape(count, half)
    d_proj_forget = d_proj_forget.reshape(count, half)
    d_proj_gate = d_proj_gate.reshape(count, half)
    grad_in_w = left_dot(normed_in, d_proj_in)
    grad_forget_w = left_dot(normed_in, d_proj_forget)
    grad_gate_w = left_dot(normed_in, d_proj_gate)
    d_normed_in = lax.psum(
        (
            right_dot(d_proj_in, w_in_all)
            + right_dot(d_proj_forget, w_forget_all)
            + right_dot(d_proj_gate, w_gate_all)
        ).astype(jnp.bfloat16),
        "mp",
    ).astype(jnp.float32)
    gain_one_full = jnp.sum(d_normed_in * tok_float * inv_one, axis=0)
    grad_tokens = d_resid + norm_back(d_normed_in, tok_float, gain_one, inv_one)
    summed = (
        lax.psum_scatter(grad_in_w, ("seq", "batch"), scatter_dimension=0, tiled=True),
        lax.psum_scatter(grad_forget_w, ("seq", "batch"), scatter_dimension=0, tiled=True),
        lax.psum_scatter(grad_gate_w, ("seq", "batch"), scatter_dimension=0, tiled=True),
        lax.psum_scatter(grad_wout, ("seq", "batch"), scatter_dimension=1, tiled=True),
        lax.psum_scatter(grad_gate, ("seq", "batch"), scatter_dimension=0, tiled=True),
        lax.psum_scatter(grad_up, ("seq", "batch"), scatter_dimension=0, tiled=True),
        lax.psum_scatter(grad_down, ("seq", "batch"), scatter_dimension=1, tiled=True),
    )
    gain_one_own = lax.dynamic_slice_in_dim(gain_one_full, own_part * half, half, 0)
    gain_two_own = lax.dynamic_slice_in_dim(gain_two_full, own_part * half, half, 0)
    small = lax.psum((gain_one_own, gain_two_own, gain_three_grad, bound_grad), ("seq", "batch"))
    bound_value, bound_pull = jax.vjp(lambda table: lower_bound(table, layer_index), bound_param)
    grad_table = bound_pull(small[3])[0]
    return (
        tokens_out,
        grad_tokens.reshape(rows, seg, width),
        summed[0],
        summed[1],
        summed[2],
        summed[3],
        summed[4],
        summed[5],
        summed[6],
        small[0],
        small[1],
        small[2],
        grad_table,
    )


def solution(mesh):
    return jax.shard_map(
        shards,
        mesh=mesh,
        in_specs=(
            P("batch", "seq", None),
            P("batch", "seq", None),
            P(("seq", "batch"), "mp"),
            P(("seq", "batch"), "mp"),
            P(("seq", "batch"), "mp"),
            P("mp", ("seq", "batch")),
            P(("seq", "batch"), "mp"),
            P(("seq", "batch"), "mp"),
            P("mp", ("seq", "batch")),
            P(),
            P(),
            P("mp"),
            P(None, "mp"),
            P(),
            P("batch", None),
        ),
        out_specs=(
            P("batch", "seq", "mp"),
            P("batch", "seq", None),
            P(("seq", "batch"), "mp"),
            P(("seq", "batch"), "mp"),
            P(("seq", "batch"), "mp"),
            P("mp", ("seq", "batch")),
            P(("seq", "batch"), "mp"),
            P(("seq", "batch"), "mp"),
            P("mp", ("seq", "batch")),
            P("mp"),
            P("mp"),
            P("mp"),
            P(None, "mp"),
        ),
        check_vma=False,
    )
```

profile of v0, /device:TPU:0, one launch (start us, length us, event | category | flops | bytes accessed | tf_op | source)
XLA Modules:
  0.0 3459.3 jit_solution(11459162344154066813)
XLA Ops:
  17.9 71.7 %all-gather.12.cloned.1.call-done = bf16[2048,1024]{1,0:T(8,128)(2,1)} async-done(((bf16[128,1024]{1,0:T(8,128)(2,1)}), bf16[2048,1024]{1,0:T(8,128)(2,1)}) %all-gather.12.cloned.1.call-update) | async-done | bytes 4194320 | tf_op jit(solution)/shard_map/all_gather | solution.py:81
  89.6 5.9 fusion.14
  95.5 71.6 %all-gather.14.cloned.1.call-done = bf16[2048,1024]{1,0:T(8,128)(2,1)} async-done(((bf16[128,1024]{1,0:T(8,128)(2,1)}), bf16[2048,1024]{1,0:T(8,128)(2,1)}) %all-gather.14.cloned.1.call-update) | async-done | bytes 4194320 | tf_op jit(solution)/shard_map/all_gather | solution.py:82
  167.1 7.7 subtract_multiply_fusion
  174.8 5.4 slice.505
  180.2 5.4 slice.509
  185.6 5.4 slice.506
  191.0 5.4 slice.507
  273.3 5.6 slice.504
  278.9 5.6 slice.561
  323.3 5.3 pad.215
  333.0 13.6 all-gather.1
  349.1 5.6 pad.231
  359.0 13.1 all-gather
  372.4 5.4 multiply_reduce_fusion.6
  380.3 6.9 multiply_convert_fusion.7
  387.1 6.9 fusion.71
  396.3 25.1 all-reduce.72.cloned.1.call-done
  426.6 141.1 %all-gather.20.cloned.1.call-done = bf16[2048,2816]{1,0:T(8,128)(2,1)} async-done(((bf16[128,2816]{1,0:T(8,128)(2,1)}), bf16[2048,2816]{1,0:T(8,128)(2,1)}) %all-gather.20.cloned.1.call-update) | async-done | bytes 11534352 | tf_op jit(solution)/shard_map/all_gather | solution.py:85
  567.7 11.3 fusion.72
  579.0 132.2 %all-gather.22.cloned.1.call-done = bf16[2048,2816]{1,0:T(8,128)(2,1)} async-done(((bf16[128,2816]{1,0:T(8,128)(2,1)}), bf16[2048,2816]{1,0:T(8,128)(2,1)}) %all-gather.22.cloned.1.call-update) | async-done | bytes 11534352 | tf_op jit(solution)/shard_map/all_gather | solution.py:86
  711.2 11.1 fusion.73
  722.3 172.8 %all-gather.24.cloned.1.call-done = bf16[2816,2048]{1,0:T(8,128)(2,1)} async-done(((bf16[2816,128]{1,0:T(8,128)(2,1)}), bf16[2816,2048]{1,0:T(8,128)(2,1)}) %all-gather.24.cloned.1.call-update) | async-done | bytes 11534352 | tf_op jit(solution)/shard_map/all_gather | solution.py:87
  895.0 16.7 multiply_convert_fusion
  911.7 10.0 fusion.74
  921.8 7.7 convolution_add_fusion
  938.7 8.9 slice.584
  947.5 5.2 slice.591
  952.7 5.3 slice.582
  958.0 10.9 convolution_convert_fusion
  969.0 5.2 multiply_reduce_fusion
  988.8 4.3 multiply_subtract_fusion
  993.2 5.8 slice.585
  998.9 4.1 slice.587
  1003.0 8.9 slice.586
  1011.9 5.3 slice.588
  1097.3 5.4 slice.643
  1129.6 5.3 pad.264
  1145.4 5.4 pad.248
  1150.8 8.9 slice.644
  1159.7 4.1 add_multiply_fusion
  1168.8 3.7 pad.263
  1172.5 4.2 add.609
  1179.4 13.1 all-gather.2
  1192.7 13.1 all-gather.3
  1205.9 16.8 rev.10
  1222.7 16.7 rev.9
  1239.6 4.5 multiply_reduce_fusion.3
  1257.3 7.0 convolution_bitcast_fusion.1
  1264.4 7.0 convolution_bitcast_fusion.2
  1271.7 8.5 fusion.29
  1280.3 5.8 convolution_bitcast_fusion
  1286.1 13.0 fusion.77
  1299.2 13.2 fusion.78
  1312.7 13.1 fusion.79
  1333.1 74.7 %all-reduce.67 = (f32[1024]{0:T(1024)}, f32[1024]{0:T(1024)}, f32[1024]{0:T(1024)}, f32[1024]{0:T(1024)S(1)}) all-reduce(f32[1024]{0:T(1024)S(1)} %dynamic_slice.49, f32[1024]{0:T(1024)S(1)} %dynamic_slice.50, f32[1024]{0:T(1024)S(1)} %copy-done.83, ...), channel_id=1, replica_groups=mesh['seq'=4,'batch'=4,'mp'=2] {'seq','batch'}, use_global_device_ids=true, to_apply=%region_29.30 | all-reduce | flops 4096 | bytes 32768 | tf_op jit(solution)/shard_map/psum | solution.py:207
  1409.1 6.1 fusion.6
  1415.2 44.4 %reduce-scatter.13.cloned.1.call-done = f32[128,1024]{1,0:T(8,128)} async-done(((f32[2048,1024]{1,0:T(8,128)}), f32[128,1024]{1,0:T(8,128)}) %reduce-scatter.13.cloned.1.call-update) | async-done | bytes 524304 | tf_op jit(solution)/shard_map/reduce_scatter | solution.py:198
  1459.6 183.1 %reduce-scatter.11.cloned.1.call-done = f32[128,1024]{1,0:T(8,128)} async-done(((f32[2048,1024]{1,0:T(8,128)}), f32[128,1024]{1,0:T(8,128)}) %reduce-scatter.11.cloned.1.call-update) | async-done | bytes 524304 | tf_op jit(solution)/shard_map/reduce_scatter | solution.py:197
  1642.7 183.0 %reduce-scatter.17.cloned.1.call-done = f32[1024,128]{1,0:T(8,128)} async-done(((f32[1024,2048]{1,0:T(8,128)}), f32[1024,128]{1,0:T(8,128)}) %reduce-scatter.17.cloned.1.call-update) | async-done | bytes 524304 | tf_op jit(solution)/shard_map/reduce_scatter | solution.py:200
  1825.7 183.0 %reduce-scatter.15.cloned.1.call-done = f32[128,1024]{1,0:T(8,128)} async-done(((f32[2048,1024]{1,0:T(8,128)}), f32[128,1024]{1,0:T(8,128)}) %reduce-scatter.15.cloned.1.call-update) | async-done | bytes 524304 | tf_op jit(solution)/shard_map/reduce_scatter | solution.py:199
  2008.7 478.2 %reduce-scatter.19.cloned.1.call-done = f32[128,2816]{1,0:T(8,128)} async-done(((f32[2048,2816]{1,0:T(8,128)}), f32[128,2816]{1,0:T(8,128)}) %reduce-scatter.19.cloned.1.call-update) | async-done | bytes 1441808 | tf_op jit(solution)/shard_map/reduce_scatter | solution.py:201
  2486.9 482.5 %reduce-scatter.21.cloned.1.call-done = f32[128,2816]{1,0:T(8,128)} async-done(((f32[2048,2816]{1,0:T(8,128)}), f32[128,2816]{1,0:T(8,128)}) %reduce-scatter.21.cloned.1.call-update) | async-done | bytes 1441808 | tf_op jit(solution)/shard_map/reduce_scatter | solution.py:202
  2969.4 482.5 %reduce-scatter.23.cloned.1.call-done = f32[2816,128]{1,0:T(8,128)} async-done(((f32[2816,2048]{1,0:T(8,128)}), f32[2816,128]{1,0:T(8,128)}) %reduce-scatter.23.cloned.1.call-update) | async-done | bytes 1441808 | tf_op jit(solution)/shard_map/reduce_scatter | solution.py:203
  (545 shorter events, 317.5 us)
Async XLA Ops:
  7.2 82.5 %copy-start.3 = (bf16[2,256,2048]{2,1,0:T(8,128)(2,1)S(1)}, bf16[2,256,2048]{2,1,0:T(8,128)(2,1)}, u32[]{:S(2)}) copy-start(bf16[2,256,2048]{2,1,0:T(8,128)(2,1)} %param.19) | copy-start | bytes 6291460
  7.2 9.8 copy-start.88
  7.2 10.1 copy-start.89
  7.2 82.4 %all-gather.12.cloned.1.call-start = ((), (), s32[]{:S(2)}) async-start(), calls=%async_computation.8 | async-start | bytes 4456448 | tf_op jit(solution)/shard_map/all_gather | solution.py:81
  7.9 159.2 %all-gather.14.cloned.1.call-start = ((), (), s32[]{:S(2)}) async-start(), calls=%async_computation.9 | async-start | bytes 4456448 | tf_op jit(solution)/shard_map/all_gather | solution.py:82
  8.7 371.6 %all-gather.16.cloned.1.call-start = ((), (), s32[]{:S(2)}) async-start(), calls=%async_computation.10 | async-start | bytes 4456448 | tf_op jit(solution)/shard_map/all_gather | solution.py:83
  9.4 377.7 %all-gather.18.cloned.1.call-start = ((), (), s32[]{:S(2)}) async-start(), calls=%async_computation.11 | async-start | bytes 4456448 | tf_op jit(solution)/shard_map/all_gather | solution.py:84
  10.0 411.3 %all-reduce.72.cloned.1.call-start = ((), (), s32[]{:S(2)}) async-start(), calls=%async_computation.12 | async-start | bytes 8388608 | tf_op jit(solution)/shard_map/psum | solution.py:121
  13.7 153.5 %copy-start.57 = (f32[1,1024]{1,0:T(1,128)}, f32[1,1024]{1,0:T(1,128)S(1)}, u32[]{:S(2)}) copy-start(f32[1,1024]{1,0:T(1,128)S(1)} %slice_subtract_fusion) | copy-start | bytes 12292
  13.7 153.4 %copy-start.59 = (f32[1024]{0:T(1024)}, f32[1024]{0:T(1024)S(1)}, u32[]{:S(2)}) copy-start(f32[1024]{0:T(1024)S(1)} %broadcast_subtract_fusion) | copy-start | bytes 12292
  14.4 365.9 %copy-start.48 = (f32[2048]{0:T(1024)}, f32[2048]{0:T(1024)S(1)}, u32[]{:S(2)}) copy-start(f32[2048]{0:T(1024)S(1)} %convert_element_type.91) | copy-start | bytes 24580
  17.0 150.1 %copy-start.90 = (f32[2,256]{1,0:T(2,128)}, f32[2,256]{1,0:T(2,128)S(1)}, u32[]{:S(2)}) copy-start(f32[2,256]{1,0:T(2,128)S(1)} %get-tuple-element.391) | copy-start | bytes 6148
  17.3 149.8 %copy-start.84 = (f32[2,256]{1,0:T(2,128)}, f32[2,256]{1,0:T(2,128)S(1)}, u32[]{:S(2)}) copy-start(f32[2,256]{1,0:T(2,128)S(1)} %convert_subtract_fusion) | copy-start | bytes 6148
  273.2 14.1 copy-start.52
  273.2 14.1 copy-start.53
  273.2 14.1 copy-start.54
  273.2 14.1 copy-start.55
  273.3 14.2 copy-start.42
  273.3 14.2 copy-start.43
  273.3 14.5 copy-start.44
  273.3 14.5 copy-start.45
  278.9 9.0 copy-start.79
  278.9 9.1 copy-start.77
  278.9 9.3 copy-start.38
  278.9 9.3 copy-start.39
  278.9 9.3 copy-start.75
  278.9 9.4 copy-start.74
  303.8 7.1 copy-start.64
  328.6 18.1 copy-start.62
  372.4 7.9 copy-start.56
  372.4 7.9 copy-start.91
  387.1 6.9 copy-start.35
  394.1 173.6 %all-gather.20.cloned.1.call-start = ((), (), s32[]{:S(2)}) async-start(), calls=%async_computation.13 | async-start | bytes 12255232 | tf_op jit(solution)/shard_map/all_gather | solution.py:85
  394.7 316.5 %all-gather.22.cloned.1.call-start = ((), (), s32[]{:S(2)}) async-start(), calls=%async_computation.14 | async-start | bytes 12255232 | tf_op jit(solution)/shard_map/all_gather | solution.py:86
  395.4 499.6 %all-gather.24.cloned.1.call-start = ((), (), s32[]{:S(2)}) async-start(), calls=%async_computation.15 | async-start | bytes 12255232 | tf_op jit(solution)/shard_map/all_gather | solution.py:87
  396.2 572.7 %all-reduce.74.cloned.1.call-start = ((), (), s32[]{:S(2)}) async-start(), calls=%async_computation.17 | async-start | bytes 8388608 | tf_op jit(solution)/shard_map/psum | solution.py:143
  426.6 284.6 %copy-start.26 = (bf16[512,2048]{1,0:T(8,128)(2,1)}, bf16[512,2048]{1,0:T(8,128)(2,1)S(1)}, u32[]{:S(2)}) copy-start(bf16[512,2048]{1,0:T(8,128)(2,1)S(1)} %multiply_convert_fusion.3) | copy-start | bytes 6291460
  895.0 26.7 slice-start
  895.0 26.7 slice-start.1
  911.7 10.1 slice-start.2
  911.7 10.1 copy-start.97
  929.6 397.0 %reduce-scatter.9.cloned.1.call-start = ((), (), s32[]{:S(2)}) async-start(), calls=%async_computation.16 | async-start | bytes 3145728 | tf_op jit(solution)/shard_map/reduce_scatter | solution.py:131
  938.0 9.5 copy-start.22
  968.9 361.0 %all-reduce.76.cloned.1.call-start = ((), (), s32[]{:S(2)}) async-start(), calls=%async_computation.18 | async-start | bytes 4194304 | tf_op jit(solution)/shard_map/psum | solution.py:186
  968.9 5.9 copy-start.1
  969.0 7.2 copy-start.7
  1095.2 13.9 copy-start.40
  1095.2 13.9 copy-start.41
  1097.3 11.9 copy-start.81
  1097.3 12.1 copy-start.80
  1102.7 6.8 copy-start.37
  1222.7 16.9 copy-start.58
  1222.7 16.9 copy-start.60
  1222.7 16.9 copy-start.61
  1222.7 16.9 copy-start.85
  1255.7 203.9 %reduce-scatter.13.cloned.1.call-start = ((), (), s32[]{:S(2)}) async-start(), calls=%async_computation.20 | async-start | bytes 8912896 | tf_op jit(solution)/shard_map/reduce_scatter | solution.py:198
  1264.3 378.4 %reduce-scatter.11.cloned.1.call-start = ((), (), s32[]{:S(2)}) async-start(), calls=%async_computation.19 | async-start | bytes 8912896 | tf_op jit(solution)/shard_map/reduce_scatter | solution.py:197
  1271.4 554.3 %reduce-scatter.17.cloned.1.call-start = ((), (), s32[]{:S(2)}) async-start(), calls=%async_computation.22 | async-start | bytes 8912896 | tf_op jit(solution)/shard_map/reduce_scatter | solution.py:200
  1280.2 728.5 %reduce-scatter.15.cloned.1.call-start = ((), (), s32[]{:S(2)}) async-start(), calls=%async_computation.21 | async-start | bytes 8912896 | tf_op jit(solution)/shard_map/reduce_scatter | solution.py:199
  1286.1 1200.8 %reduce-scatter.19.cloned.1.call-start = ((), (), s32[]{:S(2)}) async-start(), calls=%async_computation.23 | async-start | bytes 24510464 | tf_op jit(solution)/shard_map/reduce_scatter | solution.py:201
  1299.2 1670.2 %reduce-scatter.21.cloned.1.call-start = ((), (), s32[]{:S(2)}) async-start(), calls=%async_computation.24 | async-start | bytes 24510464 | tf_op jit(solution)/shard_map/reduce_scatter | solution.py:202
  1312.4 2139.5 %reduce-scatter.23.cloned.1.call-start = ((), (), s32[]{:S(2)}) async-start(), calls=%async_computation.25 | async-start | bytes 24510464 | tf_op jit(solution)/shard_map/reduce_scatter | solution.py:203
  1329.9 78.5 %copy-start.25 = (f32[24,1024]{1,0:T(8,128)S(1)}, f32[24,1024]{1,0:T(8,128)}, u32[]{:S(2)}) copy-start(f32[24,1024]{1,0:T(8,128)} %param.31) | copy-start | bytes 294916
  1329.9 78.5 %copy-start.47 = (f32[1024]{0:T(1024)S(1)}, f32[1024]{0:T(1024)}, u32[]{:S(2)}) copy-start(f32[1024]{0:T(1024)} %copy-done.46) | copy-start | bytes 12292
  (55 other events, 151.8 us)
Sparse Core Ops, SparseCore 0:
  10.8 78.7 all-gather.11
  92.4 74.6 all-gather.13
  169.9 74.6 all-gather.15
  247.2 87.7 all-gather.17
  394.2 27.0 all-reduce.71
  424.3 143.3 all-gather.19
  570.8 140.3 all-gather.21
  714.3 180.7 all-gather.23
  929.7 26.6 all-reduce.73
  969.0 7.8 reduce-scatter.8
  1255.9 19.2 all-reduce.75
  1277.9 181.6 reduce-scatter.12
  1462.5 180.2 reduce-scatter.10
  1645.4 180.2 reduce-scatter.16
  1828.4 180.2 reduce-scatter.14
  2011.5 475.3 reduce-scatter.18
  2489.6 479.7 reduce-scatter.20
  2972.2 479.7 reduce-scatter.22
where the time goes:
time: 3480 us; the launch traced here: 3460 us
  waiting for transfers between devices  2660 us (76%)
  local copies, waits for them, and re-layouts  347 us (10%)
  matrix products  173 us (5%)
  blocking collectives  133 us (4%)
  other arithmetic  132 us (4%)
    reduce_scatter x1, waiting for transfers between devices, shards(): lax.psum_scatter(grad_down, ('seq', 'batch'), scatter_dimension=1, tiled=...  483 us
    reduce_scatter x1, waiting for transfers between devices, shards(): lax.psum_scatter(grad_up, ('seq', 'batch'), scatter_dimension=0, tiled=True)  483 us
    reduce_scatter x1, waiting for transfers between devices, shards(): lax.psum_scatter(grad_gate, ('seq', 'batch'), scatter_dimension=0, tiled=...  478 us
    reduce_scatter x1, waiting for transfers between devices, shards(): lax.psum_scatter(grad_in_w, ('seq', 'batch'), scatter_dimension=0, tiled=...  183 us
    reduce_scatter x1, waiting for transfers between devices, shards(): lax.psum_scatter(grad_gate_w, ('seq', 'batch'), scatter_dimension=0, tile...  183 us
    reduce_scatter x1, waiting for transfers between devices, shards(): lax.psum_scatter(grad_wout, ('seq', 'batch'), scatter_dimension=1, tiled=...  183 us
    all_gather x1, waiting for transfers between devices, shards(): lax.all_gather(mlp_down, ('seq', 'batch'), axis=1, tiled=True)  173 us
    all_gather x1, waiting for transfers between devices, shards(): lax.all_gather(mlp_gate, ('seq', 'batch'), axis=0, tiled=True)  141 us
  transfers between devices with their start and end apart: 18, of which 13 were waited for; matrix products, arithmetic and copies ran while one was open for 17% of the time, Pallas kernels for 0%

commit v1 on v0

v1 whole, which is shorter than its diff:
```python
import functools

import jax
import jax.numpy as jnp
from jax import lax
from jax.experimental import pallas as pl
from jax.experimental.pallas import tpu as pltpu
from jax.sharding import PartitionSpec as P

EPSILON = 1e-06
LOW = jnp.bfloat16


def swap_x(v):
    return lax.ppermute(v, "batch", [(i, i ^ 1) for i in range(4)])


def swap_y(v):
    return lax.ppermute(v, "batch", [(i, i ^ 2) for i in range(4)])


def swap_xy(v):
    return lax.ppermute(v, "batch", [(i, i ^ 3) for i in range(4)])


def swap_core(v):
    return lax.ppermute(v, "mp", [(0, 1), (1, 0)])


def plain_dot(left, right):
    return jnp.dot(left, right, preferred_element_type=jnp.float32)


def left_dot(left, right):
    return lax.dot_general(
        left, right, (((0,), (0,)), ((), ())), preferred_element_type=jnp.float32
    )


def right_dot(left, right):
    return lax.dot_general(
        left, right, (((1,), (1,)), ((), ())), preferred_element_type=jnp.float32
    )


def norm_back(upstream, values, scale, inverse):
    weighted = upstream * scale
    return inverse * weighted - values * inverse**3 * jnp.mean(
        weighted * values, axis=-1, keepdims=True
    )


def by_place(blocks, batch):
    stacked = jnp.stack(blocks)
    return [
        lax.dynamic_index_in_dim(stacked, jnp.bitwise_xor(batch, a), 0, keepdims=False)
        for a in range(4)
    ]


def exchange(blocks):
    return [blocks[0], swap_x(blocks[1]), swap_y(blocks[2]), swap_xy(blocks[3])]


def hidden_shard(weights, batch):
    places = [
        jnp.concatenate([w[:, a * (w.shape[1] // 4) : (a + 1) * (w.shape[1] // 4)] for w in weights], axis=1)
        for a in range(4)
    ]
    return jnp.concatenate(by_place(exchange(by_place(places, batch)), batch), axis=0)


def hidden_weights(weights, batch):
    return lax.all_gather(hidden_shard(weights, batch), "seq", axis=0, tiled=True)


def grad_shard(grad, batch):
    part = lax.psum_scatter(grad.astype(LOW), "seq", scatter_dimension=0, tiled=True)
    rows = part.shape[0] // 4
    places = [part[a * rows : (a + 1) * rows] for a in range(4)]
    return by_place(exchange(by_place(places, batch)), batch)


def columns_of(blocks, first, size):
    return jnp.concatenate([v[:, first : first + size] for v in blocks], axis=1).astype(jnp.float32)


def gather_rows(own, other):
    x_own, y_own = swap_x(own), swap_y(own)
    half = own.shape[0] // 2
    d_first = swap_y(x_own[:half])
    d_last = swap_x(y_own[half:])
    d_own = jnp.concatenate([d_first, d_last], axis=0)
    other = swap_core(own) if other is None else other
    groups = [(own, other)] + [(v, swap_core(v)) for v in (x_own, y_own, d_own)]
    return groups


def scatter_rows(make):
    sums = {}
    for group in (3, 1, 2, 0):
        away = swap_core(make(group, 1).astype(LOW))
        sums[group] = make(group, 0) + away.astype(jnp.float32)
    half = sums[3].shape[0] // 2
    diag = sums[3].astype(LOW)
    by_x = swap_x(diag[:half]).astype(jnp.float32)
    by_y = swap_y(diag[half:]).astype(jnp.float32)
    to_x = jnp.concatenate([sums[1][:half], sums[1][half:] + by_y], axis=0).astype(LOW)
    to_y = jnp.concatenate([sums[2][:half] + by_x, sums[2][half:]], axis=0).astype(LOW)
    return sums[0] + swap_x(to_x).astype(jnp.float32) + swap_y(to_y).astype(jnp.float32)


def sum_tokens(v):
    v = v.reshape(4, 2, -1)
    got = swap_core(v)
    v = v + jnp.stack([got[:, 1], got[:, 0]], axis=1)
    got = swap_x(v)
    v = v + jnp.stack([got[1], got[0], got[3], got[2]], axis=0)
    got = swap_y(v)
    v = v + jnp.stack([got[2], got[3], got[0], got[1]], axis=0)
    return v.reshape(8, -1)


def gather_tokens(v):
    v = jnp.stack([v, swap_core(v)])
    v = jnp.concatenate([v, swap_x(v)])
    return jnp.concatenate([v, swap_y(v)])


def sum_all(v, count):
    v = v + swap_x(v)
    v = v + swap_y(v)
    step = 1
    while step < count:
        v = v + lax.ppermute(v, "seq", [(i, i ^ step) for i in range(count)])
        step *= 2
    return v


def forward_kernel(seg, rows, decay_ref, input_ref, state_ref, product_ref):
    def body(t, carry):
        h, p = carry
        at = pl.ds(t, rows, stride=seg)
        d = decay_ref[at, :]
        h = d * h + input_ref[at, :]
        p = d * p
        state_ref[at, :] = h
        product_ref[at, :] = p
        return h, p

    first = pl.ds(0, rows, stride=seg)
    h, p = input_ref[first, :], decay_ref[first, :]
    state_ref[first, :] = h
    product_ref[first, :] = p
    lax.fori_loop(1, seg, body, (h, p), unroll=5)


def backward_kernel(seg, rows, decay_ref, input_ref, state_ref, product_ref):
    def body(k, carry):
        h, p, d = carry
        at = pl.ds(seg - 1 - k, rows, stride=seg)
        h = d * h + input_ref[at, :]
        p = d * p
        state_ref[at, :] = h
        product_ref[at, :] = p
        return h, p, decay_ref[at, :]

    last = pl.ds(seg - 1, rows, stride=seg)
    h, p = input_ref[last, :], decay_ref[last, :]
    state_ref[last, :] = h
    product_ref[last, :] = jnp.ones_like(p)
    at = pl.ds(seg - 2, rows, stride=seg)
    h = p * h + input_ref[at, :]
    state_ref[at, :] = h
    product_ref[at, :] = p
    lax.fori_loop(2, seg, body, (h, p, decay_ref[at, :]), unroll=2)


def scan_rows(kernel, decay, values, seg):
    count, width = decay.shape
    block = pl.BlockSpec((count, 128), lambda i: (0, i))
    return pl.pallas_call(
        functools.partial(kernel, seg, count // seg),
        grid=(width // 128,),
        in_specs=[block, block],
        out_specs=[block, block],
        out_shape=[jax.ShapeDtypeStruct((count, width), jnp.float32)] * 2,
        compiler_params=pltpu.CompilerParams(vmem_limit_bytes=32 * 1024 * 1024),
        cost_estimate=pl.CostEstimate(
            flops=3 * count * width, bytes_accessed=16 * count * width, transcendentals=0
        ),
    )(decay, values)


def enter(product, last, count, back):
    pair = jnp.stack([product, last])
    value = jnp.zeros_like(last)
    got = []
    for k in range(1, count):
        hops = [(i, i + k) for i in range(count - k)]
        if back:
            hops = [(b, a) for a, b in hops]
        got.append(lax.ppermute(pair, "seq", hops))
    for part in reversed(got):
        value = part[0] * value + part[1]
    return value


def shards(
    tokens_in,
    grad_out,
    w_input,
    w_forget,
    w_outgate,
    w_out,
    mlp_gate,
    mlp_up,
    mlp_down,
    gain_mixer,
    gain_mlp,
    gain_state,
    bound_param,
    layer_index,
    doc_lengths,
):
    rows, seg, width = tokens_in.shape
    half = gain_state.shape[0]
    chan = half // 4
    unit = mlp_gate.shape[1] // 4
    segments = lax.axis_size("seq")
    core = lax.axis_index("mp")
    batch = lax.axis_index("batch")
    place = lax.axis_index("seq")

    w_scan = hidden_weights((w_input, w_forget), batch)
    w_gates = hidden_weights((w_outgate, w_out.T), batch)
    w_mlp = hidden_weights((mlp_gate, mlp_up), batch)
    w_down = hidden_weights((mlp_down.T,), batch)
    w_gate, w_mix = w_gates[:, :chan], w_gates[:, chan:]

    own_table = lax.dynamic_slice_in_dim(bound_param, batch * chan, chan, 1)
    layers = bound_param.shape[0]
    layer = jnp.arange(layers, dtype=jnp.int32)[:, None]
    used = jnp.logical_and(layer >= 1, layer <= layer_index[0]).astype(jnp.float32)
    bound = jnp.sum(jax.nn.softmax(own_table, axis=0) * used, axis=0)
    lengths = jnp.where(core == 0, doc_lengths, doc_lengths[::-1])
    lengths = jnp.concatenate([lengths, swap_x(lengths), swap_y(lengths), swap_xy(lengths)])
    starts = jnp.cumsum(lengths, axis=1) - lengths
    places = place * seg + jnp.arange(seg, dtype=jnp.int32)
    resets = jnp.any(places[None, :, None] == starts[:, None, :], axis=2).astype(jnp.float32)
    keep_mask = (1.0 - resets).reshape(8 * seg, 1)

    gain_one = gain_mixer.astype(jnp.float32)
    gain_two = gain_mlp.astype(jnp.float32)
    gain_three = lax.dynamic_slice_in_dim(gain_state, batch * chan, chan, 0).astype(jnp.float32)

    def own_other(v):
        return (
            lax.dynamic_index_in_dim(v, core, 0, keepdims=False),
            lax.dynamic_index_in_dim(v, 1 - core, 0, keepdims=False),
        )

    tok_own, tok_other = own_other(tokens_in)
    cot_own, cot_other = own_other(grad_out)
    tok_own = tok_own.astype(jnp.float32)

    def normed(v, gain):
        inverse = lax.rsqrt(jnp.mean(v * v, axis=-1, keepdims=True) + EPSILON)
        return (v * inverse * gain).astype(LOW), inverse

    normed_own, inv_one = normed(tok_own, gain_one)
    normed_other, _ = normed(tok_other.astype(jnp.float32), gain_one)
    normed_in = jnp.concatenate(
        [v for group in gather_rows(normed_own, normed_other) for v in group], axis=0
    )
    cot_all = jnp.concatenate([v for group in gather_rows(cot_own, cot_other) for v in group], axis=0)

    proj_scan = plain_dot(normed_in, w_scan)
    proj_in, proj_forget = proj_scan[:, :chan], proj_scan[:, chan:]
    proj_gate = plain_dot(normed_in, w_gate)
    sig_forget = jax.nn.sigmoid(proj_forget)
    forget = bound + (1.0 - bound) * sig_forget
    sig_in = jax.nn.sigmoid(proj_in)
    act_in = proj_in * sig_in
    inputs = act_in * (1.0 - forget)
    decay = forget * keep_mask
    local_state, cum_decay = scan_rows(forward_kernel, decay, inputs, seg)

    def by_row(v):
        return v.reshape(8, seg, chan)

    carry_in = enter(by_row(cum_decay)[:, -1], by_row(local_state)[:, -1], segments, False)
    state = by_row(local_state) + by_row(cum_decay) * carry_in[:, None, :]
    previous = jnp.concatenate([carry_in[:, None, :], state[:, :-1]], axis=1).reshape(8 * seg, chan)
    square_total = sum_tokens(jnp.sum(state * state, axis=-1))
    inv_all = lax.rsqrt(square_total / width + EPSILON)
    inv_own = inv_all[0][:, None]
    inv_state = inv_all.reshape(8 * seg, 1)
    state = state.reshape(8 * seg, chan)
    sig_gate = jax.nn.sigmoid(proj_gate)
    act_gate = proj_gate * sig_gate
    gated_raw = (state * gain_three * act_gate).astype(LOW)

    def row_of(v, group, part):
        first = (2 * group + part) * seg
        return v[first : first + seg]

    mix_raw = scatter_rows(lambda g, p: right_dot(row_of(gated_raw, g, p), w_mix))
    resid = tok_own + inv_own * mix_raw

    normed_mlp_own, inv_two = normed(resid, gain_two)
    normed_mlp = jnp.concatenate(
        [v for group in gather_rows(normed_mlp_own, None) for v in group], axis=0
    )
    acts = plain_dot(normed_mlp, w_mlp)
    gate_act, up_act = acts[:, :unit], acts[:, unit:]
    sig_act = jax.nn.sigmoid(gate_act)
    silu_act = gate_act * sig_act
    hidden = (silu_act * up_act).astype(LOW)
    grad_down = grad_shard(left_dot(cot_all, hidden), batch)
    d_hidden = plain_dot(cot_all, w_down)
    d_gate = (d_hidden * up_act * sig_act * (1.0 + gate_act * (1.0 - sig_act))).astype(LOW)
    d_up = (d_hidden * silu_act).astype(LOW)
    d_acts = jnp.concatenate([d_gate, d_up], axis=1)
    d_normed_mlp = scatter_rows(lambda g, p: right_dot(row_of(d_acts, g, p), w_mlp))
    grad_mlp = grad_shard(left_dot(normed_mlp, d_acts), batch)
    mlp_own = scatter_rows(lambda g, p: right_dot(row_of(hidden, g, p), w_down))
    out_own = (resid + mlp_own).astype(LOW)

    gain_two_full = jnp.sum(d_normed_mlp * resid * inv_two, axis=0)
    d_resid = cot_own.astype(jnp.float32) + norm_back(d_normed_mlp, resid, gain_two, inv_two)
    d_resid_low = d_resid.astype(LOW)
    dot_own = jnp.sum(d_resid_low.astype(jnp.float32) * mix_raw, axis=-1)
    dot_total = gather_tokens(dot_own).reshape(8 * seg, 1)
    d_resid_all = jnp.concatenate(
        [v for group in gather_rows(d_resid_low, None) for v in group], axis=0
    )
    d_gated = plain_dot(d_resid_all, w_mix)
    state_normed = state * inv_state
    gated = (state_normed * gain_three * act_gate).astype(LOW)
    grad_mix = left_dot(d_resid_all, gated)
    gain_three_grad = jnp.sum(d_gated * state_normed * act_gate, axis=0)
    d_proj_gate = (
        d_gated * state_normed * gain_three * sig_gate * (1.0 + proj_gate * (1.0 - sig_gate))
    ).astype(LOW)
    d_normed_state = d_gated * gain_three * act_gate
    d_state = inv_state * d_normed_state - state * inv_state**3 * (dot_total / width)
    back_local, back_prod = scan_rows(backward_kernel, decay, d_state, seg)
    first_decay = by_row(decay)[:, 0]
    returned = enter(
        first_decay * by_row(back_prod)[:, 0],
        first_decay * by_row(back_local)[:, 0],
        segments,
        True,
    )
    lam = (by_row(back_local) + by_row(back_prod) * returned[:, None, :]).reshape(8 * seg, chan)
    d_forget = lam * (previous * keep_mask - act_in)
    d_proj_in = (lam * (1.0 - forget) * sig_in * (1.0 + proj_in * (1.0 - sig_in))).astype(LOW)
    d_proj_forget = (d_forget * (1.0 - bound) * sig_forget * (1.0 - sig_forget)).astype(LOW)
    bound_grad = jnp.sum(d_forget * (1.0 - sig_forget), axis=0)
    d_scan = jnp.concatenate([d_proj_in, d_proj_forget], axis=1)
    grad_gates = grad_shard(
        jnp.concatenate([left_dot(normed_in, d_proj_gate), grad_mix], axis=1), batch
    )
    grad_scan = grad_shard(left_dot(normed_in, d_scan), batch)
    d_normed_in = scatter_rows(
        lambda g, p: right_dot(row_of(d_scan, g, p), w_scan)
        + right_dot(row_of(d_proj_gate, g, p), w_gate)
    )
    gain_one_full = jnp.sum(d_normed_in * tok_own * inv_one, axis=0)
    grad_own = d_resid + norm_back(d_normed_in, tok_own, gain_one, inv_one)

    def both_rows(mine, got):
        return jnp.where(core == 0, jnp.stack([mine, got]), jnp.stack([got, mine]))

    out_halves = jnp.stack([out_own[:, :half], out_own[:, half:]])
    out_keep, out_send = own_other(out_halves)
    tokens_out = both_rows(out_keep, swap_core(out_send))
    grad_tokens = both_rows(grad_own, swap_core(grad_own))

    gains = jnp.stack([gain_one_full, gain_two_full]).reshape(2, 2, half)
    gains_keep = lax.dynamic_index_in_dim(gains, core, 1, keepdims=False)
    gains_send = lax.dynamic_index_in_dim(gains, 1 - core, 1, keepdims=False)
    channels = lax.dynamic_update_slice_in_dim(
        jnp.zeros((2, half), jnp.float32),
        jnp.stack([gain_three_grad, bound_grad]),
        batch * chan,
        1,
    )
    small = sum_all(jnp.concatenate([gains_keep + swap_core(gains_send), channels]), segments)
    soft = jax.nn.softmax(bound_param, axis=0)
    grad_table = small[3] * soft * (used - jnp.sum(soft * used, axis=0))
    return (
        tokens_out,
        grad_tokens,
        columns_of(grad_scan, 0, chan),
        columns_of(grad_scan, chan, chan),
        columns_of(grad_gates, 0, chan),
        columns_of(grad_gates, chan, chan).T,
        columns_of(grad_mlp, 0, unit),
        columns_of(grad_mlp, unit, unit),
        columns_of(grad_down, 0, unit).T,
        small[0],
        small[1],
        small[2],
        grad_table,
    )


def solution(mesh):
    return jax.shard_map(
        shards,
        mesh=mesh,
        in_specs=(
            P("batch", "seq", None),
            P("batch", "seq", None),
            P(("seq", "batch"), "mp"),
            P(("seq", "batch"), "mp"),
            P(("seq", "batch"), "mp"),
            P("mp", ("seq", "batch")),
            P(("seq", "batch"), "mp"),
            P(("seq", "batch"), "mp"),
            P("mp", ("seq", "batch")),
            P(),
            P(),
            P("mp"),
            P(None, "mp"),
            P(),
            P("batch", None),
        ),
        out_specs=(
            P("batch", "seq", "mp"),
            P("batch", "seq", None),
            P(("seq", "batch"), "mp"),
            P(("seq", "batch"), "mp"),
            P(("seq", "batch"), "mp"),
            P("mp", ("seq", "batch")),
            P(("seq", "batch"), "mp"),
            P(("seq", "batch"), "mp"),
            P("mp", ("seq", "batch")),
            P("mp"),
            P("mp"),
            P("mp"),
            P(None, "mp"),
        ),
        check_vma=False,
    )
```

time: 3480 us -> 723 us (0.21)
  waiting for transfers between devices: 2660 us -> 296 us
  local copies, waits for them, and re-layouts: 347 us -> 70.6 us
  blocking collectives: 133 us -> 0 us
  starting transfers between devices: 1.19 us -> 99.2 us
  other arithmetic: 132 us -> 66.6 us
    reduce_scatter x8 -> x4, waiting for transfers between devices: 2040 us -> 45 us  [grad_shard(): lax.psum_scatter(grad.astype(LOW), 'seq', scatter_dimension=0, tiled=True)]
    all_gather x7 -> x4, waiting for transfers between devices: 589 us -> 0.03 us  [hidden_weights(): lax.all_gather(hidden_shard(weights, batch), 'seq', axis=0, tiled=True)]
    ppermute x0 -> x108, waiting for transfers between devices: none -> 251 us  [the longest x28 121 us: swap_x(): return lax.ppermute(v, 'batch', [(i, i ^ 1) for i in range(4)])]
    slice x110 -> x42, local copies, waits for them, and re-layouts: 228 us -> 12.2 us  [the longest x4 4.33 us: gather_rows(): d_first = swap_y(x_own[:half])]
    ppermute x0 -> x108, starting transfers between devices: none -> 98.7 us  [the longest x28 29.3 us: swap_y(): return lax.ppermute(v, 'batch', [(i, i ^ 2) for i in range(4)])]
    psum x3 -> x0, blocking collectives: 79.6 us -> none  [the longest x1 74.7 us: shards(): lax.psum((gain_one_own, gain_two_own, gain_three_grad, bound_grad), ('seq...]
    pad x56 -> x0, local copies, waits for them, and re-layouts: 68.2 us -> none  [the longest x28 34.3 us: shards(): lax.associative_scan(link, (jnp.flip(next_decay, 1), jnp.flip(d_state, 1)...]
    all_gather x4 -> x0, blocking collectives: 53 us -> none  [entering(): everything = jax.tree.map(lambda part: lax.all_gather(part, axis), x)]
  transfers between devices with their start and end apart: 18 -> 116, of which waited for: 13 -> 51; matrix products, arithmetic and copies ran while one was open for 17% -> 35% of each run, Pallas kernels for 0% -> 2%
where the time goes in v1:
time: 723 us; the launch traced here: 714 us
  waiting for transfers between devices  296 us (41%)
  matrix products  151 us (21%)
  starting transfers between devices  99.2 us (14%)
  local copies, waits for them, and re-layouts  70.6 us (10%)
  other arithmetic  66.6 us (9%)
  between operations  17.6 us (2%)
  Pallas kernels  13 us (2%)
    ppermute x28, waiting for transfers between devices, swap_x(): return lax.ppermute(v, 'batch', [(i, i ^ 1) for i in range(4)])  121 us
    ppermute x28, waiting for transfers between devices, swap_y(): return lax.ppermute(v, 'batch', [(i, i ^ 2) for i in range(4)])  96.4 us
    dot_general x5, matrix products, plain_dot(): return jnp.dot(left, right, preferred_element_type=jnp.float32)  55.7 us
    dot_general x40, matrix products, right_dot(): lax.dot_general(left, right, (((1,), (1,)), ((), ())), preferred_element_...  52 us
    reduce_scatter x4, waiting for transfers between devices, grad_shard(): lax.psum_scatter(grad.astype(LOW), 'seq', scatter_dimension=0, tiled=True)  45 us
    dot_general x5, matrix products, left_dot(): lax.dot_general(left, right, (((0,), (0,)), ((), ())), preferred_element_...  43.7 us
    unnamed x187, local copies, waits for them, and re-layouts  42.9 us
    ppermute x28, starting transfers between devices, swap_y(): return lax.ppermute(v, 'batch', [(i, i ^ 2) for i in range(4)])  29.3 us
  transfers between devices with their start and end apart: 116, of which 51 were waited for; matrix products, arithmetic and copies ran while one was open for 35% of the time, Pallas kernels for 2%

profile of v1, /device:TPU:0, one launch (start us, length us, event | category | flops | bytes accessed | tf_op | source)
XLA Modules:
  0.0 714.2 jit_solution(15039062791378834296)
XLA Ops:
  9.4 4.0 collective-permute-start.9
  14.0 3.3 collective-permute-done.9
  17.2 2.4 collective-permute-done.8
  25.3 3.8 collective-permute-done.21
  40.9 4.9 collective-permute-done.40
  47.1 5.0 collective-permute-done.39
  72.9 12.5 %collective-permute-done = bf16[256,2048]{1,0:T(8,128)(2,1)} collective-permute-done((bf16[256,2048]{1,0:T(8,128)(2,1)}, bf16[256,2048]{1,0:T(8,128)(2,1)}, u32[]{:S(2)}, u32[]{:S(2)}) %collective-permute-start) | collective-permute-done | bytes 1048608 | tf_op jit(solution)/shard_map/ppermute | solution.py:15
  94.0 2.4 constant_dynamic-update-slice_fusion.6
  96.4 6.6 collective-permute-done.5
  110.4 7.5 %fusion.226 = f32[2048,512]{1,0:T(8,128)S(1)} fusion(bf16[2048,2048]{1,0:T(8,128)(2,1)} %constant_dynamic-update-slice_fusion, bf16[2048,512]{1,0:T(8,128)(2,1)} %all-gather.5.cloned.1.call-done), kind=kOutput, calls=%fused_computation.547 | convolution fusion | flops 4294967296 | bytes 14680064 | tf_op jit(solution)/shard_map/dot_general | solution.py:31
  119.9 6.0 shard_map.246
  127.9 5.5 collective-permute-start.15
  134.8 3.1 collective-permute-start.13
  142.3 8.8 %multiply_convert_fusion.8 = (bf16[2048,256]{1,0:T(8,128)(2,1)S(1)}, f32[2048,256]{1,0:T(8,128)S(1)}, f32[2048,256]{1,0:T(8,128)}) fusion(f32[256]{0:T(256)S(1)} %dynamic-slice_convert_fusion, f32[2048,256]{1,0:T(8,128)S(1)} %get-tuple-element.17, f32[2048,256]{1,0:T(8,128)} %copy-done.3, f32[8,256]{1,0:T(8,128)S(1)} %bitcast.375, ...), kind=kOutput, calls=%fused_computation.133 | convolution fusion | flops 2152202240 | bytes 18883584 | tf_op jit(solution)/shard_map/dot_general | solution.py:31
  163.4 11.1 %collective-permute-done.25 = bf16[128,2048]{1,0:T(8,128)(2,1)S(1)} collective-permute-done((bf16[128,2048]{1,0:T(8,128)(2,1)S(1)}, bf16[128,2048]{1,0:T(8,128)(2,1)S(1)}, u32[]{:S(2)}, u32[]{:S(2)}) %collective-permute-start.25) | collective-permute-done | bytes 524320 | tf_op jit(solution)/shard_map/ppermute | solution.py:19
  176.2 11.8 %collective-permute-done.28 = bf16[128,2048]{1,0:T(8,128)(2,1)S(1)} collective-permute-done((bf16[128,2048]{1,0:T(8,128)(2,1)S(1)}, bf16[128,2048]{1,0:T(8,128)(2,1)S(1)}, u32[]{:S(2)}, u32[]{:S(2)}) %collective-permute-start.28) | collective-permute-done | bytes 524320 | tf_op jit(solution)/shard_map/ppermute | solution.py:15
  191.8 2.3 constant_dynamic-update-slice_fusion.23
  196.1 17.7 %collective-permute-done.18 = f32[4,2,256]{2,1,0:T(2,128)S(1)} collective-permute-done((f32[4,2,256]{2,1,0:T(2,128)S(1)}, f32[4,2,256]{2,1,0:T(2,128)S(1)}, u32[]{:S(2)}, u32[]{:S(2)}) %collective-permute-start.18) | collective-permute-done | bytes 8224 | tf_op jit(solution)/shard_map/ppermute | solution.py:19
  215.9 4.5 multiply_reduce_fusion.5
  222.6 3.0 collective-permute-done.57
  233.8 13.4 %collective-permute-done.31 = bf16[256,2048]{1,0:T(8,128)(2,1)S(1)} collective-permute-done((bf16[256,2048]{1,0:T(8,128)(2,1)S(1)}, bf16[256,2048]{1,0:T(8,128)(2,1)S(1)}, u32[]{:S(2)}, u32[]{:S(2)}) %collective-permute-start.31) | collective-permute-done | bytes 1048608 | tf_op jit(solution)/shard_map/ppermute | solution.py:15
  249.1 3.5 collective-permute-done.33
  258.1 8.1 %collective-permute-done.36 = bf16[128,2048]{1,0:T(8,128)(2,1)S(1)} collective-permute-done((bf16[128,2048]{1,0:T(8,128)(2,1)S(1)}, bf16[128,2048]{1,0:T(8,128)(2,1)S(1)}, u32[]{:S(2)}, u32[]{:S(2)}) %collective-permute-start.36) | collective-permute-done | bytes 524320 | tf_op jit(solution)/shard_map/ppermute | solution.py:15
  273.8 19.1 %fusion.227 = f32[2048,1408]{0,1:T(8,128)} fusion(bf16[2048,2048]{1,0:T(8,128)(2,1)} %constant_dynamic-update-slice_fusion.8, bf16[2048,1408]{1,0:T(8,128)(2,1)} %all-gather.9.cloned.1.call-done), kind=kOutput, calls=%fused_computation.548 | convolution fusion | flops 11811160064 | bytes 25690112 | tf_op jit(solution)/shard_map/dot_general | solution.py:31
  292.9 15.5 %multiply_convert_fusion = (bf16[2048,704]{0,1:T(8,128)(2,1)S(1)}, bf16[2048,704]{0,1:T(8,128)(2,1)S(1)}, bf16[2048,704]{0,1:T(8,128)(2,1)S(1)}) fusion(f32[2048,1408]{0,1:T(8,128)} %fusion.227, bf16[2048,2048]{1,0:T(8,128)(2,1)} %constant_dynamic-update-slice_fusion.17, bf16[2048,704]{0,1:T(8,128)(2,1)} %all-gather.11.cloned.1.call-done), kind=kOutput, calls=%fused_computation.18 | convolution fusion | flops 5927206912 | bytes 31457280 | tf_op jit(solution)/shard_map/dot_general | solution.py:31
  308.4 2.5 convolution_convert_fusion.6
  329.9 2.2 add_convert_fusion.3
  342.4 5.4 collective-permute-done.47
  348.5 12.6 %collective-permute-done.66 = bf16[128,2048]{1,0:T(8,128)(2,1)S(1)} collective-permute-done((bf16[128,2048]{1,0:T(8,128)(2,1)}, bf16[128,2048]{1,0:T(8,128)(2,1)S(1)}, u32[]{:S(2)}, u32[]{:S(2)}) %collective-permute-start.66) | collective-permute-done | bytes 524320 | tf_op jit(solution)/shard_map/ppermute | solution.py:15
  369.1 2.1 fusion.83
  371.2 17.8 %collective-permute-done.67 = bf16[256,2048]{1,0:T(8,128)(2,1)} collective-permute-done((bf16[256,2048]{1,0:T(8,128)(2,1)S(1)}, bf16[256,2048]{1,0:T(8,128)(2,1)}, u32[]{:S(2)}, u32[]{:S(2)}) %collective-permute-start.67) | collective-permute-done | bytes 1048608 | tf_op jit(solution)/shard_map/ppermute | solution.py:19
  389.0 18.7 %collective-permute-done.64 = bf16[256,2048]{1,0:T(8,128)(2,1)} collective-permute-done((bf16[256,2048]{1,0:T(8,128)(2,1)S(1)}, bf16[256,2048]{1,0:T(8,128)(2,1)}, u32[]{:S(2)}, u32[]{:S(2)}) %collective-permute-start.64) | collective-permute-done | bytes 1048608 | tf_op jit(solution)/shard_map/ppermute | solution.py:15
  407.7 3.1 multiply_reduce_fusion.2
  410.9 5.0 multiply_reduce_fusion.3
  419.9 11.3 %convolution_convert_fusion.1 = bf16[2048,704]{0,1:T(8,128)(2,1)} fusion(bf16[2048,704]{0,1:T(8,128)(2,1)S(1)} %copy-done.44, bf16[2048,2048]{1,0:T(8,128)(2,1)} %constant_dynamic-update-slice_fusion.17), kind=kOutput, calls=%fused_computation.47 | convolution fusion | flops 5907021824 | bytes 14155776 | tf_op jit(solution)/shard_map/dot_general | solution.py:35
  431.2 12.0 %collective-permute-done.77 = f32[2,256]{1,0:T(2,128)S(1)} collective-permute-done((f32[2,256]{1,0:T(2,128)S(1)}, f32[2,256]{1,0:T(2,128)S(1)}, u32[]{:S(2)}, u32[]{:S(2)}) %collective-permute-start.77) | collective-permute-done | bytes 2080 | tf_op jit(solution)/shard_map/ppermute | solution.py:15
  450.8 8.4 %collective-permute-done.74 = bf16[128,2048]{1,0:T(8,128)(2,1)S(1)} collective-permute-done((bf16[128,2048]{1,0:T(8,128)(2,1)S(1)}, bf16[128,2048]{1,0:T(8,128)(2,1)S(1)}, u32[]{:S(2)}, u32[]{:S(2)}) %collective-permute-start.74) | collective-permute-done | bytes 524320 | tf_op jit(solution)/shard_map/ppermute | solution.py:15
  459.2 2.5 collective-permute-done.73
  465.3 4.8 multiply_subtract_fusion
  470.1 2.4 convolution_convert_fusion.12
  472.5 2.9 convolution_convert_fusion.11
  477.7 2.6 slice_add_fusion
  480.7 7.0 shard_map.247
  492.0 3.3 collective-permute-done.81
  496.1 2.4 multiply_reduce_fusion
  500.1 9.6 %convolution_convert_fusion.2 = bf16[2048,512]{1,0:T(8,128)(2,1)} fusion(bf16[2048,2048]{1,0:T(8,128)(2,1)} %constant_dynamic-update-slice_fusion, bf16[2048,256]{1,0:T(8,128)(2,1)S(1)} %multiply_convert_fusion.5, bf16[2048,256]{1,0:T(8,128)(2,1)S(1)} %get-tuple-element.77), kind=kOutput, calls=%fused_computation.48 | convolution fusion | flops 4300210176 | bytes 12582912 | tf_op jit(solution)/shard_map/dot_general | solution.py:35
  513.5 17.5 %convolution_convert_fusion = bf16[2048,1408]{1,0:T(8,128)(2,1)} fusion(bf16[2048,2048]{1,0:T(8,128)(2,1)} %constant_dynamic-update-slice_fusion.8, bf16[2048,704]{0,1:T(8,128)(2,1)S(1)} %copy-done.6, bf16[2048,704]{0,1:T(8,128)(2,1)S(1)} %copy-done.8), kind=kOutput, calls=%fused_computation.17 | convolution fusion | flops 11825577984 | bytes 19922944 | tf_op jit(solution)/shard_map/dot_general | solution.py:35
  531.1 2.5 maximum_select_fusion.1
  549.1 10.4 %collective-permute-done.88 = bf16[128,2048]{1,0:T(8,128)(2,1)S(1)} collective-permute-done((bf16[128,2048]{1,0:T(8,128)(2,1)S(1)}, bf16[128,2048]{1,0:T(8,128)(2,1)S(1)}, u32[]{:S(2)}, u32[]{:S(2)}) %collective-permute-start.88) | collective-permute-done | bytes 524320 | tf_op jit(solution)/shard_map/ppermute | solution.py:15
  564.5 2.1 convolution_add_fusion.7
  571.7 15.7 %collective-permute-done.89 = bf16[256,2048]{1,0:T(8,128)(2,1)} collective-permute-done((bf16[256,2048]{1,0:T(8,128)(2,1)}, bf16[256,2048]{1,0:T(8,128)(2,1)}, u32[]{:S(2)}, u32[]{:S(2)}) %collective-permute-start.89) | collective-permute-done | bytes 1048608 | tf_op jit(solution)/shard_map/ppermute | solution.py:19
  588.7 4.0 fusion.16
  596.9 2.0 collective-permute-done.104
  602.7 2.2 collective-permute-start.106
  604.9 4.1 collective-permute-done.106
  610.6 2.2 fusion.13
  612.8 4.5 collective-permute-done.107
  620.6 2.3 collective-permute-start.96
  625.3 2.4 collective-permute-start.93
  636.9 45.0 %reduce-scatter.9.cloned.1.call-done = bf16[512,1408]{1,0:T(8,128)(2,1)} async-done(((bf16[2048,1408]{1,0:T(8,128)(2,1)}), bf16[512,1408]{1,0:T(8,128)(2,1)}) %reduce-scatter.9.cloned.1.call-update) | async-done | bytes 1441808 | tf_op jit(solution)/shard_map/reduce_scatter | solution.py:78
  683.7 2.4 collective-permute-start.99
  688.1 4.9 maximum_select_fusion
  693.0 3.0 collective-permute-done.99
  696.0 6.6 collective-permute-done.98
  (616 shorter events, 238.3 us)
Async XLA Ops:
  7.2 103.2 %all-gather.5.cloned.1.call-start = ((), (), s32[]{:S(2)}) async-start(), calls=%async_computation.4 | async-start | bytes 2621440 | tf_op jit(solution)/shard_map/all_gather | solution.py:74
  20.9 121.4 %all-gather.7.cloned.1.call-start = ((), (), s32[]{:S(2)}) async-start(), calls=%async_computation.5 | async-start | bytes 2621440 | tf_op jit(solution)/shard_map/all_gather | solution.py:74
  31.9 241.8 %all-gather.9.cloned.1.call-start = ((), (), s32[]{:S(2)}) async-start(), calls=%async_computation.6 | async-start | bytes 7208960 | tf_op jit(solution)/shard_map/all_gather | solution.py:74
  34.9 17.3 %collective-permute-start.39 = (bf16[128,1408]{1,0:T(8,128)(2,1)S(1)}, bf16[128,1408]{1,0:T(8,128)(2,1)}, u32[]{:S(2)}, u32[]{:S(2)}) collective-permute-start(bf16[128,1408]{1,0:T(8,128)(2,1)S(1)} %get-tuple-element.104), channel_id=1, source_target_pairs={{0,4},{2,6},{4,0},{6,2},{1,5},{3,7},{5,1},{7,3},{8,12},{10,14},{12... | collective-permute-start | bytes 1081352 | tf_op jit(solution)/shard_map/ppermute | solution.py:19
  36.3 16.2 %collective-permute-start.38 = (bf16[128,1408]{1,0:T(8,128)(2,1)S(1)}, bf16[128,1408]{1,0:T(8,128)(2,1)}, u32[]{:S(2)}, u32[]{:S(2)}) collective-permute-start(bf16[128,1408]{1,0:T(8,128)(2,1)S(1)} %get-tuple-element.105), channel_id=1, source_target_pairs={{0,2},{2,0},{4,6},{6,4},{1,3},{3,1},{5,7},{7,5},{8,10},{10,8},{12,... | collective-permute-start | bytes 1081352 | tf_op jit(solution)/shard_map/ppermute | solution.py:15
  36.9 30.9 %collective-permute-start.12 = (s32[2,4]{1,0:T(2,128)S(1)}, s32[2,4]{1,0:T(2,128)}, u32[]{:S(2)}, u32[]{:S(2)}) collective-permute-start(s32[2,4]{1,0:T(2,128)S(1)} %broadcast_select_fusion), channel_id=1, source_target_pairs={{0,6},{2,4},{4,2},{6,0},{1,7},{3,5},{5,3},{7,1},{8,14},{10,12},{12... | collective-permute-start | bytes 104 | tf_op jit(solution)/shard_map/ppermute | solution.py:23
  38.5 30.9 %collective-permute-start.11 = (s32[2,4]{1,0:T(2,128)S(1)}, s32[2,4]{1,0:T(2,128)}, u32[]{:S(2)}, u32[]{:S(2)}) collective-permute-start(s32[2,4]{1,0:T(2,128)S(1)} %broadcast_select_fusion), channel_id=1, source_target_pairs={{0,4},{2,6},{4,0},{6,2},{1,5},{3,7},{5,1},{7,3},{8,12},{10,14},{12... | collective-permute-start | bytes 104 | tf_op jit(solution)/shard_map/ppermute | solution.py:19
  45.8 25.0 %collective-permute-start.10 = (s32[2,4]{1,0:T(2,128)S(1)}, s32[2,4]{1,0:T(2,128)S(1)}, u32[]{:S(2)}, u32[]{:S(2)}) collective-permute-start(s32[2,4]{1,0:T(2,128)S(1)} %broadcast_select_fusion), channel_id=1, source_target_pairs={{0,2},{2,0},{4,6},{6,4},{1,3},{3,1},{5,7},{7,5},{8,10},{10,8},{12,... | collective-permute-start | bytes 104 | tf_op jit(solution)/shard_map/ppermute | solution.py:15
  55.3 237.6 %all-gather.11.cloned.1.call-start = ((), (), s32[]{:S(2)}) async-start(), calls=%async_computation.7 | async-start | bytes 3604480 | tf_op jit(solution)/shard_map/all_gather | solution.py:74
  57.6 28.6 %collective-permute-start.2 = (bf16[256,2048]{1,0:T(8,128)(2,1)}, bf16[256,2048]{1,0:T(8,128)(2,1)S(1)}, u32[]{:S(2)}, u32[]{:S(2)}) collective-permute-start(bf16[256,2048]{1,0:T(8,128)(2,1)} %get-tuple-element.73), channel_id=1, source_target_pairs={{0,4},{2,6},{4,0},{6,2},{1,5},{3,7},{5,1},{7,3},{8,12},{10,14},{12... | collective-permute-start | bytes 3145736 | tf_op jit(solution)/shard_map/ppermute | solution.py:19
  59.0 26.4 %collective-permute-start = (bf16[256,2048]{1,0:T(8,128)(2,1)}, bf16[256,2048]{1,0:T(8,128)(2,1)}, u32[]{:S(2)}, u32[]{:S(2)}) collective-permute-start(bf16[256,2048]{1,0:T(8,128)(2,1)} %get-tuple-element.73), channel_id=1, source_target_pairs={{0,2},{2,0},{4,6},{6,4},{1,3},{3,1},{5,7},{7,5},{8,10},{10,8},{12,... | collective-permute-start | bytes 3145736 | tf_op jit(solution)/shard_map/ppermute | solution.py:15
  67.8 21.4 %collective-permute-start.43 = (bf16[128,704]{0,1:T(8,128)(2,1)}, bf16[128,704]{0,1:T(8,128)(2,1)S(1)}, u32[]{:S(2)}, u32[]{:S(2)}) collective-permute-start(bf16[128,704]{0,1:T(8,128)(2,1)} %get-tuple-element.143), channel_id=1, source_target_pairs={{0,6},{2,4},{4,2},{6,0},{1,7},{3,5},{5,3},{7,1},{8,14},{10,12},{12... | collective-permute-start | bytes 540680 | tf_op jit(solution)/shard_map/ppermute | solution.py:23
  69.3 21.3 %collective-permute-start.42 = (bf16[128,704]{0,1:T(8,128)(2,1)}, bf16[128,704]{0,1:T(8,128)(2,1)S(1)}, u32[]{:S(2)}, u32[]{:S(2)}) collective-permute-start(bf16[128,704]{0,1:T(8,128)(2,1)} %get-tuple-element.144), channel_id=1, source_target_pairs={{0,4},{2,6},{4,0},{6,2},{1,5},{3,7},{5,1},{7,3},{8,12},{10,14},{12... | collective-permute-start | bytes 540680 | tf_op jit(solution)/shard_map/ppermute | solution.py:19
  70.7 22.3 %collective-permute-start.41 = (bf16[128,704]{0,1:T(8,128)(2,1)S(1)}, bf16[128,704]{0,1:T(8,128)(2,1)S(1)}, u32[]{:S(2)}, u32[]{:S(2)}) collective-permute-start(bf16[128,704]{0,1:T(8,128)(2,1)S(1)} %get-tuple-element.145), channel_id=1, source_target_pairs={{0,2},{2,0},{4,6},{6,4},{1,3},{3,1},{5,7},{7,5},{8,10},{10,8},{12,... | collective-permute-start | bytes 540680 | tf_op jit(solution)/shard_map/ppermute | solution.py:15
  85.4 18.9 %collective-permute-start.1 = (bf16[256,2048]{1,0:T(8,128)(2,1)}, bf16[256,2048]{1,0:T(8,128)(2,1)S(1)}, u32[]{:S(2)}, u32[]{:S(2)}) collective-permute-start(bf16[256,2048]{1,0:T(8,128)(2,1)} %collective-permute-done), channel_id=1, source_target_pairs={{0,1},{1,0},{2,3},{3,2},{4,5},{5,4},{6,7},{7,6},{8,9},{9,8},{10,11... | collective-permute-start | bytes 3145736 | tf_op jit(solution)/shard_map/ppermute | solution.py:27
  86.3 16.7 %collective-permute-start.5 = (bf16[128,2048]{1,0:T(8,128)(2,1)S(1)}, bf16[128,2048]{1,0:T(8,128)(2,1)S(1)}, u32[]{:S(2)}, u32[]{:S(2)}) collective-permute-start(bf16[128,2048]{1,0:T(8,128)(2,1)S(1)} %slice.729), channel_id=1, source_target_pairs={{0,2},{2,0},{4,6},{6,4},{1,3},{3,1},{5,7},{7,5},{8,10},{10,8},{12,... | collective-permute-start | bytes 1572872 | tf_op jit(solution)/shard_map/ppermute | solution.py:15
  89.2 14.9 %collective-permute-start.4 = (bf16[128,2048]{1,0:T(8,128)(2,1)S(1)}, bf16[128,2048]{1,0:T(8,128)(2,1)S(1)}, u32[]{:S(2)}, u32[]{:S(2)}) collective-permute-start(bf16[128,2048]{1,0:T(8,128)(2,1)S(1)} %slice.728), channel_id=1, source_target_pairs={{0,4},{2,6},{4,0},{6,2},{1,5},{3,7},{5,1},{7,3},{8,12},{10,14},{12... | collective-permute-start | bytes 1572872 | tf_op jit(solution)/shard_map/ppermute | solution.py:19
  90.7 48.4 %collective-permute-start.55 = (bf16[256,2048]{1,0:T(8,128)(2,1)}, bf16[256,2048]{1,0:T(8,128)(2,1)S(1)}, u32[]{:S(2)}, u32[]{:S(2)}) collective-permute-start(bf16[256,2048]{1,0:T(8,128)(2,1)} %get-tuple-element.63), channel_id=1, source_target_pairs={{0,4},{2,6},{4,0},{6,2},{1,5},{3,7},{5,1},{7,3},{8,12},{10,14},{12... | collective-permute-start | bytes 3145736 | tf_op jit(solution)/shard_map/ppermute | solution.py:19
  103.0 88.2 %collective-permute-start.53 = (bf16[256,2048]{1,0:T(8,128)(2,1)}, bf16[256,2048]{1,0:T(8,128)(2,1)}, u32[]{:S(2)}, u32[]{:S(2)}) collective-permute-start(bf16[256,2048]{1,0:T(8,128)(2,1)} %get-tuple-element.63), channel_id=1, source_target_pairs={{0,2},{2,0},{4,6},{6,4},{1,3},{3,1},{5,7},{7,5},{8,10},{10,8},{12,... | collective-permute-start | bytes 3145736 | tf_op jit(solution)/shard_map/ppermute | solution.py:15
  138.8 427.8 %reduce-scatter.11.cloned.1.call-start = ((), (), s32[]{:S(2)}) async-start(), calls=%async_computation.11 | async-start | bytes 3604480 | tf_op jit(solution)/shard_map/reduce_scatter | solution.py:78
  140.0 82.7 %collective-permute-start.58 = (bf16[128,2048]{1,0:T(8,128)(2,1)}, bf16[128,2048]{1,0:T(8,128)(2,1)}, u32[]{:S(2)}, u32[]{:S(2)}) collective-permute-start(bf16[128,2048]{1,0:T(8,128)(2,1)} %slice.797), channel_id=1, source_target_pairs={{0,2},{2,0},{4,6},{6,4},{1,3},{3,1},{5,7},{7,5},{8,10},{10,8},{12,... | collective-permute-start | bytes 1572872 | tf_op jit(solution)/shard_map/ppermute | solution.py:15
  156.0 59.3 %collective-permute-start.22 = (bf16[256,2048]{1,0:T(8,128)(2,1)}, bf16[256,2048]{1,0:T(8,128)(2,1)}, u32[]{:S(2)}, u32[]{:S(2)}) collective-permute-start(bf16[256,2048]{1,0:T(8,128)(2,1)} %convolution_convert_fusion.10), channel_id=1, source_target_pairs={{0,1},{1,0},{2,3},{3,2},{4,5},{5,4},{6,7},{7,6},{8,9},{9,8},{10,11... | collective-permute-start | bytes 3145736 | tf_op jit(solution)/shard_map/ppermute | solution.py:27
  161.8 27.9 %collective-permute-start.17 = (f32[4,2,256]{2,1,0:T(2,128)S(1)}, f32[4,2,256]{2,1,0:T(2,128)S(1)}, u32[]{:S(2)}, u32[]{:S(2)}) collective-permute-start(f32[4,2,256]{2,1,0:T(2,128)S(1)} %get-tuple-element.237), channel_id=1, source_target_pairs={{0,2},{2,0},{4,6},{6,4},{1,3},{3,1},{5,7},{7,5},{8,10},{10,8},{12,... | collective-permute-start | bytes 24584 | tf_op jit(solution)/shard_map/ppermute | solution.py:15
  188.0 27.4 %collective-permute-start.26 = (bf16[256,2048]{1,0:T(8,128)(2,1)}, bf16[256,2048]{1,0:T(8,128)(2,1)}, u32[]{:S(2)}, u32[]{:S(2)}) collective-permute-start(bf16[256,2048]{1,0:T(8,128)(2,1)} %pad_maximum_fusion.12), channel_id=1, source_target_pairs={{0,2},{2,0},{4,6},{6,4},{1,3},{3,1},{5,7},{7,5},{8,10},{10,8},{12,... | collective-permute-start | bytes 3145736 | tf_op jit(solution)/shard_map/ppermute | solution.py:15
  189.7 26.2 %collective-permute-start.29 = (bf16[256,2048]{1,0:T(8,128)(2,1)}, bf16[256,2048]{1,0:T(8,128)(2,1)}, u32[]{:S(2)}, u32[]{:S(2)}) collective-permute-start(bf16[256,2048]{1,0:T(8,128)(2,1)} %pad_maximum_fusion.13), channel_id=1, source_target_pairs={{0,4},{2,6},{4,0},{6,2},{1,5},{3,7},{5,1},{7,3},{8,12},{10,14},{12... | collective-permute-start | bytes 3145736 | tf_op jit(solution)/shard_map/ppermute | solution.py:19
  191.2 22.6 %collective-permute-start.18 = (f32[4,2,256]{2,1,0:T(2,128)S(1)}, f32[4,2,256]{2,1,0:T(2,128)S(1)}, u32[]{:S(2)}, u32[]{:S(2)}) collective-permute-start(f32[4,2,256]{2,1,0:T(2,128)S(1)} %get-tuple-element.70), channel_id=1, source_target_pairs={{0,4},{2,6},{4,0},{6,2},{1,5},{3,7},{5,1},{7,3},{8,12},{10,14},{12... | collective-permute-start | bytes 24584 | tf_op jit(solution)/shard_map/ppermute | solution.py:19
  215.3 15.6 %collective-permute-start.56 = (bf16[256,2048]{1,0:T(8,128)(2,1)}, bf16[256,2048]{1,0:T(8,128)(2,1)S(1)}, u32[]{:S(2)}, u32[]{:S(2)}) collective-permute-start(bf16[256,2048]{1,0:T(8,128)(2,1)} %copy-done.29), channel_id=1, source_target_pairs={{0,1},{1,0},{2,3},{3,2},{4,5},{5,4},{6,7},{7,6},{8,9},{9,8},{10,11... | collective-permute-start | bytes 3145736 | tf_op jit(solution)/shard_map/ppermute | solution.py:27
  222.1 25.1 %collective-permute-start.31 = (bf16[256,2048]{1,0:T(8,128)(2,1)S(1)}, bf16[256,2048]{1,0:T(8,128)(2,1)S(1)}, u32[]{:S(2)}, u32[]{:S(2)}) collective-permute-start(bf16[256,2048]{1,0:T(8,128)(2,1)S(1)} %get-tuple-element.65), channel_id=1, source_target_pairs={{0,2},{2,0},{4,6},{6,4},{1,3},{3,1},{5,7},{7,5},{8,10},{10,8},{12,... | collective-permute-start | bytes 3145736 | tf_op jit(solution)/shard_map/ppermute | solution.py:15
  226.9 27.9 %collective-permute-start.59 = (bf16[256,2048]{1,0:T(8,128)(2,1)S(1)}, bf16[256,2048]{1,0:T(8,128)(2,1)S(1)}, u32[]{:S(2)}, u32[]{:S(2)}) collective-permute-start(bf16[256,2048]{1,0:T(8,128)(2,1)S(1)} %pad_maximum_fusion.17), channel_id=1, source_target_pairs={{0,1},{1,0},{2,3},{3,2},{4,5},{5,4},{6,7},{7,6},{8,9},{9,8},{10,11... | collective-permute-start | bytes 3145736 | tf_op jit(solution)/shard_map/ppermute | solution.py:27
  227.0 25.6 %collective-permute-start.33 = (bf16[256,2048]{1,0:T(8,128)(2,1)S(1)}, bf16[256,2048]{1,0:T(8,128)(2,1)S(1)}, u32[]{:S(2)}, u32[]{:S(2)}) collective-permute-start(bf16[256,2048]{1,0:T(8,128)(2,1)S(1)} %get-tuple-element.65), channel_id=1, source_target_pairs={{0,4},{2,6},{4,0},{6,2},{1,5},{3,7},{5,1},{7,3},{8,12},{10,14},{12... | collective-permute-start | bytes 3145736 | tf_op jit(solution)/shard_map/ppermute | solution.py:19
  229.6 26.4 %collective-permute-start.30 = (bf16[256,2048]{1,0:T(8,128)(2,1)S(1)}, bf16[256,2048]{1,0:T(8,128)(2,1)S(1)}, u32[]{:S(2)}, u32[]{:S(2)}) collective-permute-start(bf16[256,2048]{1,0:T(8,128)(2,1)S(1)} %get-tuple-element.65), channel_id=1, source_target_pairs={{0,1},{1,0},{2,3},{3,2},{4,5},{5,4},{6,7},{7,6},{8,9},{9,8},{10,11... | collective-permute-start | bytes 3145736 | tf_op jit(solution)/shard_map/ppermute | solution.py:27
  247.2 20.6 %collective-permute-start.32 = (bf16[256,2048]{1,0:T(8,128)(2,1)S(1)}, bf16[256,2048]{1,0:T(8,128)(2,1)S(1)}, u32[]{:S(2)}, u32[]{:S(2)}) collective-permute-start(bf16[256,2048]{1,0:T(8,128)(2,1)S(1)} %collective-permute-done.31), channel_id=1, source_target_pairs={{0,1},{1,0},{2,3},{3,2},{4,5},{5,4},{6,7},{7,6},{8,9},{9,8},{10,11... | collective-permute-start | bytes 3145736 | tf_op jit(solution)/shard_map/ppermute | solution.py:27
  310.9 99.9 %collective-permute-start.44 = (bf16[256,2048]{1,0:T(8,128)(2,1)}, bf16[256,2048]{1,0:T(8,128)(2,1)S(1)}, u32[]{:S(2)}, u32[]{:S(2)}) collective-permute-start(bf16[256,2048]{1,0:T(8,128)(2,1)} %convolution_convert_fusion.6), channel_id=1, source_target_pairs={{0,1},{1,0},{2,3},{3,2},{4,5},{5,4},{6,7},{7,6},{8,9},{9,8},{10,11... | collective-permute-start | bytes 3145736 | tf_op jit(solution)/shard_map/ppermute | solution.py:27
  314.5 15.3 %collective-permute-start.46 = (bf16[256,2048]{1,0:T(8,128)(2,1)}, bf16[256,2048]{1,0:T(8,128)(2,1)S(1)}, u32[]{:S(2)}, u32[]{:S(2)}) collective-permute-start(bf16[256,2048]{1,0:T(8,128)(2,1)} %convolution_convert_fusion.4), channel_id=1, source_target_pairs={{0,1},{1,0},{2,3},{3,2},{4,5},{5,4},{6,7},{7,6},{8,9},{9,8},{10,11... | collective-permute-start | bytes 3145736 | tf_op jit(solution)/shard_map/ppermute | solution.py:27
  329.8 36.6 %collective-permute-start.60 = (bf16[256,2048]{1,0:T(8,128)(2,1)S(1)}, bf16[256,2048]{1,0:T(8,128)(2,1)}, u32[]{:S(2)}, u32[]{:S(2)}) collective-permute-start(bf16[256,2048]{1,0:T(8,128)(2,1)S(1)} %convolution_convert_fusion.16), channel_id=1, source_target_pairs={{0,1},{1,0},{2,3},{3,2},{4,5},{5,4},{6,7},{7,6},{8,9},{9,8},{10,11... | collective-permute-start | bytes 3145736 | tf_op jit(solution)/shard_map/ppermute | solution.py:27
  333.0 14.7 %collective-permute-start.47 = (bf16[128,2048]{1,0:T(8,128)(2,1)S(1)}, bf16[128,2048]{1,0:T(8,128)(2,1)S(1)}, u32[]{:S(2)}, u32[]{:S(2)}) collective-permute-start(bf16[128,2048]{1,0:T(8,128)(2,1)S(1)} %get-tuple-element.114), channel_id=1, source_target_pairs={{0,4},{2,6},{4,0},{6,2},{1,5},{3,7},{5,1},{7,3},{8,12},{10,14},{12... | collective-permute-start | bytes 1572872 | tf_op jit(solution)/shard_map/ppermute | solution.py:19
  335.5 28.2 %collective-permute-start.50 = (bf16[128,2048]{1,0:T(8,128)(2,1)}, bf16[128,2048]{1,0:T(8,128)(2,1)}, u32[]{:S(2)}, u32[]{:S(2)}) collective-permute-start(bf16[128,2048]{1,0:T(8,128)(2,1)} %get-tuple-element.115), channel_id=1, source_target_pairs={{0,2},{2,0},{4,6},{6,4},{1,3},{3,1},{5,7},{7,5},{8,10},{10,8},{12,... | collective-permute-start | bytes 1572872 | tf_op jit(solution)/shard_map/ppermute | solution.py:15
  339.8 22.9 %collective-permute-start.63 = (bf16[128,2048]{1,0:T(8,128)(2,1)S(1)}, bf16[128,2048]{1,0:T(8,128)(2,1)S(1)}, u32[]{:S(2)}, u32[]{:S(2)}) collective-permute-start(bf16[128,2048]{1,0:T(8,128)(2,1)S(1)} %get-tuple-element.108), channel_id=1, source_target_pairs={{0,4},{2,6},{4,0},{6,2},{1,5},{3,7},{5,1},{7,3},{8,12},{10,14},{12... | collective-permute-start | bytes 1572872 | tf_op jit(solution)/shard_map/ppermute | solution.py:19
  361.2 49.7 %collective-permute-start.48 = (bf16[256,2048]{1,0:T(8,128)(2,1)S(1)}, bf16[256,2048]{1,0:T(8,128)(2,1)S(1)}, u32[]{:S(2)}, u32[]{:S(2)}) collective-permute-start(bf16[256,2048]{1,0:T(8,128)(2,1)S(1)} %pad_maximum_fusion.15), channel_id=1, source_target_pairs={{0,2},{2,0},{4,6},{6,4},{1,3},{3,1},{5,7},{7,5},{8,10},{10,8},{12,... | collective-permute-start | bytes 3145736 | tf_op jit(solution)/shard_map/ppermute | solution.py:15
  362.8 26.3 %collective-permute-start.67 = (bf16[256,2048]{1,0:T(8,128)(2,1)S(1)}, bf16[256,2048]{1,0:T(8,128)(2,1)}, u32[]{:S(2)}, u32[]{:S(2)}) collective-permute-start(bf16[256,2048]{1,0:T(8,128)(2,1)S(1)} %pad_maximum_fusion.19), channel_id=1, source_target_pairs={{0,4},{2,6},{4,0},{6,2},{1,5},{3,7},{5,1},{7,3},{8,12},{10,14},{12... | collective-permute-start | bytes 3145736 | tf_op jit(solution)/shard_map/ppermute | solution.py:19
  363.7 44.0 %collective-permute-start.64 = (bf16[256,2048]{1,0:T(8,128)(2,1)S(1)}, bf16[256,2048]{1,0:T(8,128)(2,1)}, u32[]{:S(2)}, u32[]{:S(2)}) collective-permute-start(bf16[256,2048]{1,0:T(8,128)(2,1)S(1)} %pad_maximum_fusion.18), channel_id=1, source_target_pairs={{0,2},{2,0},{4,6},{6,4},{1,3},{3,1},{5,7},{7,5},{8,10},{10,8},{12,... | collective-permute-start | bytes 3145736 | tf_op jit(solution)/shard_map/ppermute | solution.py:15
  366.5 44.4 %collective-permute-start.51 = (bf16[256,2048]{1,0:T(8,128)(2,1)S(1)}, bf16[256,2048]{1,0:T(8,128)(2,1)S(1)}, u32[]{:S(2)}, u32[]{:S(2)}) collective-permute-start(bf16[256,2048]{1,0:T(8,128)(2,1)S(1)} %pad_maximum_fusion.16), channel_id=1, source_target_pairs={{0,4},{2,6},{4,0},{6,2},{1,5},{3,7},{5,1},{7,3},{8,12},{10,14},{12... | collective-permute-start | bytes 3145736 | tf_op jit(solution)/shard_map/ppermute | solution.py:19
  415.9 27.8 %collective-permute-start.71 = (bf16[256,2048]{1,0:T(8,128)(2,1)S(1)}, bf16[256,2048]{1,0:T(8,128)(2,1)}, u32[]{:S(2)}, u32[]{:S(2)}) collective-permute-start(bf16[256,2048]{1,0:T(8,128)(2,1)S(1)} %get-tuple-element.59), channel_id=1, source_target_pairs={{0,4},{2,6},{4,0},{6,2},{1,5},{3,7},{5,1},{7,3},{8,12},{10,14},{12... | collective-permute-start | bytes 3145736 | tf_op jit(solution)/shard_map/ppermute | solution.py:19
  417.8 25.8 %collective-permute-start.69 = (bf16[256,2048]{1,0:T(8,128)(2,1)S(1)}, bf16[256,2048]{1,0:T(8,128)(2,1)}, u32[]{:S(2)}, u32[]{:S(2)}) collective-permute-start(bf16[256,2048]{1,0:T(8,128)(2,1)S(1)} %get-tuple-element.59), channel_id=1, source_target_pairs={{0,2},{2,0},{4,6},{6,4},{1,3},{3,1},{5,7},{7,5},{8,10},{10,8},{12,... | collective-permute-start | bytes 3145736 | tf_op jit(solution)/shard_map/ppermute | solution.py:15
  418.0 30.1 %collective-permute-start.68 = (bf16[256,2048]{1,0:T(8,128)(2,1)S(1)}, bf16[256,2048]{1,0:T(8,128)(2,1)}, u32[]{:S(2)}, u32[]{:S(2)}) collective-permute-start(bf16[256,2048]{1,0:T(8,128)(2,1)S(1)} %get-tuple-element.59), channel_id=1, source_target_pairs={{0,1},{1,0},{2,3},{3,2},{4,5},{5,4},{6,7},{7,6},{8,9},{9,8},{10,11... | collective-permute-start | bytes 3145736 | tf_op jit(solution)/shard_map/ppermute | solution.py:27
  418.1 25.1 %collective-permute-start.77 = (f32[2,256]{1,0:T(2,128)S(1)}, f32[2,256]{1,0:T(2,128)S(1)}, u32[]{:S(2)}, u32[]{:S(2)}) collective-permute-start(f32[2,256]{1,0:T(2,128)S(1)} %pad_maximum_fusion.45), channel_id=1, source_target_pairs={{0,2},{2,0},{4,6},{6,4},{1,3},{3,1},{5,7},{7,5},{8,10},{10,8},{12,... | collective-permute-start | bytes 6152 | tf_op jit(solution)/shard_map/ppermute | solution.py:15
  431.2 187.5 %reduce-scatter.7.cloned.1.call-start = ((), (), s32[]{:S(2)}) async-start(), calls=%async_computation.9 | async-start | bytes 2621440 | tf_op jit(solution)/shard_map/reduce_scatter | solution.py:78
  443.6 18.3 %collective-permute-start.70 = (bf16[256,2048]{1,0:T(8,128)(2,1)}, bf16[256,2048]{1,0:T(8,128)(2,1)S(1)}, u32[]{:S(2)}, u32[]{:S(2)}) collective-permute-start(bf16[256,2048]{1,0:T(8,128)(2,1)} %collective-permute-done.69), channel_id=1, source_target_pairs={{0,1},{1,0},{2,3},{3,2},{4,5},{5,4},{6,7},{7,6},{8,9},{9,8},{10,11... | collective-permute-start | bytes 3145736 | tf_op jit(solution)/shard_map/ppermute | solution.py:27
  444.8 14.4 %collective-permute-start.74 = (bf16[128,2048]{1,0:T(8,128)(2,1)S(1)}, bf16[128,2048]{1,0:T(8,128)(2,1)S(1)}, u32[]{:S(2)}, u32[]{:S(2)}) collective-permute-start(bf16[128,2048]{1,0:T(8,128)(2,1)S(1)} %slice.821), channel_id=1, source_target_pairs={{0,2},{2,0},{4,6},{6,4},{1,3},{3,1},{5,7},{7,5},{8,10},{10,8},{12,... | collective-permute-start | bytes 1572872 | tf_op jit(solution)/shard_map/ppermute | solution.py:15
  448.0 15.4 %collective-permute-start.72 = (bf16[256,2048]{1,0:T(8,128)(2,1)}, bf16[256,2048]{1,0:T(8,128)(2,1)S(1)}, u32[]{:S(2)}, u32[]{:S(2)}) collective-permute-start(bf16[256,2048]{1,0:T(8,128)(2,1)} %collective-permute-done.71), channel_id=1, source_target_pairs={{0,1},{1,0},{2,3},{3,2},{4,5},{5,4},{6,7},{7,6},{8,9},{9,8},{10,11... | collective-permute-start | bytes 3145736 | tf_op jit(solution)/shard_map/ppermute | solution.py:27
  477.0 147.1 %reduce-scatter.5.cloned.1.call-start = ((), (), s32[]{:S(2)}) async-start(), calls=%async_computation.8 | async-start | bytes 2621440 | tf_op jit(solution)/shard_map/reduce_scatter | solution.py:78
  509.8 172.1 %reduce-scatter.9.cloned.1.call-start = ((), (), s32[]{:S(2)}) async-start(), calls=%async_computation.10 | async-start | bytes 7208960 | tf_op jit(solution)/shard_map/reduce_scatter | solution.py:78
  513.4 17.6 %collective-permute-start.52 = (bf16[256,1024]{1,0:T(8,128)(2,1)}, bf16[256,1024]{1,0:T(8,128)(2,1)}, u32[]{:S(2)}, u32[]{:S(2)}) collective-permute-start(bf16[256,1024]{1,0:T(8,128)(2,1)} %get-tuple-element.111), channel_id=1, source_target_pairs={{0,1},{1,0},{2,3},{3,2},{4,5},{5,4},{6,7},{7,6},{8,9},{9,8},{10,11... | collective-permute-start | bytes 1572872 | tf_op jit(solution)/shard_map/ppermute | solution.py:27
  544.3 25.7 %collective-permute-start.82 = (bf16[256,2048]{1,0:T(8,128)(2,1)}, bf16[256,2048]{1,0:T(8,128)(2,1)}, u32[]{:S(2)}, u32[]{:S(2)}) collective-permute-start(bf16[256,2048]{1,0:T(8,128)(2,1)} %fusion.1), channel_id=1, source_target_pairs={{0,1},{1,0},{2,3},{3,2},{4,5},{5,4},{6,7},{7,6},{8,9},{9,8},{10,11... | collective-permute-start | bytes 3145736 | tf_op jit(solution)/shard_map/ppermute | solution.py:27
  545.2 14.4 %collective-permute-start.88 = (bf16[128,2048]{1,0:T(8,128)(2,1)S(1)}, bf16[128,2048]{1,0:T(8,128)(2,1)S(1)}, u32[]{:S(2)}, u32[]{:S(2)}) collective-permute-start(bf16[128,2048]{1,0:T(8,128)(2,1)S(1)} %get-tuple-element.107), channel_id=1, source_target_pairs={{0,2},{2,0},{4,6},{6,4},{1,3},{3,1},{5,7},{7,5},{8,10},{10,8},{12,... | collective-permute-start | bytes 1572872 | tf_op jit(solution)/shard_map/ppermute | solution.py:15
  546.5 14.6 %collective-permute-start.85 = (bf16[128,2048]{1,0:T(8,128)(2,1)S(1)}, bf16[128,2048]{1,0:T(8,128)(2,1)S(1)}, u32[]{:S(2)}, u32[]{:S(2)}) collective-permute-start(bf16[128,2048]{1,0:T(8,128)(2,1)S(1)} %get-tuple-element.106), channel_id=1, source_target_pairs={{0,4},{2,6},{4,0},{6,2},{1,5},{3,7},{5,1},{7,3},{8,12},{10,14},{12... | collective-permute-start | bytes 1572872 | tf_op jit(solution)/shard_map/ppermute | solution.py:19
  560.7 26.7 %collective-permute-start.89 = (bf16[256,2048]{1,0:T(8,128)(2,1)}, bf16[256,2048]{1,0:T(8,128)(2,1)}, u32[]{:S(2)}, u32[]{:S(2)}) collective-permute-start(bf16[256,2048]{1,0:T(8,128)(2,1)} %pad_maximum_fusion.22), channel_id=1, source_target_pairs={{0,4},{2,6},{4,0},{6,2},{1,5},{3,7},{5,1},{7,3},{8,12},{10,14},{12... | collective-permute-start | bytes 3145736 | tf_op jit(solution)/shard_map/ppermute | solution.py:19
  562.3 26.4 %collective-permute-start.86 = (bf16[256,2048]{1,0:T(8,128)(2,1)}, bf16[256,2048]{1,0:T(8,128)(2,1)}, u32[]{:S(2)}, u32[]{:S(2)}) collective-permute-start(bf16[256,2048]{1,0:T(8,128)(2,1)} %pad_maximum_fusion.21), channel_id=1, source_target_pairs={{0,2},{2,0},{4,6},{6,4},{1,3},{3,1},{5,7},{7,5},{8,10},{10,8},{12,... | collective-permute-start | bytes 3145736 | tf_op jit(solution)/shard_map/ppermute | solution.py:15
  568.2 25.3 %collective-permute-start.102 = (bf16[128,704]{0,1:T(8,128)(2,1)S(1)}, bf16[128,704]{0,1:T(8,128)(2,1)S(1)}, u32[]{:S(2)}, u32[]{:S(2)}) collective-permute-start(bf16[128,704]{0,1:T(8,128)(2,1)S(1)} %get-tuple-element.123), channel_id=1, source_target_pairs={{0,6},{2,4},{4,2},{6,0},{1,7},{3,5},{5,3},{7,1},{8,14},{10,12},{12... | collective-permute-start | bytes 540680 | tf_op jit(solution)/shard_map/ppermute | solution.py:23
  569.6 23.9 %collective-permute-start.101 = (bf16[128,704]{0,1:T(8,128)(2,1)S(1)}, bf16[128,704]{0,1:T(8,128)(2,1)S(1)}, u32[]{:S(2)}, u32[]{:S(2)}) collective-permute-start(bf16[128,704]{0,1:T(8,128)(2,1)S(1)} %get-tuple-element.124), channel_id=1, source_target_pairs={{0,4},{2,6},{4,0},{6,2},{1,5},{3,7},{5,1},{7,3},{8,12},{10,14},{12... | collective-permute-start | bytes 540680 | tf_op jit(solution)/shard_map/ppermute | solution.py:19
  570.0 24.9 %collective-permute-start.100 = (bf16[128,704]{0,1:T(8,128)(2,1)S(1)}, bf16[128,704]{0,1:T(8,128)(2,1)S(1)}, u32[]{:S(2)}, u32[]{:S(2)}) collective-permute-start(bf16[128,704]{0,1:T(8,128)(2,1)S(1)} %get-tuple-element.125), channel_id=1, source_target_pairs={{0,2},{2,0},{4,6},{6,4},{1,3},{3,1},{5,7},{7,5},{8,10},{10,8},{12,... | collective-permute-start | bytes 540680 | tf_op jit(solution)/shard_map/ppermute | solution.py:15
  612.8 75.3 %collective-permute-start.90 = (f32[256,2048]{1,0:T(8,128)}, f32[256,2048]{1,0:T(8,128)S(1)}, u32[]{:S(2)}, u32[]{:S(2)}) collective-permute-start(f32[256,2048]{1,0:T(8,128)} %fusion.13), channel_id=1, source_target_pairs={{0,1},{1,0},{2,3},{3,2},{4,5},{5,4},{6,7},{7,6},{8,9},{9,8},{10,11... | collective-permute-start | bytes 6291464 | tf_op jit(solution)/shard_map/ppermute | solution.py:27
  686.2 16.5 %collective-permute-start.98 = (bf16[128,1408]{1,0:T(8,128)(2,1)S(1)}, bf16[128,1408]{1,0:T(8,128)(2,1)S(1)}, u32[]{:S(2)}, u32[]{:S(2)}) collective-permute-start(bf16[128,1408]{1,0:T(8,128)(2,1)S(1)} %get-tuple-element.92), channel_id=1, source_target_pairs={{0,4},{2,6},{4,0},{6,2},{1,5},{3,7},{5,1},{7,3},{8,12},{10,14},{12... | collective-permute-start | bytes 1081352 | tf_op jit(solution)/shard_map/ppermute | solution.py:19
  686.7 16.0 %collective-permute-start.97 = (bf16[128,1408]{1,0:T(8,128)(2,1)S(1)}, bf16[128,1408]{1,0:T(8,128)(2,1)S(1)}, u32[]{:S(2)}, u32[]{:S(2)}) collective-permute-start(bf16[128,1408]{1,0:T(8,128)(2,1)S(1)} %get-tuple-element.93), channel_id=1, source_target_pairs={{0,2},{2,0},{4,6},{6,4},{1,3},{3,1},{5,7},{7,5},{8,10},{10,8},{12,... | collective-permute-start | bytes 1081352 | tf_op jit(solution)/shard_map/ppermute | solution.py:15
  (124 other events, 1220.5 us)
Sparse Core Ops, SparseCore 0:
  21.0 46.4 all-gather.4
  69.6 44.6 all-gather.6
  116.5 105.4 all-gather.8
  223.4 58.6 all-gather.10
  431.3 54.3 reduce-scatter.10
  487.8 44.0 reduce-scatter.6
  534.3 42.9 reduce-scatter.4
  579.6 102.2 reduce-scatter.8

commit v2 on v1

v2 whole, which is shorter than its diff:
```python
import functools

import jax
import jax.numpy as jnp
from jax import lax
from jax.experimental import pallas as pl
from jax.experimental.pallas import tpu as pltpu
from jax.sharding import PartitionSpec as P

EPSILON = 1e-06
LOW = jnp.bfloat16
FULL = jnp.float32
VMEM_BYTES = 56 * 1024 * 1024
ANYWHERE = pl.BlockSpec(memory_space=pl.ANY)


def swap_x(v):
    return lax.ppermute(v, "batch", [(i, i ^ 1) for i in range(4)])


def swap_y(v):
    return lax.ppermute(v, "batch", [(i, i ^ 2) for i in range(4)])


def swap_xy(v):
    return lax.ppermute(v, "batch", [(i, i ^ 3) for i in range(4)])


def swap_core(v):
    return lax.ppermute(v, "mp", [(0, 1), (1, 0)])


def after(v, *first):
    return lax.optimization_barrier((v, *first))[0]


def settled(*first):
    return swap_core(lax.optimization_barrier(first)[0][:16, :128])


def contract(left, right, left_dim, right_dim):
    return lax.dot_general(
        left, right, (((left_dim,), (right_dim,)), ((), ())), preferred_element_type=FULL
    )


def by_place(blocks, batch):
    stacked = jnp.stack(blocks)
    return [
        lax.dynamic_index_in_dim(stacked, jnp.bitwise_xor(batch, a), 0, keepdims=False)
        for a in range(4)
    ]


def exchange(blocks):
    return [blocks[0], swap_x(blocks[1]), swap_y(blocks[2]), swap_xy(blocks[3])]


def hidden_blocks(weights, batch):
    places = [
        jnp.concatenate(
            [w[:, a * (w.shape[1] // 4) : (a + 1) * (w.shape[1] // 4)] for w in weights], axis=1
        )
        for a in range(4)
    ]
    return lax.optimization_barrier(exchange(by_place(places, batch)))


def gather_width(shard):
    return lax.all_gather(shard, "seq", axis=0, tiled=True)


def shard_of(blocks, batch):
    return jnp.concatenate(by_place(blocks, batch), axis=0)


def scatter_width(grad):
    return lax.psum_scatter(grad, "seq", scatter_dimension=0, tiled=True)


def rows_by_place(part, batch):
    rows = part.shape[0] // 4
    return by_place([part[a * rows : (a + 1) * rows] for a in range(4)], batch)


def gather_rows(own, then=(), between=()):
    first, last = own
    late_first, late_last = lax.optimization_barrier((first, last, *between))[:2]
    x_first, y_last, x_last, y_first = lax.optimization_barrier(
        (swap_x(first), swap_y(last), swap_x(late_last), swap_y(late_first), *then)
    )[:4]
    d_first, d_last = lax.optimization_barrier((swap_y(x_first), swap_x(y_last)))
    return [first, last, x_first, x_last, y_first, y_last, d_first, d_last]


def scatter_rows(terms, then=()):
    mine, x_first, x_last, y_first, y_last, d_first, d_last = terms
    by_x, by_y, gx_first, gy_last = lax.optimization_barrier(
        (swap_x(d_first), swap_y(d_last), swap_x(x_first), swap_y(y_last), *then)
    )[:4]
    x_last = (x_last + by_y.astype(FULL)).astype(LOW)
    y_first = (y_first + by_x.astype(FULL)).astype(LOW)
    gx_last, gy_first = lax.optimization_barrier((swap_x(x_last), swap_y(y_first)))
    return [mine, gx_first, gx_last, gy_first, gy_last], (x_last, y_first)


def sum_tokens(v):
    got = swap_x(v)
    v = v + jnp.stack([got[1], got[0], got[3], got[2]])
    got = swap_y(v)
    return v + jnp.stack([got[2], got[3], got[0], got[1]])


def sum_all(v, count):
    v = v + swap_x(v)
    v = v + swap_y(v)
    step = 1
    while step < count:
        v = v + lax.ppermute(v, "seq", [(i, i ^ step) for i in range(count)])
        step *= 2
    return v


def enter(product, last, count, back):
    def shift(pair, k):
        hops = [(i, i + k) for i in range(count - k)]
        return lax.ppermute(pair, "seq", [(b, a) for a, b in hops] if back else hops)

    def link(earlier, later):
        return jnp.stack([earlier[0] * later[0], later[0] * earlier[1] + later[1]])

    ends = jnp.stack([product, last])
    value = shift(ends, 1)
    step = 2
    while step < count:
        value = link(shift(link(value, ends), step), value)
        step *= 2
    return value[1]


def call(kernel, arrays, outs, scratch, cost, first=()):
    count = len(arrays)
    arrays = [*arrays, *first]

    def body(*refs):
        kernel(*refs[:count], *refs[len(arrays) :])

    return pl.pallas_call(
        body,
        in_specs=[ANYWHERE] * len(arrays),
        out_specs=[ANYWHERE] * len(outs),
        out_shape=[jax.ShapeDtypeStruct(shape, kind) for shape, kind in outs],
        scratch_shapes=[
            pltpu.SemaphoreType.DMA(v) if isinstance(v[0], int) else pltpu.VMEM(*v) for v in scratch
        ],
        compiler_params=pltpu.CompilerParams(vmem_limit_bytes=VMEM_BYTES),
        cost_estimate=pl.CostEstimate(
            flops=0, bytes_accessed=int(cost * 3.5e6), transcendentals=0
        ),
    )(*arrays)


def copy_in(source, target, sem):
    copy = pltpu.make_async_copy(source, target, sem)
    copy.start()
    return copy


def wait_all(copies):
    for copy in copies:
        copy.wait()


def dot_kernel(n, first, wide, *refs):
    xs, ws, out, (x_s, w_s, o_s, x_sem, w_sem, out_sem) = (
        refs[: 2 * n],
        refs[2 * n : 2 * n + 2],
        refs[2 * n + 2],
        refs[2 * n + 3 :],
    )
    rows = x_s.shape[1] // 2
    cols = pl.ds(first, wide)
    loads_w = [copy_in(ws[0].at[:, cols], w_s.at[0], w_sem.at[0])]
    loads = []
    for p, x in enumerate(xs):
        x = x.at[:, pl.ds(0, x_s.shape[2])]
        loads.append(copy_in(x, x_s.at[p // 2, pl.ds(p % 2 * rows, rows)], x_sem.at[p]))
        if p == 1:
            loads_w.append(copy_in(ws[1].at[:, cols], w_s.at[1], w_sem.at[1]))
    stores = []
    for r in range(n):
        wait_all(loads[2 * r : 2 * r + 2])
        for h in range(2):
            if r == 0:
                loads_w[h].wait()
            o_s[2 * r + h] = contract(x_s[r], w_s[h], 1, 0)
            at = pl.ds((2 * r + h) * 2 * rows, 2 * rows)
            stores.append(copy_in(o_s.at[2 * r + h], out.at[at], out_sem.at[2 * r + h]))
    wait_all(stores)


def rows_dot(xs, ws, first, wide, cost=7):
    n, rows, depth = len(xs) // 2, xs[0].shape[0], ws[0].shape[0]
    return call(
        functools.partial(dot_kernel, n, first, wide),
        [*xs, *ws],
        [((4 * n * rows, wide), FULL)],
        [
            ((n, 2 * rows, depth), LOW),
            ((2, depth, wide), LOW),
            ((2 * n, 2 * rows, wide), FULL),
            (2 * n,),
            (2,),
            (2 * n,),
        ],
        cost,
    )[0]


def acts_kernel(n, *refs):
    xs, w, outs, held, (x_s, w_s, sem, out_sem) = (
        refs[: 2 * n],
        refs[2 * n],
        refs[2 * n + 1 : 2 * n + 4],
        refs[2 * n + 4 : 2 * n + 7],
        refs[2 * n + 7 :],
    )
    rows, unit = x_s.shape[1] // 2, held[0].shape[1]
    load_w = copy_in(w, w_s, sem.at[2 * n])
    loads = [
        copy_in(x, x_s.at[p // 2, pl.ds(p % 2 * rows, rows)], sem.at[p]) for p, x in enumerate(xs)
    ]
    load_w.wait()
    stores = []
    for r in range(n):
        wait_all(loads[2 * r : 2 * r + 2])
        acts = contract(x_s[r], w_s[...], 1, 0)
        g, u = acts[:, :unit], acts[:, unit:]
        at = pl.ds(r * 2 * rows, 2 * rows)
        held[0][at, :] = g
        held[1][at, :] = u
        held[2][at, :unit] = (g * jax.nn.sigmoid(g) * u).astype(LOW)
        held[2][at, unit:] = jnp.zeros((2 * rows, held[2].shape[1] - unit), LOW)
        for k in range(3):
            stores.append(copy_in(held[k].at[at], outs[k].at[at], out_sem.at[r, k]))
    wait_all(stores)


def rows_acts(xs, w):
    n, (rows, depth), unit = len(xs) // 2, xs[0].shape, w.shape[1] // 2
    padded = pl.cdiv(unit, 128) * 128
    outs = [((2 * n * rows, v), kind) for v, kind in ((unit, FULL), (unit, FULL), (padded, LOW))]
    return call(
        functools.partial(acts_kernel, n),
        [*xs, w],
        outs,
        [*outs, ((n, 2 * rows, depth), LOW), (w.shape, LOW), (2 * n + 1,), (n, 3)],
        12,
    )


def grad_kernel(x_at, y_at, more, *refs):
    n = len(y_at)
    outs, (x_s, y_s, m_s), held = refs[-5 - 2 * n - 2 : -5 - n - 2], refs[-5 - n - 2 : -4 - n], refs[-4 - n : -4]
    x_sem, y_sem, m_sem, out_sem = refs[-4:]
    wide = held[0].shape[1]
    chunks = [chunk for group in y_at for chunk in group]
    each = y_s.shape[1] // len(chunks)
    loads = []
    for g, (target, places) in enumerate(((x_s, x_at), *[(y_s, v) for v in chunks])):
        start = 0
        for k, (i, first, rows) in enumerate(places):
            at = target.at[pl.ds(start, rows)]
            if g:
                at = target.at[pl.ds(start, rows), pl.ds((g - 1) * each, each)]
            sem = y_sem.at[g - 1, k] if g else x_sem.at[k]
            source = refs[i].at[pl.ds(first, rows), pl.ds(0, at.shape[1])]
            loads.append(copy_in(source, at, sem))
            start += rows
    if more is not None:
        load_more = copy_in(refs[more], m_s, m_sem.at[0])
    wait_all(loads)
    depth, stores = x_s.shape[1], []
    for block, first in enumerate(range(0, depth, 256)):
        cols = pl.ds(first, min(256, depth - first))
        total = contract(x_s[:, cols], y_s[...], 0, 0)
        if more is not None:
            if block == 0:
                load_more.wait()
            total = total + m_s[cols, :].astype(FULL)
        for g in range(n):
            held[g][cols, :] = total[:, g * wide : (g + 1) * wide].astype(LOW)
            stores.append(copy_in(held[g].at[cols], outs[g].at[cols], out_sem.at[g, block]))
    wait_all(stores)


def rows_grad(xs, groups, cost, more=None, depth=None):
    arrays, x_at, y_at = list(xs), [(k, 0, x.shape[0]) for k, x in enumerate(xs)], []
    for group in groups:
        y_at.append([])
        for chunk in group:
            y_at[-1].append([])
            for v, first, rows in chunk:
                found = [k for k, other in enumerate(arrays) if other is v]
                if not found:
                    found = [len(arrays)]
                    arrays.append(v)
                y_at[-1][-1].append((found[0], first, rows))
    count = sum(rows for _, _, rows in x_at)
    depth = depth or xs[0].shape[1]
    n, each = len(groups), groups[0][0][0][0].shape[1]
    wide = each * len(groups[0])
    at = None
    if more is not None:
        at = len(arrays)
        arrays.append(more)
    outs = [((depth, wide), LOW)] * n
    return call(
        functools.partial(grad_kernel, x_at, y_at, at),
        arrays,
        outs,
        [
            ((count, depth), LOW),
            ((count, n * wide), LOW),
            ((depth if more is not None else 16, wide), LOW),
            *outs,
            (len(x_at),),
            (n * len(groups[0]), len(y_at[0][0])),
            (1,),
            (n, pl.cdiv(depth, 256)),
        ],
        cost,
    )


def block_pieces(v, half, seg):
    return [(v, (2 * r + half) * seg, seg) for r in range(4)]


PIECES = (((0, 2, FULL),), ((0, 1, LOW), (1, 2, FULL)), ((0, 1, FULL), (1, 2, LOW)), ((0, 1, LOW), (1, 2, LOW)))


def term_outs(picked, seg, wide):
    return [
        (((b - a) * seg // 2, wide), kind) for r in picked for a, b, kind in PIECES[r]
    ]


def store_term(term, r, seg, held, outs, sem, start):
    stores = []
    for k, (a, b, kind) in enumerate(PIECES[r]):
        held[start + k][...] = term[a * seg // 2 : b * seg // 2].astype(kind)
        stores.append(copy_in(held[start + k], outs[start + k], sem.at[start + k]))
    return stores


def term_kernel(picked, parts, count, *refs):
    n = sum(len(PIECES[r]) for r in picked)
    arrays, outs, held = refs[:count], refs[count : count + n], refs[count + n : count + 2 * n]
    scratch = refs[count + 2 * n :]
    l_s, w_s = scratch[: len(parts)], scratch[len(parts) : 2 * len(parts)]
    l_sem, w_sem, out_sem = scratch[2 * len(parts) :]
    seg = l_s[0].shape[1]
    loads, loads_w = [], []
    for k, r in enumerate(picked):
        loads.append([])
        for p, (left, (each, half), w, first, depth) in enumerate(parts):
            if k == 0:
                source = arrays[w].at[:, pl.ds(first, depth)]
                loads_w.append(copy_in(source, w_s[p], w_sem.at[p]))
            at = pl.ds((each * r + half) * seg, seg)
            loads[k].append(copy_in(arrays[left].at[at], l_s[p].at[k], l_sem.at[k, p]))
    stores, start = [], 0
    for k, r in enumerate(picked):
        term = None
        for p in range(len(parts)):
            loads[k][p].wait()
            if k == 0:
                loads_w[p].wait()
            part = contract(l_s[p][k], w_s[p][...], 1, 1)
            term = part if term is None else term + part
        stores += store_term(term, r, seg, held, outs, out_sem, start)
        start += len(PIECES[r])
    wait_all(stores)


def rows_terms(parts, picked, seg, first=(), cost=0):
    arrays, places = [], []
    for left, block, w, column in parts:
        at = []
        for v in (left, w):
            found = [k for k, other in enumerate(arrays) if other is v]
            if not found:
                found = [len(arrays)]
                arrays.append(v)
            at.append(found[0])
        places.append((at[0], block, at[1], column, left.shape[1]))
    wide = parts[0][2].shape[0]
    outs = term_outs(picked, seg, wide)
    return call(
        functools.partial(term_kernel, picked, places, len(arrays)),
        arrays,
        outs,
        [
            *outs,
            *[((len(picked), seg, depth), LOW) for *_, depth in places],
            *[((wide, depth), LOW) for *_, depth in places],
            (len(picked), len(parts)),
            (len(parts),),
            (len(outs),),
        ],
        cost,
        first,
    )


def back_kernel(picked, *refs):
    n = len(picked)
    m = sum(len(PIECES[r]) for r in picked)
    dys, gates, ups, downs, mlps, d_acts = (
        refs[: 2 * n],
        refs[2 * n : 2 * n + 2],
        refs[2 * n + 2 : 2 * n + 4],
        refs[2 * n + 4 : 2 * n + 6],
        refs[2 * n + 6 : 2 * n + 8],
        refs[2 * n + 8],
    )
    outs, held = refs[2 * n + 9 : 2 * n + 9 + m], refs[2 * n + 9 + m : 2 * n + 9 + 2 * m]
    y_s, g_s, u_s, down_s, mlp_s, a_s, y_sem, act_sem, w_sem, a_sem, out_sem = refs[
        2 * n + 9 + 2 * m :
    ]
    seg, unit = g_s.shape[2:]
    loads_w, loads_y, loads_act = [], [], []
    for k, r in enumerate(picked):
        at = pl.ds(r * seg, seg)
        loads_y.append(
            [
                copy_in(
                    dys[2 * k + p], y_s.at[k, pl.ds(p * seg // 2, seg // 2)], y_sem.at[k, p]
                )
                for p in range(2)
            ]
        )
        loads_act.append([])
        for h in range(2):
            if k == 0:
                loads_w.append(copy_in(downs[h], down_s.at[h], w_sem.at[h, 0]))
            loads_act[k].append(
                [
                    copy_in(gates[h].at[at], g_s.at[k, h], act_sem.at[k, h, 0]),
                    copy_in(ups[h].at[at], u_s.at[k, h], act_sem.at[k, h, 1]),
                ]
            )
            if k == 0:
                loads_w.append(copy_in(mlps[h], mlp_s.at[h], w_sem.at[h, 1]))
    stores, start = [], 0
    for k, r in enumerate(picked):
        wait_all(loads_y[k])
        term = None
        for h in range(2):
            if k == 0:
                loads_w[2 * h].wait()
            d_hidden = contract(y_s[k], down_s[h], 1, 0)[:, :unit]
            wait_all(loads_act[k][h])
            g, u = g_s[k, h], u_s[k, h]
            sig = jax.nn.sigmoid(g)
            a_s[k, h, :, :unit] = (d_hidden * u * sig * (1.0 + g * (1.0 - sig))).astype(LOW)
            a_s[k, h, :, unit:] = (d_hidden * (g * sig)).astype(LOW)
            at = pl.ds((2 * k + h) * seg, seg)
            stores.append(copy_in(a_s.at[k, h], d_acts.at[at], a_sem.at[k, h]))
            if k == 0:
                loads_w[2 * h + 1].wait()
            part = contract(a_s[k, h], mlp_s[h], 1, 1)
            term = part if term is None else term + part
        stores += store_term(term, r, seg, held, outs, out_sem, start)
        start += len(PIECES[r])
    wait_all(stores)


def rows_back(dys, gates, ups, downs, mlps, picked, seg, cost):
    n, (wide, both) = len(picked), mlps[0].shape
    unit = both // 2
    outs = term_outs(picked, seg, wide)
    return call(
        functools.partial(back_kernel, picked),
        [*[dys[2 * r + p] for r in picked for p in range(2)], *gates, *ups, *downs, *mlps],
        [((2 * n * seg, both), LOW), *outs],
        [
            *outs,
            ((n, seg, wide), LOW),
            ((n, 2, seg, unit), FULL),
            ((n, 2, seg, unit), FULL),
            ((2, *downs[0].shape), LOW),
            ((2, wide, both), LOW),
            ((n, 2, seg, both), LOW),
            (n, 2),
            (n, 2, 2),
            (2, 2),
            (n, 2),
            (len(outs),),
        ],
        cost,
    )


def channel_call(kernel, arrays, outs, scratch=(), cost=0):
    def spec(shape, skip=0):
        if shape[1] == 1:
            return pl.BlockSpec(shape, lambda i: (0, 0))
        return pl.BlockSpec((shape[0], 128), lambda i: (0, i + skip))

    skips = [v[1] if isinstance(v, tuple) else 0 for v in arrays]
    arrays = [v[0] if isinstance(v, tuple) else v for v in arrays]

    return pl.pallas_call(
        kernel,
        grid=(2,),
        in_specs=[spec(v.shape, skip) for v, skip in zip(arrays, skips)],
        out_specs=[spec(shape) for shape, _ in outs],
        out_shape=[jax.ShapeDtypeStruct(shape, kind) for shape, kind in outs],
        scratch_shapes=[pltpu.VMEM(*v) for v in scratch],
        compiler_params=pltpu.CompilerParams(vmem_limit_bytes=VMEM_BYTES),
        cost_estimate=pl.CostEstimate(
            flops=0, bytes_accessed=int(cost * 3.5e6), transcendentals=0
        ),
    )(*arrays)


def forward_scan(seg, rows, decay_ref, input_ref, state_ref, product_ref):
    def body(t, carry):
        h, p = carry
        at = pl.ds(t, rows, stride=seg)
        d = decay_ref[at, :]
        h = d * h + input_ref[at, :]
        p = d * p
        state_ref[at, :] = h
        product_ref[at, :] = p
        return h, p

    first = pl.ds(0, rows, stride=seg)
    h, p = input_ref[first, :], decay_ref[first, :]
    state_ref[first, :] = h
    product_ref[first, :] = p
    lax.fori_loop(1, seg, body, (h, p), unroll=5)


def backward_scan(seg, rows, decay_ref, input_ref, state_ref, product_ref):
    def body(k, carry):
        h, p, d = carry
        at = pl.ds(seg - 1 - k, rows, stride=seg)
        h = d * h + input_ref[at, :]
        p = d * p
        state_ref[at, :] = h
        product_ref[at, :] = p
        return h, p, decay_ref[at, :]

    last = pl.ds(seg - 1, rows, stride=seg)
    h, p = input_ref[last, :], decay_ref[last, :]
    state_ref[last, :] = h
    product_ref[last, :] = jnp.ones_like(p)
    at = pl.ds(seg - 2, rows, stride=seg)
    h = p * h + input_ref[at, :]
    state_ref[at, :] = h
    product_ref[at, :] = p
    lax.fori_loop(2, seg, body, (h, p, decay_ref[at, :]), unroll=2)


def scan_kernel(seg, proj_in, proj_forget, bound, keep, decay, local, product, inputs):
    rows = bound.shape[0]
    for k in range(rows):
        at = pl.ds(k * seg, seg)
        low = bound[pl.ds(k, 1), :]
        forget = low + (1.0 - low) * jax.nn.sigmoid(proj_forget[at, :])
        v = proj_in[at, :]
        decay[at, :] = forget * keep[at, :]
        inputs[at, :] = v * jax.nn.sigmoid(v) * (1.0 - forget)
    forward_scan(seg, rows, decay, inputs, local, product)


def state_kernel(seg, local, product, carry, gate, gain, state, gated, squares):
    first = pl.program_id(0) == 0
    for k in range(carry.shape[0]):
        at, one = pl.ds(k * seg, seg), pl.ds(k, 1)
        h = local[at, :] + product[at, :] * carry[one, :]
        g = gate[at, :]
        state[at, :] = h
        gated[at, :] = (h * gain[one, :] * (g * jax.nn.sigmoid(g))).astype(LOW)
        total = jnp.sum(h * h, axis=-1, keepdims=True)
        squares[at, :] = jnp.where(first, 0.0, squares[at, :]) + total


def gate_back_kernel(
    seg, wide, d_gated, gate, state, gain, inverse, dot, decay, gated, d_gate, gain_sum, local, product, held
):
    rows = gain.shape[0]
    for k in range(rows):
        at, one = pl.ds(k * seg, seg), pl.ds(k, 1)
        up, g, h, scale, inv = d_gated[at, :], gate[at, :], state[at, :], gain[one, :], inverse[at, :]
        sig = jax.nn.sigmoid(g)
        act, normed = g * sig, h * inv
        gated[at, :] = (normed * scale * act).astype(LOW)
        d_gate[at, :] = (up * normed * scale * sig * (1.0 + g * (1.0 - sig))).astype(LOW)
        gain_sum[one, :] = jnp.sum(up * normed * act, axis=0, keepdims=True)
        shrink = inv * inv * inv * (dot[at, :] * (1.0 / wide))
        held[at, :] = inv * (up * scale * act) - h * shrink
    backward_scan(seg, rows, decay, held, local, product)


def scan_back_kernel(
    seg, local, product, returned, state, carry, proj_in, proj_forget, bound, keep, d_in_ref, d_forget_ref, bound_sum
):
    for k in range(bound.shape[0]):
        at, one = pl.ds(k * seg, seg), pl.ds(k, 1)
        lam = local[at, :] + product[at, :] * returned[one, :]
        h = state[at, :]
        step = lax.broadcasted_iota(jnp.int32, h.shape, 0)
        previous = jnp.where(step == 0, carry[one, :], pltpu.roll(h, 1, 0))
        low, v = bound[one, :], proj_in[at, :]
        sig_forget, sig_in = jax.nn.sigmoid(proj_forget[at, :]), jax.nn.sigmoid(v)
        forget = low + (1.0 - low) * sig_forget
        d_forget = lam * (previous * keep[at, :] - v * sig_in)
        d_in = lam * (1.0 - forget) * sig_in * (1.0 + v * (1.0 - sig_in))
        d_in_ref[at, :] = d_in.astype(LOW)
        d_forget_ref[at, :] = (d_forget * (1.0 - low) * sig_forget * (1.0 - sig_forget)).astype(LOW)
        bound_sum[one, :] = jnp.sum(d_forget * (1.0 - sig_forget), axis=0, keepdims=True)


STEP = 32


def token_call(kernel, arrays, outs, seg, wide, cost=5):
    half = seg // 2

    def spec(shape):
        if shape[0] == 1:
            return pl.BlockSpec(shape, lambda i: (0, 0))
        if shape[0] == 2:
            return pl.BlockSpec((2, STEP, shape[2]), lambda i: (0, i, 0))
        return pl.BlockSpec((STEP, shape[1]), lambda i: (i, 0))

    def folded(shape):
        return (2, half, shape[1]) if shape[0] == seg else shape

    arrays = [v.reshape(folded(v.shape)) for v in arrays]
    got = pl.pallas_call(
        kernel,
        grid=(half // STEP,),
        in_specs=[spec(v.shape) for v in arrays],
        out_specs=[spec(folded(shape)) for shape, _ in outs],
        out_shape=[jax.ShapeDtypeStruct(folded(shape), kind) for shape, kind in outs],
        compiler_params=pltpu.CompilerParams(vmem_limit_bytes=VMEM_BYTES),
        cost_estimate=pl.CostEstimate(
            flops=0, bytes_accessed=int(cost * 3.5e6), transcendentals=0
        ),
    )(*arrays)
    return [v.reshape(shape) for v, (shape, _) in zip(got, outs)]


def both_rows(core, mine, got):
    return jnp.where(core == 0, jnp.stack([mine, got]), jnp.stack([got, mine]))


def final_kernel(place, core, *refs):
    mlp, mixer, (mine, got), refs = refs[:4], refs[4:8], refs[8:10], refs[10:]
    outs, (m_s, x_s, t_s), refs = refs[:8], refs[8:11], refs[11:]
    held, (sem, out_sem) = refs[:7], refs[7:]
    rows = [copy_in(v, t_s.at[k], sem.at[8 + k]) for k, v in enumerate((mine, got))]
    loads = [copy_in(v, m_s.at[k], sem.at[k]) for k, v in enumerate(mlp)]
    loads += [copy_in(v, x_s.at[k], sem.at[4 + k]) for k, v in enumerate(mixer)]
    wait_all(rows)
    stores = [
        copy_in(t_s.at[0], outs[7].at[core[0]], out_sem.at[7]),
        copy_in(t_s.at[1], outs[7].at[1 - core[0]], out_sem.at[8]),
    ]
    wait_all(loads)
    chan, unit = held[0].shape[1] // 4, held[4].shape[1] // 4
    for a in range(4):
        block = jnp.bitwise_xor(place[0], a)
        m, x = m_s[block].astype(FULL), x_s[block].astype(FULL)
        for k in range(3):
            held[k][:, a * chan : (a + 1) * chan] = x[:, k * chan : (k + 1) * chan]
        held[3][a * chan : (a + 1) * chan, :] = x[:, 3 * chan : 4 * chan].T
        for k in range(2):
            held[4 + k][:, a * unit : (a + 1) * unit] = m[:, k * unit : (k + 1) * unit]
        held[6][a * unit : (a + 1) * unit, :] = m[:, 2 * unit : 3 * unit].T
    stores += [copy_in(held[k], outs[k], out_sem.at[k]) for k in range(7)]
    wait_all(stores)


def final(place, core, mlp, mixer, mine, got, half, hidden, first):
    rows = mixer[0].shape[0]
    outs = [((rows, half), FULL)] * 3 + [((half, rows), FULL)]
    outs += [((rows, hidden), FULL)] * 2 + [((hidden, rows), FULL)]
    arrays = [*mlp, *mixer, mine, got, *first]
    more = [((2, *mine.shape), FULL)]

    def body(place_ref, core_ref, *refs):
        final_kernel(place_ref, core_ref, *refs[:10], *refs[len(arrays) :])

    return pl.pallas_call(
        body,
        in_specs=[pl.BlockSpec(memory_space=pltpu.SMEM)] * 2 + [ANYWHERE] * len(arrays),
        out_specs=[ANYWHERE] * 8,
        out_shape=[jax.ShapeDtypeStruct(shape, kind) for shape, kind in outs + more],
        scratch_shapes=[
            pltpu.VMEM((4, *mlp[0].shape), LOW),
            pltpu.VMEM((4, *mixer[0].shape), LOW),
            pltpu.VMEM((2, *mine.shape), FULL),
            *[pltpu.VMEM(*v) for v in outs],
            pltpu.SemaphoreType.DMA((10,)),
            pltpu.SemaphoreType.DMA((9,)),
        ],
        compiler_params=pltpu.CompilerParams(vmem_limit_bytes=VMEM_BYTES),
    )(place.reshape(1), core.reshape(1), *arrays)


def total_of(refs, h):
    mine, gx_first, gx_last, gy_first, gy_last = refs
    got_x, got_y = ((gx_first, gy_first), (gx_last, gy_last))[h]
    return mine[h] + got_x[...].astype(FULL) + got_y[...].astype(FULL)


def inverse_of(v):
    return lax.rsqrt(jnp.mean(v * v, axis=-1, keepdims=True) + EPSILON)


def enter_kernel(tok, gain, first, last, inverse):
    for h, out in enumerate((first, last)):
        v = tok[h].astype(FULL)
        inv = inverse_of(v)
        out[...] = (v * inv * gain[...]).astype(LOW)
        inverse[h] = inv


def mixed_kernel(*refs):
    *sums, tok, inv_state, gain, mix, resid, first, last, inverse = refs
    for h, out in enumerate((first, last)):
        raw = total_of(sums, h)
        v = tok[h].astype(FULL) + inv_state[h] * raw
        inv = inverse_of(v)
        mix[h] = raw
        resid[h] = v
        out[...] = (v * inv * gain[...]).astype(LOW)
        inverse[h] = inv


def norm_back(upstream, v, scale, inv):
    weighted = upstream * scale
    mean = jnp.mean(weighted * v, axis=-1, keepdims=True)
    return inv * weighted - v * (inv * inv * inv * mean)


def add_rows(ref, v):
    total = jnp.sum(v, axis=0, keepdims=True)

    @pl.when(pl.program_id(0) == 0)
    def _():
        ref[...] = jnp.zeros_like(ref)

    ref[...] += total


def d_mlp_kernel(*refs):
    *sums, resid, inverse, cot_first, cot_last, gain, mix, d_resid, first, last, gain_sum = refs
    terms = 0.0
    for h, (cot, out) in enumerate(((cot_first, first), (cot_last, last))):
        up, v, inv = total_of(sums, h), resid[h], inverse[h]
        terms = terms + up * v * inv
        grad = cot[...].astype(FULL) + norm_back(up, v, gain[...], inv)
        low = grad.astype(LOW)
        d_resid[h] = grad
        wide = low.shape[1]
        out[:, :wide] = low
        dot = jnp.sum(low.astype(FULL) * mix[h], axis=-1, keepdims=True)
        high = dot.astype(LOW)
        dot = dot - high.astype(FULL)
        middle = dot.astype(LOW)
        rest = (dot - middle.astype(FULL)).astype(LOW)
        lane = lax.broadcasted_iota(jnp.int32, (low.shape[0], 128), 1)
        parts = jnp.where(lane == 1, middle.astype(FULL), jnp.where(lane == 2, rest.astype(FULL), 0.0))
        out[:, wide:] = jnp.where(lane == 0, high.astype(FULL), parts).astype(LOW)
    add_rows(gain_sum, terms)


def d_in_kernel(*refs):
    *sums, tok, inverse, gain, d_resid, grad, gain_sum = refs
    terms = 0.0
    for h in range(2):
        up, v, inv = total_of(sums, h), tok[h].astype(FULL), inverse[h]
        terms = terms + up * v * inv
        grad[h] = d_resid[h] + norm_back(up, v, gain[...], inv)
    add_rows(gain_sum, terms)


def out_kernel(*refs):
    *sums, resid, out = refs
    for h in range(2):
        out[h] = (resid[h] + total_of(sums, h)).astype(LOW)


def shards(
    tokens_in,
    grad_out,
    w_input,
    w_forget,
    w_outgate,
    w_out,
    mlp_gate,
    mlp_up,
    mlp_down,
    gain_mixer,
    gain_mlp,
    gain_state,
    bound_param,
    layer_index,
    doc_lengths,
):
    rows, seg, width = tokens_in.shape
    half = gain_state.shape[0]
    chan = half // 4
    unit = mlp_gate.shape[1] // 4
    segments = lax.axis_size("seq")
    core = lax.axis_index("mp")
    batch = lax.axis_index("batch")
    place = lax.axis_index("seq")
    piece = (seg // 2, width)
    wider = (seg // 2, width + 128)
    whole = (seg, width)
    column = (seg, 1)

    def own_other(v):
        return [v, swap_core(v)]

    mixer = hidden_blocks((w_input, w_forget, w_outgate, w_out.T), batch)
    shard = shard_of(mixer, batch)
    w_scan, w_gates = gather_width(shard[:, : 2 * chan]), gather_width(shard[:, 2 * chan :])
    layers = bound_param.shape[0]
    layer = jnp.arange(layers, dtype=jnp.int32)[:, None]
    used = jnp.logical_and(layer >= 1, layer <= layer_index[0]).astype(FULL)
    table = jnp.concatenate([bound_param, gain_state.astype(FULL)[None]])
    table = jnp.stack(own_other(lax.dynamic_slice_in_dim(table, batch * chan, chan, 1)))
    bound = jnp.tile(jnp.sum(jax.nn.softmax(table[:, :layers], axis=1) * used, axis=1), (4, 1))
    gain_three = jnp.tile(table[:, layers], (4, 1))
    lengths = lax.dynamic_slice_in_dim(doc_lengths, core, 1, 0)
    lengths = jnp.concatenate([lengths, swap_x(lengths)])
    lengths = jnp.concatenate([lengths, swap_y(lengths)])
    starts = jnp.cumsum(lengths, axis=1) - lengths
    places = place * seg + jnp.arange(seg, dtype=jnp.int32)
    resets = jnp.any(places[None, :, None] == starts[:, None, :], axis=2).astype(FULL)
    keep_mask = jnp.repeat(1.0 - resets, 2, axis=0).reshape(8 * seg, 1)
    mlp_blocks = hidden_blocks((after(mlp_gate, lengths, table, *mixer), mlp_up, mlp_down.T), batch)
    shard = shard_of(mlp_blocks, batch)
    w_mlp, down = gather_width(shard[:, : 2 * unit]), shard[:, 2 * unit :]
    down = jnp.pad(down, ((0, 0), (0, -unit % 128)))

    gain_one = gain_mixer.astype(FULL)[None]
    gain_two = gain_mlp.astype(FULL)[None]
    tok_own, cot_own = lax.optimization_barrier(
        [lax.dynamic_index_in_dim(v, core, 0, keepdims=False) for v in (tokens_in, grad_out)]
    )

    def by_row(v):
        return v.reshape(8, seg, chan)

    def columns(v):
        return jnp.repeat(v, 2, axis=0).reshape(8 * seg, 1)

    channel = ((8 * seg, chan), FULL)

    *normed, inv_one = token_call(
        enter_kernel,
        [tok_own, gain_one],
        [(piece, LOW), (piece, LOW), (column, FULL)],
        seg,
        width,
    )
    normed = lax.optimization_barrier((*normed, *mixer))[:2]
    normed_in = gather_rows(normed, (), mlp_blocks)
    w_scan = own_other(after(w_scan, normed_in[6]))
    proj_scan = rows_dot(normed_in, w_scan, 0, 2 * chan, 0)
    proj_in, proj_forget = (proj_scan, 0), (proj_scan, chan // 128)
    decay, local_state, cum_decay = channel_call(
        functools.partial(scan_kernel, seg),
        [proj_in, proj_forget, bound, keep_mask],
        [channel] * 3,
        [((8 * seg, 128), FULL)],
    )
    w_gates = own_other(after(w_gates, local_state))
    carry_in = enter(by_row(cum_decay)[:, -1], by_row(local_state)[:, -1], segments, False)
    cot_pieces = [cot_own[: seg // 2], cot_own[seg // 2 :]]
    proj_gate = rows_dot(normed_in, w_gates, 0, chan, 0)
    carry_in = after(carry_in, proj_gate)
    state, gated_raw, squares = channel_call(
        functools.partial(state_kernel, seg),
        [local_state, cum_decay, carry_in, proj_gate, gain_three],
        [channel, ((8 * seg, chan), LOW), ((8 * seg, 1), FULL)],
    )
    square_total = sum_tokens(jnp.sum(squares.reshape(4, 2, seg), axis=1))
    inv_all = lax.rsqrt(square_total / width + EPSILON)
    inv_own = inv_all[0][:, None]
    gated_raw = after(gated_raw, square_total)

    def two_step(parts, cost=5, behind=False):
        diag = rows_terms(parts, (3,), seg, cost=cost)
        first = settled(*diag) if behind else diag[0]
        rest = rows_terms(parts, (1, 2, 0), seg, (first,))
        return [rest[4], *rest[:4], *diag]

    mix_parts = [(gated_raw, (2, h), w_gates[h], chan) for h in range(2)]
    mix_sums, _ = scatter_rows(two_step(mix_parts))
    mix_raw, resid, *normed, inv_two = token_call(
        mixed_kernel,
        [*mix_sums, tok_own, inv_own, gain_two],
        [(whole, FULL), (whole, FULL), (piece, LOW), (piece, LOW), (column, FULL)],
        seg,
        width,
    )

    normed_mlp = gather_rows(normed)
    cot_pieces = lax.optimization_barrier((*cot_pieces, normed_mlp[6]))[:2]
    w_mlp = own_other(after(w_mlp, normed_mlp[2]))
    acts = [rows_acts(normed_mlp, w) for w in w_mlp]
    gate_act, up_act, hidden = zip(*acts)
    cot_all = gather_rows(cot_pieces, (hidden[1],))

    def hidden_pieces(h):
        return [(hidden[h], r * seg, seg) for r in range(4)]

    (grad_other,) = rows_grad(cot_all, [[hidden_pieces(1)]], 7)
    (grad_down,) = rows_grad(cot_all, [[hidden_pieces(0)]], 8, swap_core(grad_other))
    w_down = gather_width(after(down, normed_mlp[2]))
    w_down = own_other(after(w_down, *hidden))
    w_down[0] = after(w_down[0], grad_down)
    grad_down = scatter_width(grad_down)
    d_acts = {}

    def back_terms(picked, cost, *first):
        downs = [after(w_down[0], *first), w_down[1]] if first else w_down
        d_acts[picked], *terms = rows_back(cot_all, gate_act, up_act, downs, w_mlp, picked, seg, cost)
        return terms

    diag = back_terms((3,), 13)
    sides = back_terms((1, 2), 0, diag[0])
    mine = back_terms((0,), 0, sides[0])
    mlp_sums, sent = scatter_rows([*mine, *sides, *diag], tuple(mine))
    def d_act_pieces(h):
        return [
            (d_acts[picked], (2 * k + h) * seg, seg)
            for picked, k in (((0,), 0), ((1, 2), 0), ((1, 2), 1), ((3,), 0))
        ]

    normed_mlp[0] = after(normed_mlp[0], *sent)
    (grad_other,) = rows_grad(normed_mlp, [[d_act_pieces(1)]], 0)
    mlp_sums[0] = after(mlp_sums[0], grad_other)

    d_resid, *d_low, gain_two_sum = token_call(
        d_mlp_kernel,
        [*mlp_sums, resid, inv_two, *cot_all[:2], gain_two, mix_raw],
        [(whole, FULL), (wider, LOW), (wider, LOW), ((1, width), FULL)],
        seg,
        width,
    )
    hidden = [after(hidden[0], *d_low), hidden[1]]
    out_terms = two_step([(hidden[h], (1, 0), w_down[h], 0) for h in range(2)], 0)
    d_resid_all = gather_rows(d_low)
    normed_mlp[0] = after(normed_mlp[0], *d_low)
    (grad_mlp,) = rows_grad(normed_mlp, [[d_act_pieces(0)]], 0, swap_core(grad_other))
    d_resid_all[6] = after(d_resid_all[6], grad_mlp, *out_terms)
    grad_mlp = scatter_width(grad_mlp)
    out_terms = list(lax.optimization_barrier((*out_terms, d_resid_all[6]))[:-1])
    out_sums, sent = scatter_rows(out_terms)
    dot_total = jnp.stack([v[:, width : width + 128] for v in d_resid_all]).astype(FULL)
    dot_total = jnp.sum(dot_total, axis=-1).reshape(4, seg)
    d_gated = rows_dot(d_resid_all, w_gates, chan, chan)
    gated, d_proj_gate, gain_three_grad, back_local, back_prod = channel_call(
        functools.partial(gate_back_kernel, seg, width),
        [
            d_gated,
            proj_gate,
            state,
            gain_three,
            columns(inv_all),
            columns(dot_total),
            after(decay, grad_down),
        ],
        [((8 * seg, chan), LOW)] * 2 + [((8, chan), FULL)] + [channel] * 2,
        [((8 * seg, 128), FULL)],
    )
    both = [
        rows_grad(xs, [[block_pieces(v, h, seg)] for h in range(2)], 0, None, width)
        for xs, v in ((normed_in, d_proj_gate), (d_resid_all, gated))
    ]
    grad_gates = [jnp.concatenate([v[h] for v in both], axis=1) for h in range(2)]
    first_decay = by_row(decay)[:, 0]
    returned = enter(
        first_decay * by_row(back_prod)[:, 0],
        first_decay * by_row(back_local)[:, 0],
        segments,
        True,
    )

    def chip_sum(own, other):
        return (own.astype(FULL) + swap_core(other).astype(FULL)).astype(LOW)

    grad_gates = chip_sum(*grad_gates)
    mlp_places = rows_by_place(jnp.concatenate([grad_mlp, grad_down], axis=1), batch)
    returned = after(returned, grad_gates, *mlp_places, *out_sums)
    grad_gates = scatter_width(grad_gates)
    *d_scan, bound_grad = channel_call(
        functools.partial(scan_back_kernel, seg),
        [
            back_local,
            back_prod,
            returned,
            state,
            carry_in,
            proj_in,
            proj_forget,
            bound,
            keep_mask,
        ],
        [((8 * seg, chan), LOW), ((8 * seg, chan), LOW), ((8, chan), FULL)],
    )
    grad_scan = rows_grad(
        normed_in, [[block_pieces(v, h, seg) for v in d_scan] for h in range(2)], 0
    )
    grad_scan = chip_sum(*grad_scan)
    d_scan[0] = after(d_scan[0], grad_scan)
    grad_scan = scatter_width(grad_scan)
    in_parts = [(d_scan[k], (2, h), w_scan[h], k * chan) for h in range(2) for k in range(2)]
    in_parts += [(d_proj_gate, (2, h), w_gates[h], 0) for h in range(2)]
    in_sums, sent = scatter_rows(two_step(in_parts, 5, True), (grad_gates,))
    in_sums[0] = after(in_sums[0], grad_scan)
    behind = settled(*sent)
    mlp = exchange(list(lax.optimization_barrier((*mlp_places, behind))[:4]))
    grad_own, gain_one_sum = token_call(
        d_in_kernel,
        [*in_sums, tok_own, inv_one, gain_one, d_resid],
        [(whole, FULL), ((1, width), FULL)],
        seg,
        width,
        0,
    )
    mixer = exchange(rows_by_place(jnp.concatenate([grad_scan, grad_gates], axis=1), batch))

    def own_rest(v):
        return (
            lax.dynamic_index_in_dim(v, core, 0, keepdims=False),
            lax.dynamic_index_in_dim(v, 1 - core, 0, keepdims=False),
        )

    (out_own,) = token_call(out_kernel, [*out_sums, after(resid, grad_own)], [(whole, LOW)], seg, width)
    out_keep, out_send = own_rest(jnp.stack([out_own[:, :half], out_own[:, half:]]))
    tokens_out = both_rows(core, out_keep, swap_core(out_send))

    gains = jnp.concatenate([gain_one_sum, gain_two_sum]).reshape(2, 2, half)
    gains_keep, gains_send = own_rest(jnp.swapaxes(gains, 0, 1))
    channels = lax.dynamic_update_slice_in_dim(
        jnp.zeros((2, 2, half), FULL),
        jnp.sum(jnp.stack([gain_three_grad, bound_grad]).reshape(2, 4, 2, chan), axis=1).swapaxes(0, 1),
        batch * chan,
        2,
    )
    small = jnp.concatenate([gains_keep, channels[0]]) + swap_core(
        jnp.concatenate([gains_send, channels[1]])
    )
    small = sum_all(after(small, *mlp), segments)
    soft = jax.nn.softmax(bound_param, axis=0)
    grad_table = small[3] * soft * (used - jnp.sum(soft * used, axis=0))
    *grads, grad_tokens = final(
        batch, core, mlp, mixer, grad_own, swap_core(grad_own), half, 4 * unit, (behind,)
    )
    return (tokens_out, grad_tokens, *grads, small[0], small[1], small[2], grad_table)


def solution(mesh):
    return jax.shard_map(
        shards,
        mesh=mesh,
        in_specs=(
            P("batch", "seq", None),
            P("batch", "seq", None),
            P(("seq", "batch"), "mp"),
            P(("seq", "batch"), "mp"),
            P(("seq", "batch"), "mp"),
            P("mp", ("seq", "batch")),
            P(("seq", "batch"), "mp"),
            P(("seq", "batch"), "mp"),
            P("mp", ("seq", "batch")),
            P(),
            P(),
            P("mp"),
            P(None, "mp"),
            P(),
            P("batch", None),
        ),
        out_specs=(
            P("batch", "seq", "mp"),
            P("batch", "seq", None),
            P(("seq", "batch"), "mp"),
            P(("seq", "batch"), "mp"),
            P(("seq", "batch"), "mp"),
            P("mp", ("seq", "batch")),
            P(("seq", "batch"), "mp"),
            P(("seq", "batch"), "mp"),
            P("mp", ("seq", "batch")),
            P("mp"),
            P("mp"),
            P("mp"),
            P(None, "mp"),
        ),
        check_vma=False,
    )
```

time: 723 us -> 677 us (0.936)
  Pallas kernels: 13 us -> 264 us
  matrix products: 151 us -> 0 us
  waiting for transfers between devices: 296 us -> 217 us
  other arithmetic: 66.6 us -> 26.7 us
  local copies, waits for them, and re-layouts: 70.6 us -> 53.5 us
  starting transfers between devices: 99.2 us -> 90.1 us
    pallas_call x2 -> x31, Pallas kernels: 13 us -> 264 us  [the longest x21 194 us: call(): pl.pallas_call(body, in_specs=[ANYWHERE] * len(arrays), out_specs=[ANYWHE...]
    dot_general x50 -> x0, matrix products: 151 us -> none  [the longest x5 55.7 us: plain_dot(): return jnp.dot(left, right, preferred_element_type=jnp.float32)]
    ppermute x28 -> x31, waiting for transfers between devices: 96.4 us -> 59.4 us  [swap_y(): return lax.ppermute(v, 'batch', [(i, i ^ 2) for i in range(4)])]
    reduce_scatter x4, waiting for transfers between devices: 45 us -> 9.55 us  [scatter_width(): return lax.psum_scatter(grad, 'seq', scatter_dimension=0, tiled=True)]
    unnamed x187 -> x189, local copies, waits for them, and re-layouts: 42.9 us -> 19.8 us
    ppermute x28 -> x31, waiting for transfers between devices: 121 us -> 104 us  [swap_x(): return lax.ppermute(v, 'batch', [(i, i ^ 1) for i in range(4)])]
    reduce_sum x8 -> x3, other arithmetic: 16 us -> 0.18 us  [the longest x1 0.14 us: shards(): dot_total = jnp.sum(dot_total, axis=-1).reshape(4, seg)]
    ppermute x35 -> x14, waiting for transfers between devices: 2.97 us -> 14.7 us  [swap_core(): return lax.ppermute(v, 'mp', [(0, 1), (1, 0)])]
  transfers between devices with their start and end apart: 116 -> 94, of which waited for: 51 -> 54; matrix products, arithmetic and copies ran while one was open for 35% -> 9% of each run, Pallas kernels for 2% -> 36%
where the time goes in v2:
time: 677 us; the launch traced here: 668 us
  Pallas kernels  264 us (39%)
  waiting for transfers between devices  217 us (32%)
  starting transfers between devices  90.1 us (13%)
  local copies, waits for them, and re-layouts  53.5 us (8%)
  other arithmetic  26.7 us (4%)
  between operations  17.1 us (3%)
    pallas_call x21, Pallas kernels, call(): pl.pallas_call(body, in_specs=[ANYWHERE] * len(arrays), out_specs=[ANYWHE...  194 us
    ppermute x31, waiting for transfers between devices, swap_x(): return lax.ppermute(v, 'batch', [(i, i ^ 1) for i in range(4)])  104 us
    ppermute x31, waiting for transfers between devices, swap_y(): return lax.ppermute(v, 'batch', [(i, i ^ 2) for i in range(4)])  59.4 us
    pallas_call x4, Pallas kernels, channel_call(): pl.pallas_call(kernel, grid=(2,), in_specs=[spec(v.shape, skip) for v, sk...  36.2 us
    ppermute x31, starting transfers between devices, swap_y(): return lax.ppermute(v, 'batch', [(i, i ^ 2) for i in range(4)])  32.9 us
    ppermute x31, starting transfers between devices, swap_x(): return lax.ppermute(v, 'batch', [(i, i ^ 1) for i in range(4)])  30.3 us
    pallas_call x5, Pallas kernels, token_call(): pl.pallas_call(kernel, grid=(half // STEP,), in_specs=[spec(v.shape) for...  26.7 us
    unnamed x189, local copies, waits for them, and re-layouts  19.8 us
  transfers between devices with their start and end apart: 94, of which 54 were waited for; matrix products, arithmetic and copies ran while one was open for 9% of the time, Pallas kernels for 36%

profile of v2, /device:TPU:0, one launch (start us, length us, event | category | flops | bytes accessed | tf_op | source)
XLA Modules:
  0.0 667.6 jit_solution(3172344380303876588)
XLA Ops:
  10.8 4.0 collective-permute-start.2
  15.4 6.5 collective-permute-done.2
  21.9 4.7 collective-permute-done.1
  42.5 3.6 shard_map.246
  48.2 4.8 collective-permute-done.10
  53.0 8.7 %collective-permute-done.9 = bf16[128,2112]{0,1:T(8,128)(2,1)S(1)} collective-permute-done((bf16[128,2112]{0,1:T(8,128)(2,1)S(1)}, bf16[128,2112]{0,1:T(8,128)(2,1)S(1)}, u32[]{:S(2)}, u32[]{:S(2)}) %collective-permute-start.9) | collective-permute-done | bytes 540704 | tf_op jit(solution)/shard_map/ppermute | solution.py:22
  61.7 2.9 collective-permute-done.8
  77.2 6.6 collective-permute-done.11.refs_3_
  86.1 11.8 %collective-permute-done.13.refs_6_ = bf16[128,2048]{1,0:T(8,128)(2,1)S(1)} collective-permute-done((bf16[128,2048]{1,0:T(8,128)(2,1)S(1)}, bf16[128,2048]{1,0:T(8,128)(2,1)S(1)}, u32[]{:S(2)}, u32[]{:S(2)}) %collective-permute-start.13) | collective-permute-done | bytes 524320 | tf_op jit(solution)/shard_map/ppermute | solution.py:22
  105.4 8.8 %shard_map.247.proj_in.proj_forget = f32[2048,512]{1,0:T(8,128)} custom-call(bf16[128,2048]{1,0:T(8,128)(2,1)} %get-tuple-element.212.refs_0_, bf16[128,2048]{1,0:T(8,128)(2,1)} %get-tuple-element.211.refs_1_, bf16[128,2048]{1,0:T(8,128)(2,1)} %copy-done.7, bf16[128,2048]{1,0:T(8,128)(2,1)} %copy-done.9, bf16[128,2048]{1,0:T(8,128)(2,1)} %copy-done.10, ...), custom_call_target="tpu_custom_call" | custom-call | tf_op jit(solution)/shard_map/pallas_call | solution.py:148
  114.2 10.2 %shard_map.248 = (f32[2048,256]{1,0:T(8,128)}, f32[2048,256]{1,0:T(8,128)}, f32[2048,256]{1,0:T(8,128)}) custom-call(f32[2048,512]{1,0:T(8,128)} %shard_map.247.proj_in.proj_forget, f32[2048,512]{1,0:T(8,128)} %shard_map.247.proj_in.proj_forget, f32[8,256]{1,0:T(8,128)} %tile.20.bound, f32[2048,1]{1,0:T(8,128)} %reshape_reshape.12.keep), custom_call_target="tpu_custom_call" | custom-call | tf_op jit(solution)/shard_map/pallas_call | solution.py:515
  126.5 3.5 collective-permute-start.16
  131.4 5.4 collective-permute-start.17
  140.1 6.7 shard_map.249.gate
  146.8 4.7 shard_map.250
  154.3 2.5 collective-permute-done.19
  158.0 2.5 collective-permute-done.20
  160.6 3.3 shard_map.251
  166.0 5.7 shard_map.252
  173.8 3.9 collective-permute-done.22
  180.0 6.5 collective-permute-done.23.refs_1_
  192.0 6.3 collective-permute-done.25.refs_2_
  200.1 5.7 shard_map.253
  209.9 10.7 %collective-permute-done.29.refs_3_ = bf16[128,2048]{1,0:T(8,128)(2,1)S(1)} collective-permute-done((bf16[128,2048]{1,0:T(8,128)(2,1)}, bf16[128,2048]{1,0:T(8,128)(2,1)S(1)}, u32[]{:S(2)}, u32[]{:S(2)}) %collective-permute-start.29) | collective-permute-done | bytes 524320 | tf_op jit(solution)/shard_map/ppermute | solution.py:18
  221.3 4.8 collective-permute-done.27.refs_2_
  235.5 10.0 %collective-permute-done.32.refs_7_ = bf16[128,2048]{1,0:T(8,128)(2,1)S(1)} collective-permute-done((bf16[128,2048]{1,0:T(8,128)(2,1)S(1)}, bf16[128,2048]{1,0:T(8,128)(2,1)S(1)}, u32[]{:S(2)}, u32[]{:S(2)}) %collective-permute-start.32) | collective-permute-done | bytes 524320 | tf_op jit(solution)/shard_map/ppermute | solution.py:18
  250.7 11.9 %shard_map.255 = (f32[1024,704]{1,0:T(8,128)}, f32[1024,704]{1,0:T(8,128)}, bf16[1024,768]{1,0:T(8,128)(2,1)}) custom-call(bf16[128,2048]{1,0:T(8,128)(2,1)} %get-tuple-element.309.refs_0_, bf16[128,2048]{1,0:T(8,128)(2,1)} %get-tuple-element.242.refs_1_, bf16[128,2048]{1,0:T(8,128)(2,1)} %copy-done.15, bf16[128,2048]{1,0:T(8,128)(2,1)} %copy-done.13, ...), custom_call_target="tpu_custom_call" | custom-call | bytes 42000000 | tf_op jit(solution)/shard_map/pallas_call | solution.py:148
  262.7 8.6 %collective-permute-done.34.refs_2_.refs_0_ = bf16[128,2048]{1,0:T(8,128)(2,1)S(1)} collective-permute-done((bf16[128,2048]{1,0:T(8,128)(2,1)S(1)}, bf16[128,2048]{1,0:T(8,128)(2,1)S(1)}, u32[]{:S(2)}, u32[]{:S(2)}) %collective-permute-start.34) | collective-permute-done | bytes 524320 | tf_op jit(solution)/shard_map/ppermute | solution.py:18
  274.5 12.3 %shard_map.254 = (f32[1024,704]{1,0:T(8,128)}, f32[1024,704]{1,0:T(8,128)}, bf16[1024,768]{1,0:T(8,128)(2,1)}) custom-call(bf16[128,2048]{1,0:T(8,128)(2,1)} %get-tuple-element.309.refs_0_, bf16[128,2048]{1,0:T(8,128)(2,1)} %get-tuple-element.242.refs_1_, bf16[128,2048]{1,0:T(8,128)(2,1)} %copy-done.15, bf16[128,2048]{1,0:T(8,128)(2,1)} %copy-done.13, ...), custom_call_target="tpu_custom_call" | custom-call | bytes 42000000 | tf_op jit(solution)/shard_map/pallas_call | solution.py:148
  288.4 7.0 %shard_map.256 = bf16[2048,768]{1,0:T(8,128)(2,1)} custom-call(bf16[128,2048]{1,0:T(8,128)(2,1)} %copy-done.6, bf16[128,2048]{1,0:T(8,128)(2,1)} %copy-done.5, bf16[128,2048]{1,0:T(8,128)(2,1)} %copy-done.26, bf16[128,2048]{1,0:T(8,128)(2,1)} %copy-done.24, bf16[128,2048]{1,0:T(8,128)(2,1)} %copy-done.25, bf16[128,2048]{1,0:T(8,128)(2,1)} %copy-done.27, ...), custom_call_target="tpu_custom_call" | custom-call | bytes 24500000 | tf_op jit(solution)/shard_map/pallas_call | solution.py:148
  296.0 8.9 %collective-permute-done.40.refs_9_ = bf16[2048,768]{1,0:T(8,128)(2,1)} collective-permute-done((bf16[2048,768]{1,0:T(8,128)(2,1)}, bf16[2048,768]{1,0:T(8,128)(2,1)}, u32[]{:S(2)}, u32[]{:S(2)}) %collective-permute-start.40) | collective-permute-done | bytes 3145760 | tf_op jit(solution)/shard_map/ppermute | solution.py:30
  304.9 8.0 %shard_map.257 = bf16[2048,768]{1,0:T(8,128)(2,1)} custom-call(bf16[128,2048]{1,0:T(8,128)(2,1)} %copy-done.6, bf16[128,2048]{1,0:T(8,128)(2,1)} %copy-done.5, bf16[128,2048]{1,0:T(8,128)(2,1)} %copy-done.26, bf16[128,2048]{1,0:T(8,128)(2,1)} %copy-done.24, bf16[128,2048]{1,0:T(8,128)(2,1)} %copy-done.25, bf16[128,2048]{1,0:T(8,128)(2,1)} %copy-done.27, ...), custom_call_target="tpu_custom_call" | custom-call | bytes 28000000 | tf_op jit(solution)/shard_map/pallas_call | solution.py:148
  314.6 13.8 %shard_map.258 = (bf16[512,1408]{1,0:T(8,128)(2,1)}, bf16[128,2048]{1,0:T(8,128)(2,1)}, bf16[128,2048]{1,0:T(8,128)(2,1)}) custom-call(bf16[128,2048]{1,0:T(8,128)(2,1)} %copy-done.28, bf16[128,2048]{1,0:T(8,128)(2,1)} %copy-done.29, f32[1024,704]{1,0:T(8,128)} %get-tuple-element.255.refs_2_.refs_4_, f32[1024,704]{1,0:T(8,128)} %get-tuple-element.256.refs_3_.refs_5_, ...), custom_call_target="tpu_custom_call" | custom-call | bytes 45500000 | tf_op jit(solution)/shard_map/pallas_call | solution.py:148
  329.2 19.9 %shard_map.259 = (bf16[1024,1408]{1,0:T(8,128)(2,1)}, bf16[128,2048]{1,0:T(8,128)(2,1)}, f32[128,2048]{1,0:T(8,128)}, f32[128,2048]{1,0:T(8,128)}, bf16[128,2048]{1,0:T(8,128)(2,1)}) custom-call(bf16[128,2048]{1,0:T(8,128)(2,1)} %copy-done.26, bf16[128,2048]{1,0:T(8,128)(2,1)} %copy-done.24, bf16[128,2048]{1,0:T(8,128)(2,1)} %copy-done.25, ...), custom_call_target="tpu_custom_call" | custom-call | tf_op jit(solution)/shard_map/pallas_call | solution.py:148
  352.8 14.6 %shard_map.260 = (bf16[512,1408]{1,0:T(8,128)(2,1)}, f32[256,2048]{1,0:T(8,128)}) custom-call(bf16[128,2048]{1,0:T(8,128)(2,1)} %copy-done.6, bf16[128,2048]{1,0:T(8,128)(2,1)} %copy-done.5, f32[1024,704]{1,0:T(8,128)} %get-tuple-element.255.refs_2_.refs_4_, f32[1024,704]{1,0:T(8,128)} %get-tuple-element.256.refs_3_.refs_5_, ...), custom_call_target="tpu_custom_call" | custom-call | tf_op jit(solution)/shard_map/pallas_call | solution.py:148
  369.1 10.9 %shard_map.261 = bf16[2048,1408]{1,0:T(8,128)(2,1)} custom-call(bf16[128,2048]{1,0:T(8,128)(2,1)} %get-tuple-element.309.refs_0_, bf16[128,2048]{1,0:T(8,128)(2,1)} %get-tuple-element.242.refs_1_, bf16[128,2048]{1,0:T(8,128)(2,1)} %copy-done.15, bf16[128,2048]{1,0:T(8,128)(2,1)} %copy-done.13, bf16[128,2048]{1,0:T(8,128)(2,1)} %copy-done.14, ...), custom_call_target="tpu_custom_call" | custom-call | tf_op jit(solution)/shard_map/pallas_call | solution.py:148
  380.3 14.1 %collective-permute-done.46.refs_2_ = bf16[128,2048]{1,0:T(8,128)(2,1)S(1)} collective-permute-done((bf16[128,2048]{1,0:T(8,128)(2,1)S(1)}, bf16[128,2048]{1,0:T(8,128)(2,1)S(1)}, u32[]{:S(2)}, u32[]{:S(2)}) %collective-permute-start.46) | collective-permute-done | bytes 524320 | tf_op jit(solution)/shard_map/ppermute | solution.py:18
  395.4 7.1 %shard_map.262 = (f32[2,128,2048]{2,1,0:T(8,128)}, bf16[128,2176]{1,0:T(8,128)(2,1)}, bf16[128,2176]{1,0:T(8,128)(2,1)}, f32[1,2048]{1,0:T(1,128)}) custom-call(f32[2,128,2048]{2,1,0:T(8,128)} %bitcast.200, bf16[128,2048]{1,0:T(8,128)(2,1)} %copy-done.70, bf16[128,2048]{1,0:T(8,128)(2,1)} %copy-done.71, bf16[128,2048]{1,0:T(8,128)(2,1)} %copy-done.72, ...), custom_call_target="tpu_custom_call" | custom-call | bytes 17500000 | tf_op jit(solution)/shard_map/pallas_call | solution.py:645
  402.5 2.5 copy-done.19
  405.0 12.7 %shard_map.265 = bf16[2048,1408]{1,0:T(8,128)(2,1)} custom-call(bf16[128,2048]{1,0:T(8,128)(2,1)} %get-tuple-element.309.refs_0_, bf16[128,2048]{1,0:T(8,128)(2,1)} %get-tuple-element.242.refs_1_, bf16[128,2048]{1,0:T(8,128)(2,1)} %copy-done.15, bf16[128,2048]{1,0:T(8,128)(2,1)} %copy-done.13, bf16[128,2048]{1,0:T(8,128)(2,1)} %copy-done.14, ...), custom_call_target="tpu_custom_call" | custom-call | tf_op jit(solution)/shard_map/pallas_call | solution.py:148
  424.7 5.8 shard_map.263
  430.5 10.9 %shard_map.264 = (bf16[128,2048]{1,0:T(8,128)(2,1)}, f32[128,2048]{1,0:T(8,128)}, f32[128,2048]{1,0:T(8,128)}, bf16[128,2048]{1,0:T(8,128)(2,1)}, f32[256,2048]{1,0:T(8,128)}) custom-call(bf16[1024,768]{1,0:T(8,128)(2,1)} %get-tuple-element.296.refs_8_.refs_0_, bf16[2048,768]{1,0:T(8,128)(2,1)} %all-gather.11.cloned.1.call-done.refs_6_.refs_8_.refs_1_, ...), custom_call_target="tpu_custom_call" | custom-call | tf_op jit(solution)/shard_map/pallas_call | solution.py:148
  441.5 3.5 collective-permute-done.48.refs_2_
  447.9 10.9 %collective-permute-done.52.refs_6_ = bf16[128,2176]{1,0:T(8,128)(2,1)S(1)} collective-permute-done((bf16[128,2176]{1,0:T(8,128)(2,1)S(1)}, bf16[128,2176]{1,0:T(8,128)(2,1)S(1)}, u32[]{:S(2)}, u32[]{:S(2)}) %collective-permute-start.52) | collective-permute-done | bytes 557088 | tf_op jit(solution)/shard_map/ppermute | solution.py:22
  465.9 6.7 %shard_map.266.d_gated = f32[2048,256]{1,0:T(8,128)} custom-call(bf16[128,2176]{1,0:T(8,128)(2,1)} %get-tuple-element.305.refs_0_, bf16[128,2176]{1,0:T(8,128)(2,1)} %get-tuple-element.304.refs_1_, bf16[128,2176]{1,0:T(8,128)(2,1)} %copy-done.35, bf16[128,2176]{1,0:T(8,128)(2,1)} %copy-done.33, bf16[128,2176]{1,0:T(8,128)(2,1)} %copy-done.34, ...), custom_call_target="tpu_custom_call" | custom-call | bytes 24500000 | tf_op jit(solution)/shard_map/pallas_call | solution.py:148
  472.6 13.6 %shard_map.267 = (bf16[2048,256]{1,0:T(8,128)(2,1)}, bf16[2048,256]{1,0:T(8,128)(2,1)}, f32[8,256]{1,0:T(8,128)}, f32[2048,256]{1,0:T(8,128)}, f32[2048,256]{1,0:T(8,128)}) custom-call(f32[2048,256]{1,0:T(8,128)} %shard_map.266.d_gated, f32[2048,256]{1,0:T(8,128)} %shard_map.249.gate, f32[2048,256]{1,0:T(8,128)} %get-tuple-element.327.state, ...), custom_call_target="tpu_custom_call" | custom-call | tf_op jit(solution)/shard_map/pallas_call | solution.py:515
  486.2 5.8 shard_map.269
  492.1 5.9 shard_map.268
  510.9 7.1 %collective-permute-done.62 = f32[2,8,256]{2,1,0:T(8,128)S(1)} collective-permute-done((f32[2,8,256]{2,1,0:T(8,128)S(1)}, f32[2,8,256]{2,1,0:T(8,128)S(1)}, u32[]{:S(2)}, u32[]{:S(2)}) %collective-permute-start.62) | collective-permute-done | bytes 16416 | tf_op jit(solution)/shard_map/ppermute | solution.py:127
  526.6 7.7 %shard_map.270 = (bf16[2048,256]{1,0:T(8,128)(2,1)}, bf16[2048,256]{1,0:T(8,128)(2,1)}, f32[8,256]{1,0:T(8,128)}) custom-call(f32[2048,256]{1,0:T(8,128)} %get-tuple-element.330.local, f32[2048,256]{1,0:T(8,128)} %get-tuple-element.331.product, f32[8,256]{1,0:T(8,128)} %fusion.21.returned, f32[2048,256]{1,0:T(8,128)} %get-tuple-element.327.state, ...), custom_call_target="tpu_custom_call" | custom-call | tf_op jit(solution)/shard_map/pallas_call | solution.py:515
  534.3 8.6 %shard_map.271 = (bf16[2048,512]{1,0:T(8,128)(2,1)}, bf16[2048,512]{1,0:T(8,128)(2,1)}) custom-call(bf16[128,2048]{1,0:T(8,128)(2,1)} %get-tuple-element.212.refs_0_, bf16[128,2048]{1,0:T(8,128)(2,1)} %get-tuple-element.211.refs_1_, bf16[128,2048]{1,0:T(8,128)(2,1)} %copy-done.7, bf16[128,2048]{1,0:T(8,128)(2,1)} %copy-done.9, bf16[128,2048]{1,0:T(8,128)(2,1)} %copy-done.10, ...), custom_call_target="tpu_custom_call" | custom-call | tf_op jit(solution)/shard_map/pallas_call | solution.py:148
  542.9 4.4 collective-permute-done.64
  547.3 3.6 add_convert_fusion
  551.0 4.8 shard_map.272
  559.7 10.4 %shard_map.273 = (bf16[128,2048]{1,0:T(8,128)(2,1)}, f32[128,2048]{1,0:T(8,128)}, f32[128,2048]{1,0:T(8,128)}, bf16[128,2048]{1,0:T(8,128)(2,1)}, f32[256,2048]{1,0:T(8,128)}) custom-call(bf16[2048,256]{1,0:T(8,128)(2,1)} %get-tuple-element.343.refs_8_.refs_0_, bf16[2048,512]{1,0:T(8,128)(2,1)} %all-gather.5.cloned.1.call-done.refs_8_.refs_1_, ...), custom_call_target="tpu_custom_call" | custom-call | tf_op jit(solution)/shard_map/pallas_call | solution.py:148
  572.0 12.1 %collective-permute-done.68.refs_1_ = bf16[128,2048]{1,0:T(8,128)(2,1)S(1)} collective-permute-done((bf16[128,2048]{1,0:T(8,128)(2,1)}, bf16[128,2048]{1,0:T(8,128)(2,1)S(1)}, u32[]{:S(2)}, u32[]{:S(2)}) %collective-permute-start.68) | collective-permute-done | bytes 524320 | tf_op jit(solution)/shard_map/ppermute | solution.py:18
  594.0 7.4 %collective-permute-done.70.refs_2_ = bf16[128,2048]{1,0:T(8,128)(2,1)S(1)} collective-permute-done((bf16[128,2048]{1,0:T(8,128)(2,1)S(1)}, bf16[128,2048]{1,0:T(8,128)(2,1)S(1)}, u32[]{:S(2)}, u32[]{:S(2)}) %collective-permute-start.70) | collective-permute-done | bytes 524320 | tf_op jit(solution)/shard_map/ppermute | solution.py:18
  603.5 9.5 %reduce-scatter.9.cloned.1.call-done = bf16[512,512]{1,0:T(8,128)(2,1)} async-done(((bf16[2048,512]{1,0:T(8,128)(2,1)}), bf16[512,512]{1,0:T(8,128)(2,1)}) %reduce-scatter.9.cloned.1.call-update) | async-done | bytes 524304 | tf_op jit(solution)/shard_map/reduce_scatter | solution.py:78
  613.0 5.8 shard_map.274
  620.3 4.5 shard_map.275
  635.0 2.6 collective-permute-done.84
  646.4 3.2 collective-permute-done.79.refs_7_
  649.6 2.7 collective-permute-done.78.refs_6_
  653.8 6.4 shard_map.276
  (481 shorter events, 179.6 us)
Async XLA Ops:
  7.2 92.4 %all-gather.5.cloned.1.call-start = ((), (), s32[]{:S(2)}) async-start(), calls=%async_computation.4 | async-start | bytes 2621440 | tf_op jit(solution)/shard_map/all_gather | solution.py:70
  28.3 96.1 %all-gather.7.cloned.1.call-start = ((), (), s32[]{:S(2)}) async-start(), calls=%async_computation.5 | async-start | bytes 2621440 | tf_op jit(solution)/shard_map/all_gather | solution.py:70
  36.1 192.6 %all-gather.9.cloned.1.call-start = ((), (), s32[]{:S(2)}) async-start(), calls=%async_computation.6 | async-start | bytes 7208960 | tf_op jit(solution)/shard_map/all_gather | solution.py:70
  36.8 16.2 %collective-permute-start.10 = (bf16[128,2112]{0,1:T(8,128)(2,1)S(1)}, bf16[128,2112]{0,1:T(8,128)(2,1)S(1)}, u32[]{:S(2)}, u32[]{:S(2)}) collective-permute-start(bf16[128,2112]{0,1:T(8,128)(2,1)S(1)} %get-tuple-element.394), channel_id=1, source_target_pairs={{0,6},{2,4},{4,2},{6,0},{1,7},{3,5},{5,3},{7,1},{8,14},{10,12},{12... | collective-permute-start | bytes 1622024 | tf_op jit(solution)/shard_map/ppermute | solution.py:26
  38.4 23.3 %collective-permute-start.9 = (bf16[128,2112]{0,1:T(8,128)(2,1)S(1)}, bf16[128,2112]{0,1:T(8,128)(2,1)S(1)}, u32[]{:S(2)}, u32[]{:S(2)}) collective-permute-start(bf16[128,2112]{0,1:T(8,128)(2,1)S(1)} %get-tuple-element.395), channel_id=1, source_target_pairs={{0,4},{2,6},{4,0},{6,2},{1,5},{3,7},{5,1},{7,3},{8,12},{10,14},{12... | collective-permute-start | bytes 1622024 | tf_op jit(solution)/shard_map/ppermute | solution.py:22
  39.9 24.7 %collective-permute-start.8 = (bf16[128,2112]{0,1:T(8,128)(2,1)S(1)}, bf16[128,2112]{0,1:T(8,128)(2,1)S(1)}, u32[]{:S(2)}, u32[]{:S(2)}) collective-permute-start(bf16[128,2112]{0,1:T(8,128)(2,1)S(1)} %get-tuple-element.396), channel_id=1, source_target_pairs={{0,2},{2,0},{4,6},{6,4},{1,3},{3,1},{5,7},{7,5},{8,10},{10,8},{12,... | collective-permute-start | bytes 1622024 | tf_op jit(solution)/shard_map/ppermute | solution.py:18
  46.1 31.1 %collective-permute-start.3 = (bf16[128,2048]{1,0:T(8,128)(2,1)}, bf16[128,2048]{1,0:T(8,128)(2,1)S(1)}, u32[]{:S(2)}, u32[]{:S(2)}) collective-permute-start(bf16[128,2048]{1,0:T(8,128)(2,1)} %get-tuple-element.212.refs_0_), channel_id=1, source_target_pairs={{0,2},{2,0},{4,6},{6,4},{1,3},{3,1},{5,7},{7,5},{8,10},{10,8},{12,... | collective-permute-start | bytes 1572872 | tf_op jit(solution)/shard_map/ppermute | solution.py:18
  47.6 29.6 %collective-permute-start.4 = (bf16[128,2048]{1,0:T(8,128)(2,1)}, bf16[128,2048]{1,0:T(8,128)(2,1)S(1)}, u32[]{:S(2)}, u32[]{:S(2)}) collective-permute-start(bf16[128,2048]{1,0:T(8,128)(2,1)} %get-tuple-element.211.refs_1_), channel_id=1, source_target_pairs={{0,4},{2,6},{4,0},{6,2},{1,5},{3,7},{5,1},{7,3},{8,12},{10,14},{12... | collective-permute-start | bytes 1572872 | tf_op jit(solution)/shard_map/ppermute | solution.py:22
  64.6 19.2 %collective-permute-start.11 = (bf16[128,2048]{1,0:T(8,128)(2,1)}, bf16[128,2048]{1,0:T(8,128)(2,1)S(1)}, u32[]{:S(2)}, u32[]{:S(2)}) collective-permute-start(bf16[128,2048]{1,0:T(8,128)(2,1)} %get-tuple-element.211.refs_1_), channel_id=1, source_target_pairs={{0,2},{2,0},{4,6},{6,4},{1,3},{3,1},{5,7},{7,5},{8,10},{10,8},{12,... | collective-permute-start | bytes 1572872 | tf_op jit(solution)/shard_map/ppermute | solution.py:18
  65.2 18.9 %collective-permute-start.12 = (bf16[128,2048]{1,0:T(8,128)(2,1)}, bf16[128,2048]{1,0:T(8,128)(2,1)S(1)}, u32[]{:S(2)}, u32[]{:S(2)}) collective-permute-start(bf16[128,2048]{1,0:T(8,128)(2,1)} %get-tuple-element.212.refs_0_), channel_id=1, source_target_pairs={{0,4},{2,6},{4,0},{6,2},{1,5},{3,7},{5,1},{7,3},{8,12},{10,14},{12... | collective-permute-start | bytes 1572872 | tf_op jit(solution)/shard_map/ppermute | solution.py:22
  77.1 218.4 %all-gather.11.cloned.1.call-start = ((), (), s32[]{:S(2)}) async-start(), calls=%async_computation.7 | async-start | bytes 3932160 | tf_op jit(solution)/shard_map/all_gather | solution.py:70
  84.1 13.8 %collective-permute-start.13 = (bf16[128,2048]{1,0:T(8,128)(2,1)S(1)}, bf16[128,2048]{1,0:T(8,128)(2,1)S(1)}, u32[]{:S(2)}, u32[]{:S(2)}) collective-permute-start(bf16[128,2048]{1,0:T(8,128)(2,1)S(1)} %collective-permute-done.3.refs_2_), channel_id=1, source_target_pairs={{0,4},{2,6},{4,0},{6,2},{1,5},{3,7},{5,1},{7,3},{8,12},{10,14},{12... | collective-permute-start | bytes 1572872 | tf_op jit(solution)/shard_map/ppermute | solution.py:22
  85.2 13.6 %collective-permute-start.14 = (bf16[128,2048]{1,0:T(8,128)(2,1)S(1)}, bf16[128,2048]{1,0:T(8,128)(2,1)S(1)}, u32[]{:S(2)}, u32[]{:S(2)}) collective-permute-start(bf16[128,2048]{1,0:T(8,128)(2,1)S(1)} %collective-permute-done.4.refs_5_), channel_id=1, source_target_pairs={{0,2},{2,0},{4,6},{6,4},{1,3},{3,1},{5,7},{7,5},{8,10},{10,8},{12,... | collective-permute-start | bytes 1572872 | tf_op jit(solution)/shard_map/ppermute | solution.py:18
  124.4 14.4 %collective-permute-start.18 = (bf16[2048,512]{1,0:T(8,128)(2,1)}, bf16[2048,512]{1,0:T(8,128)(2,1)S(1)}, u32[]{:S(2)}, u32[]{:S(2)}) collective-permute-start(bf16[2048,512]{1,0:T(8,128)(2,1)} %all-gather.7.cloned.1.call-done.refs_8_.refs_1_.refs_5_), channel_id=1, source_target_pairs={{0,1},{1,0},{2,3},{3,2},{4,5},{5,4},{6,7},{7,6},{8,9},{9,8},{10,11... | collective-permute-start | bytes 6291464 | tf_op jit(solution)/shard_map/ppermute | solution.py:30
  163.9 13.8 %collective-permute-start.22 = (bf16[128,2048]{1,0:T(8,128)(2,1)}, bf16[128,2048]{1,0:T(8,128)(2,1)S(1)}, u32[]{:S(2)}, u32[]{:S(2)}) collective-permute-start(bf16[128,2048]{1,0:T(8,128)(2,1)} %get-tuple-element.229), channel_id=1, source_target_pairs={{0,4},{2,6},{4,0},{6,2},{1,5},{3,7},{5,1},{7,3},{8,12},{10,14},{12... | collective-permute-start | bytes 1572872 | tf_op jit(solution)/shard_map/ppermute | solution.py:22
  165.1 15.0 %collective-permute-start.21 = (bf16[128,2048]{1,0:T(8,128)(2,1)}, bf16[128,2048]{1,0:T(8,128)(2,1)S(1)}, u32[]{:S(2)}, u32[]{:S(2)}) collective-permute-start(bf16[128,2048]{1,0:T(8,128)(2,1)} %get-tuple-element.227.refs_3_), channel_id=1, source_target_pairs={{0,2},{2,0},{4,6},{6,4},{1,3},{3,1},{5,7},{7,5},{8,10},{10,8},{12,... | collective-permute-start | bytes 1572872 | tf_op jit(solution)/shard_map/ppermute | solution.py:18
  171.8 14.8 %collective-permute-start.23 = (bf16[128,2048]{1,0:T(8,128)(2,1)}, bf16[128,2048]{1,0:T(8,128)(2,1)S(1)}, u32[]{:S(2)}, u32[]{:S(2)}) collective-permute-start(bf16[128,2048]{1,0:T(8,128)(2,1)} %get-tuple-element.230), channel_id=1, source_target_pairs={{0,2},{2,0},{4,6},{6,4},{1,3},{3,1},{5,7},{7,5},{8,10},{10,8},{12,... | collective-permute-start | bytes 1572872 | tf_op jit(solution)/shard_map/ppermute | solution.py:18
  172.9 13.7 %collective-permute-start.24 = (bf16[128,2048]{1,0:T(8,128)(2,1)}, bf16[128,2048]{1,0:T(8,128)(2,1)S(1)}, u32[]{:S(2)}, u32[]{:S(2)}) collective-permute-start(bf16[128,2048]{1,0:T(8,128)(2,1)} %get-tuple-element.231), channel_id=1, source_target_pairs={{0,4},{2,6},{4,0},{6,2},{1,5},{3,7},{5,1},{7,3},{8,12},{10,14},{12... | collective-permute-start | bytes 1572872 | tf_op jit(solution)/shard_map/ppermute | solution.py:22
  205.8 14.8 %collective-permute-start.29 = (bf16[128,2048]{1,0:T(8,128)(2,1)}, bf16[128,2048]{1,0:T(8,128)(2,1)S(1)}, u32[]{:S(2)}, u32[]{:S(2)}) collective-permute-start(bf16[128,2048]{1,0:T(8,128)(2,1)} %get-tuple-element.242.refs_1_), channel_id=1, source_target_pairs={{0,2},{2,0},{4,6},{6,4},{1,3},{3,1},{5,7},{7,5},{8,10},{10,8},{12,... | collective-permute-start | bytes 1572872 | tf_op jit(solution)/shard_map/ppermute | solution.py:18
  206.9 14.4 %collective-permute-start.30 = (bf16[128,2048]{1,0:T(8,128)(2,1)}, bf16[128,2048]{1,0:T(8,128)(2,1)S(1)}, u32[]{:S(2)}, u32[]{:S(2)}) collective-permute-start(bf16[128,2048]{1,0:T(8,128)(2,1)} %get-tuple-element.309.refs_0_), channel_id=1, source_target_pairs={{0,4},{2,6},{4,0},{6,2},{1,5},{3,7},{5,1},{7,3},{8,12},{10,14},{12... | collective-permute-start | bytes 1572872 | tf_op jit(solution)/shard_map/ppermute | solution.py:22
  207.9 18.3 %collective-permute-start.27 = (bf16[128,2048]{1,0:T(8,128)(2,1)}, bf16[128,2048]{1,0:T(8,128)(2,1)S(1)}, u32[]{:S(2)}, u32[]{:S(2)}) collective-permute-start(bf16[128,2048]{1,0:T(8,128)(2,1)} %get-tuple-element.309.refs_0_), channel_id=1, source_target_pairs={{0,2},{2,0},{4,6},{6,4},{1,3},{3,1},{5,7},{7,5},{8,10},{10,8},{12,... | collective-permute-start | bytes 1572872 | tf_op jit(solution)/shard_map/ppermute | solution.py:18
  208.9 18.0 %collective-permute-start.28 = (bf16[128,2048]{1,0:T(8,128)(2,1)}, bf16[128,2048]{1,0:T(8,128)(2,1)S(1)}, u32[]{:S(2)}, u32[]{:S(2)}) collective-permute-start(bf16[128,2048]{1,0:T(8,128)(2,1)} %get-tuple-element.242.refs_1_), channel_id=1, source_target_pairs={{0,4},{2,6},{4,0},{6,2},{1,5},{3,7},{5,1},{7,3},{8,12},{10,14},{12... | collective-permute-start | bytes 1572872 | tf_op jit(solution)/shard_map/ppermute | solution.py:22
  228.7 22.0 %collective-permute-start.33 = (bf16[2048,1408]{1,0:T(8,128)(2,1)}, bf16[2048,1408]{1,0:T(8,128)(2,1)}, u32[]{:S(2)}, u32[]{:S(2)}) collective-permute-start(bf16[2048,1408]{1,0:T(8,128)(2,1)} %all-gather.9.cloned.1.call-done.refs_8_.refs_10_), channel_id=1, source_target_pairs={{0,1},{1,0},{2,3},{3,2},{4,5},{5,4},{6,7},{7,6},{8,9},{9,8},{10,11... | collective-permute-start | bytes 17301512 | tf_op jit(solution)/shard_map/ppermute | solution.py:30
  230.8 228.8 %reduce-scatter.5.cloned.1.call-start = ((), (), s32[]{:S(2)}) async-start(), calls=%async_computation.8 | async-start | bytes 3932160 | tf_op jit(solution)/shard_map/reduce_scatter | solution.py:78
  231.1 14.3 %collective-permute-start.32 = (bf16[128,2048]{1,0:T(8,128)(2,1)S(1)}, bf16[128,2048]{1,0:T(8,128)(2,1)S(1)}, u32[]{:S(2)}, u32[]{:S(2)}) collective-permute-start(bf16[128,2048]{1,0:T(8,128)(2,1)S(1)} %collective-permute-done.28.refs_5_), channel_id=1, source_target_pairs={{0,2},{2,0},{4,6},{6,4},{1,3},{3,1},{5,7},{7,5},{8,10},{10,8},{12,... | collective-permute-start | bytes 1572872 | tf_op jit(solution)/shard_map/ppermute | solution.py:18
  232.6 14.0 %collective-permute-start.31 = (bf16[128,2048]{1,0:T(8,128)(2,1)S(1)}, bf16[128,2048]{1,0:T(8,128)(2,1)S(1)}, u32[]{:S(2)}, u32[]{:S(2)}) collective-permute-start(bf16[128,2048]{1,0:T(8,128)(2,1)S(1)} %collective-permute-done.27.refs_2_), channel_id=1, source_target_pairs={{0,4},{2,6},{4,0},{6,2},{1,5},{3,7},{5,1},{7,3},{8,12},{10,14},{12... | collective-permute-start | bytes 1572872 | tf_op jit(solution)/shard_map/ppermute | solution.py:22
  246.7 16.0 %collective-permute-start.36 = (bf16[128,2048]{1,0:T(8,128)(2,1)S(1)}, bf16[128,2048]{1,0:T(8,128)(2,1)S(1)}, u32[]{:S(2)}, u32[]{:S(2)}) collective-permute-start(bf16[128,2048]{1,0:T(8,128)(2,1)S(1)} %get-tuple-element.262.refs_1_.refs_8_), channel_id=1, source_target_pairs={{0,2},{2,0},{4,6},{6,4},{1,3},{3,1},{5,7},{7,5},{8,10},{10,8},{12,... | collective-permute-start | bytes 1572872 | tf_op jit(solution)/shard_map/ppermute | solution.py:18
  247.2 15.5 %collective-permute-start.37 = (bf16[128,2048]{1,0:T(8,128)(2,1)S(1)}, bf16[128,2048]{1,0:T(8,128)(2,1)S(1)}, u32[]{:S(2)}, u32[]{:S(2)}) collective-permute-start(bf16[128,2048]{1,0:T(8,128)(2,1)S(1)} %get-tuple-element.263.refs_0_.refs_7_), channel_id=1, source_target_pairs={{0,4},{2,6},{4,0},{6,2},{1,5},{3,7},{5,1},{7,3},{8,12},{10,14},{12... | collective-permute-start | bytes 1572872 | tf_op jit(solution)/shard_map/ppermute | solution.py:22
  248.7 22.5 %collective-permute-start.34 = (bf16[128,2048]{1,0:T(8,128)(2,1)S(1)}, bf16[128,2048]{1,0:T(8,128)(2,1)S(1)}, u32[]{:S(2)}, u32[]{:S(2)}) collective-permute-start(bf16[128,2048]{1,0:T(8,128)(2,1)S(1)} %get-tuple-element.263.refs_0_.refs_7_), channel_id=1, source_target_pairs={{0,2},{2,0},{4,6},{6,4},{1,3},{3,1},{5,7},{7,5},{8,10},{10,8},{12,... | collective-permute-start | bytes 1572872 | tf_op jit(solution)/shard_map/ppermute | solution.py:18
  250.2 21.4 %collective-permute-start.35 = (bf16[128,2048]{1,0:T(8,128)(2,1)S(1)}, bf16[128,2048]{1,0:T(8,128)(2,1)S(1)}, u32[]{:S(2)}, u32[]{:S(2)}) collective-permute-start(bf16[128,2048]{1,0:T(8,128)(2,1)S(1)} %get-tuple-element.262.refs_1_.refs_8_), channel_id=1, source_target_pairs={{0,4},{2,6},{4,0},{6,2},{1,5},{3,7},{5,1},{7,3},{8,12},{10,14},{12... | collective-permute-start | bytes 1572872 | tf_op jit(solution)/shard_map/ppermute | solution.py:22
  271.6 15.1 %collective-permute-start.38 = (bf16[128,2048]{1,0:T(8,128)(2,1)S(1)}, bf16[128,2048]{1,0:T(8,128)(2,1)S(1)}, u32[]{:S(2)}, u32[]{:S(2)}) collective-permute-start(bf16[128,2048]{1,0:T(8,128)(2,1)S(1)} %collective-permute-done.34.refs_2_.refs_0_), channel_id=1, source_target_pairs={{0,4},{2,6},{4,0},{6,2},{1,5},{3,7},{5,1},{7,3},{8,12},{10,14},{12... | collective-permute-start | bytes 1572872 | tf_op jit(solution)/shard_map/ppermute | solution.py:22
  273.1 13.7 %collective-permute-start.39 = (bf16[128,2048]{1,0:T(8,128)(2,1)S(1)}, bf16[128,2048]{1,0:T(8,128)(2,1)S(1)}, u32[]{:S(2)}, u32[]{:S(2)}) collective-permute-start(bf16[128,2048]{1,0:T(8,128)(2,1)S(1)} %collective-permute-done.35.refs_5_.refs_3_), channel_id=1, source_target_pairs={{0,2},{2,0},{4,6},{6,4},{1,3},{3,1},{5,7},{7,5},{8,10},{10,8},{12,... | collective-permute-start | bytes 1572872 | tf_op jit(solution)/shard_map/ppermute | solution.py:18
  295.5 17.4 %collective-permute-start.41 = (bf16[2048,768]{1,0:T(8,128)(2,1)}, bf16[2048,768]{1,0:T(8,128)(2,1)S(1)}, u32[]{:S(2)}, u32[]{:S(2)}) collective-permute-start(bf16[2048,768]{1,0:T(8,128)(2,1)} %all-gather.11.cloned.1.call-done.refs_6_.refs_8_.refs_1_), channel_id=1, source_target_pairs={{0,1},{1,0},{2,3},{3,2},{4,5},{5,4},{6,7},{7,6},{8,9},{9,8},{10,11... | collective-permute-start | bytes 9437192 | tf_op jit(solution)/shard_map/ppermute | solution.py:30
  328.4 39.0 %collective-permute-start.42 = (bf16[128,2048]{1,0:T(8,128)(2,1)}, bf16[128,2048]{1,0:T(8,128)(2,1)S(1)}, u32[]{:S(2)}, u32[]{:S(2)}) collective-permute-start(bf16[128,2048]{1,0:T(8,128)(2,1)} %get-tuple-element.271), channel_id=1, source_target_pairs={{0,2},{2,0},{4,6},{6,4},{1,3},{3,1},{5,7},{7,5},{8,10},{10,8},{12,... | collective-permute-start | bytes 1572872 | tf_op jit(solution)/shard_map/ppermute | solution.py:18
  329.2 38.2 %collective-permute-start.43 = (bf16[128,2048]{1,0:T(8,128)(2,1)}, bf16[128,2048]{1,0:T(8,128)(2,1)S(1)}, u32[]{:S(2)}, u32[]{:S(2)}) collective-permute-start(bf16[128,2048]{1,0:T(8,128)(2,1)} %get-tuple-element.277), channel_id=1, source_target_pairs={{0,4},{2,6},{4,0},{6,2},{1,5},{3,7},{5,1},{7,3},{8,12},{10,14},{12... | collective-permute-start | bytes 1572872 | tf_op jit(solution)/shard_map/ppermute | solution.py:22
  349.1 18.4 %collective-permute-start.45 = (bf16[128,2048]{1,0:T(8,128)(2,1)}, bf16[128,2048]{1,0:T(8,128)(2,1)S(1)}, u32[]{:S(2)}, u32[]{:S(2)}) collective-permute-start(bf16[128,2048]{1,0:T(8,128)(2,1)} %get-tuple-element.278), channel_id=1, source_target_pairs={{0,4},{2,6},{4,0},{6,2},{1,5},{3,7},{5,1},{7,3},{8,12},{10,14},{12... | collective-permute-start | bytes 1572872 | tf_op jit(solution)/shard_map/ppermute | solution.py:22
  351.2 16.3 %collective-permute-start.44 = (bf16[128,2048]{1,0:T(8,128)(2,1)}, bf16[128,2048]{1,0:T(8,128)(2,1)S(1)}, u32[]{:S(2)}, u32[]{:S(2)}) collective-permute-start(bf16[128,2048]{1,0:T(8,128)(2,1)} %get-tuple-element.273), channel_id=1, source_target_pairs={{0,2},{2,0},{4,6},{6,4},{1,3},{3,1},{5,7},{7,5},{8,10},{10,8},{12,... | collective-permute-start | bytes 1572872 | tf_op jit(solution)/shard_map/ppermute | solution.py:18
  352.5 170.5 %reduce-scatter.7.cloned.1.call-start = ((), (), s32[]{:S(2)}) async-start(), calls=%async_computation.9 | async-start | bytes 7208960 | tf_op jit(solution)/shard_map/reduce_scatter | solution.py:78
  380.0 22.5 %collective-permute-start.54 = (bf16[2048,1408]{1,0:T(8,128)(2,1)}, bf16[2048,1408]{1,0:T(8,128)(2,1)S(1)}, u32[]{:S(2)}, u32[]{:S(2)}) collective-permute-start(bf16[2048,1408]{1,0:T(8,128)(2,1)} %shard_map.261), channel_id=1, source_target_pairs={{0,1},{1,0},{2,3},{3,2},{4,5},{5,4},{6,7},{7,6},{8,9},{9,8},{10,11... | collective-permute-start | bytes 17301512 | tf_op jit(solution)/shard_map/ppermute | solution.py:30
  380.1 14.3 %collective-permute-start.46 = (bf16[128,2048]{1,0:T(8,128)(2,1)S(1)}, bf16[128,2048]{1,0:T(8,128)(2,1)S(1)}, u32[]{:S(2)}, u32[]{:S(2)}) collective-permute-start(bf16[128,2048]{1,0:T(8,128)(2,1)S(1)} %add_convert_fusion.7), channel_id=1, source_target_pairs={{0,2},{2,0},{4,6},{6,4},{1,3},{3,1},{5,7},{7,5},{8,10},{10,8},{12,... | collective-permute-start | bytes 1572872 | tf_op jit(solution)/shard_map/ppermute | solution.py:18
  380.3 14.1 %collective-permute-start.47 = (bf16[128,2048]{1,0:T(8,128)(2,1)S(1)}, bf16[128,2048]{1,0:T(8,128)(2,1)S(1)}, u32[]{:S(2)}, u32[]{:S(2)}) collective-permute-start(bf16[128,2048]{1,0:T(8,128)(2,1)S(1)} %add_convert_fusion.6), channel_id=1, source_target_pairs={{0,4},{2,6},{4,0},{6,2},{1,5},{3,7},{5,1},{7,3},{8,12},{10,14},{12... | collective-permute-start | bytes 1572872 | tf_op jit(solution)/shard_map/ppermute | solution.py:22
  417.7 154.1 %reduce-scatter.11.cloned.1.call-start = ((), (), s32[]{:S(2)}) async-start(), calls=%async_computation.11 | async-start | bytes 2621440 | tf_op jit(solution)/shard_map/reduce_scatter | solution.py:78
  418.7 22.7 %collective-permute-start.50 = (bf16[128,2176]{1,0:T(8,128)(2,1)S(1)}, bf16[128,2176]{1,0:T(8,128)(2,1)S(1)}, u32[]{:S(2)}, u32[]{:S(2)}) collective-permute-start(bf16[128,2176]{1,0:T(8,128)(2,1)S(1)} %copy-done.32), channel_id=1, source_target_pairs={{0,2},{2,0},{4,6},{6,4},{1,3},{3,1},{5,7},{7,5},{8,10},{10,8},{12,... | collective-permute-start | bytes 1671176 | tf_op jit(solution)/shard_map/ppermute | solution.py:18
  420.3 21.1 %collective-permute-start.51 = (bf16[128,2176]{1,0:T(8,128)(2,1)S(1)}, bf16[128,2176]{1,0:T(8,128)(2,1)S(1)}, u32[]{:S(2)}, u32[]{:S(2)}) collective-permute-start(bf16[128,2176]{1,0:T(8,128)(2,1)S(1)} %copy-done.31), channel_id=1, source_target_pairs={{0,4},{2,6},{4,0},{6,2},{1,5},{3,7},{5,1},{7,3},{8,12},{10,14},{12... | collective-permute-start | bytes 1671176 | tf_op jit(solution)/shard_map/ppermute | solution.py:22
  420.7 24.3 %collective-permute-start.48 = (bf16[128,2176]{1,0:T(8,128)(2,1)S(1)}, bf16[128,2176]{1,0:T(8,128)(2,1)S(1)}, u32[]{:S(2)}, u32[]{:S(2)}) collective-permute-start(bf16[128,2176]{1,0:T(8,128)(2,1)S(1)} %copy-done.31), channel_id=1, source_target_pairs={{0,2},{2,0},{4,6},{6,4},{1,3},{3,1},{5,7},{7,5},{8,10},{10,8},{12,... | collective-permute-start | bytes 1671176 | tf_op jit(solution)/shard_map/ppermute | solution.py:18
  420.9 25.1 %collective-permute-start.49 = (bf16[128,2176]{1,0:T(8,128)(2,1)S(1)}, bf16[128,2176]{1,0:T(8,128)(2,1)}, u32[]{:S(2)}, u32[]{:S(2)}) collective-permute-start(bf16[128,2176]{1,0:T(8,128)(2,1)S(1)} %copy-done.32), channel_id=1, source_target_pairs={{0,4},{2,6},{4,0},{6,2},{1,5},{3,7},{5,1},{7,3},{8,12},{10,14},{12... | collective-permute-start | bytes 1671176 | tf_op jit(solution)/shard_map/ppermute | solution.py:22
  459.8 42.4 %collective-permute-start.55 = (bf16[128,2048]{1,0:T(8,128)(2,1)}, bf16[128,2048]{1,0:T(8,128)(2,1)}, u32[]{:S(2)}, u32[]{:S(2)}) collective-permute-start(bf16[128,2048]{1,0:T(8,128)(2,1)} %get-tuple-element.312.refs_4_), channel_id=1, source_target_pairs={{0,2},{2,0},{4,6},{6,4},{1,3},{3,1},{5,7},{7,5},{8,10},{10,8},{12,... | collective-permute-start | bytes 1572872 | tf_op jit(solution)/shard_map/ppermute | solution.py:18
  460.5 43.1 %collective-permute-start.56 = (bf16[128,2048]{1,0:T(8,128)(2,1)}, bf16[128,2048]{1,0:T(8,128)(2,1)}, u32[]{:S(2)}, u32[]{:S(2)}) collective-permute-start(bf16[128,2048]{1,0:T(8,128)(2,1)} %get-tuple-element.313), channel_id=1, source_target_pairs={{0,4},{2,6},{4,0},{6,2},{1,5},{3,7},{5,1},{7,3},{8,12},{10,14},{12... | collective-permute-start | bytes 1572872 | tf_op jit(solution)/shard_map/ppermute | solution.py:22
  462.1 41.5 %collective-permute-start.57 = (bf16[128,2048]{1,0:T(8,128)(2,1)}, bf16[128,2048]{1,0:T(8,128)(2,1)}, u32[]{:S(2)}, u32[]{:S(2)}) collective-permute-start(bf16[128,2048]{1,0:T(8,128)(2,1)} %get-tuple-element.314), channel_id=1, source_target_pairs={{0,2},{2,0},{4,6},{6,4},{1,3},{3,1},{5,7},{7,5},{8,10},{10,8},{12,... | collective-permute-start | bytes 1572872 | tf_op jit(solution)/shard_map/ppermute | solution.py:18
  463.1 40.6 %collective-permute-start.58 = (bf16[128,2048]{1,0:T(8,128)(2,1)}, bf16[128,2048]{1,0:T(8,128)(2,1)}, u32[]{:S(2)}, u32[]{:S(2)}) collective-permute-start(bf16[128,2048]{1,0:T(8,128)(2,1)} %get-tuple-element.315), channel_id=1, source_target_pairs={{0,4},{2,6},{4,0},{6,2},{1,5},{3,7},{5,1},{7,3},{8,12},{10,14},{12... | collective-permute-start | bytes 1572872 | tf_op jit(solution)/shard_map/ppermute | solution.py:22
  499.5 21.5 %collective-permute-start.63 = (bf16[2048,512]{1,0:T(8,128)(2,1)S(1)}, bf16[2048,512]{1,0:T(8,128)(2,1)S(1)}, u32[]{:S(2)}, u32[]{:S(2)}) collective-permute-start(bf16[2048,512]{1,0:T(8,128)(2,1)S(1)} %pad_maximum_fusion.4), channel_id=1, source_target_pairs={{0,1},{1,0},{2,3},{3,2},{4,5},{5,4},{6,7},{7,6},{8,9},{9,8},{10,11... | collective-permute-start | bytes 6291464 | tf_op jit(solution)/shard_map/ppermute | solution.py:30
  504.9 14.3 %collective-permute-start.59 = (bf16[128,2048]{1,0:T(8,128)(2,1)S(1)}, bf16[128,2048]{1,0:T(8,128)(2,1)S(1)}, u32[]{:S(2)}, u32[]{:S(2)}) collective-permute-start(bf16[128,2048]{1,0:T(8,128)(2,1)S(1)} %add_convert_fusion.5), channel_id=1, source_target_pairs={{0,2},{2,0},{4,6},{6,4},{1,3},{3,1},{5,7},{7,5},{8,10},{10,8},{12,... | collective-permute-start | bytes 1572872 | tf_op jit(solution)/shard_map/ppermute | solution.py:18
  506.9 14.1 %collective-permute-start.60 = (bf16[128,2048]{1,0:T(8,128)(2,1)S(1)}, bf16[128,2048]{1,0:T(8,128)(2,1)S(1)}, u32[]{:S(2)}, u32[]{:S(2)}) collective-permute-start(bf16[128,2048]{1,0:T(8,128)(2,1)S(1)} %add_convert_fusion.4), channel_id=1, source_target_pairs={{0,4},{2,6},{4,0},{6,2},{1,5},{3,7},{5,1},{7,3},{8,12},{10,14},{12... | collective-permute-start | bytes 1572872 | tf_op jit(solution)/shard_map/ppermute | solution.py:22
  523.0 90.0 %reduce-scatter.9.cloned.1.call-start = ((), (), s32[]{:S(2)}) async-start(), calls=%async_computation.10 | async-start | bytes 2621440 | tf_op jit(solution)/shard_map/reduce_scatter | solution.py:78
  556.6 15.4 %collective-permute-start.66 = (bf16[128,2048]{1,0:T(8,128)(2,1)}, bf16[128,2048]{1,0:T(8,128)(2,1)S(1)}, u32[]{:S(2)}, u32[]{:S(2)}) collective-permute-start(bf16[128,2048]{1,0:T(8,128)(2,1)} %get-tuple-element.344), channel_id=1, source_target_pairs={{0,2},{2,0},{4,6},{6,4},{1,3},{3,1},{5,7},{7,5},{8,10},{10,8},{12,... | collective-permute-start | bytes 1572872 | tf_op jit(solution)/shard_map/ppermute | solution.py:18
  557.9 14.1 %collective-permute-start.67 = (bf16[128,2048]{1,0:T(8,128)(2,1)}, bf16[128,2048]{1,0:T(8,128)(2,1)S(1)}, u32[]{:S(2)}, u32[]{:S(2)}) collective-permute-start(bf16[128,2048]{1,0:T(8,128)(2,1)} %get-tuple-element.347), channel_id=1, source_target_pairs={{0,4},{2,6},{4,0},{6,2},{1,5},{3,7},{5,1},{7,3},{8,12},{10,14},{12... | collective-permute-start | bytes 1572872 | tf_op jit(solution)/shard_map/ppermute | solution.py:22
  570.1 14.0 %collective-permute-start.68 = (bf16[128,2048]{1,0:T(8,128)(2,1)}, bf16[128,2048]{1,0:T(8,128)(2,1)S(1)}, u32[]{:S(2)}, u32[]{:S(2)}) collective-permute-start(bf16[128,2048]{1,0:T(8,128)(2,1)} %get-tuple-element.348), channel_id=1, source_target_pairs={{0,2},{2,0},{4,6},{6,4},{1,3},{3,1},{5,7},{7,5},{8,10},{10,8},{12,... | collective-permute-start | bytes 1572872 | tf_op jit(solution)/shard_map/ppermute | solution.py:18
  571.4 13.6 %collective-permute-start.69 = (bf16[128,2048]{1,0:T(8,128)(2,1)}, bf16[128,2048]{1,0:T(8,128)(2,1)S(1)}, u32[]{:S(2)}, u32[]{:S(2)}) collective-permute-start(bf16[128,2048]{1,0:T(8,128)(2,1)} %get-tuple-element.349), channel_id=1, source_target_pairs={{0,4},{2,6},{4,0},{6,2},{1,5},{3,7},{5,1},{7,3},{8,12},{10,14},{12... | collective-permute-start | bytes 1572872 | tf_op jit(solution)/shard_map/ppermute | solution.py:22
  586.5 14.9 %collective-permute-start.70 = (bf16[128,2048]{1,0:T(8,128)(2,1)S(1)}, bf16[128,2048]{1,0:T(8,128)(2,1)S(1)}, u32[]{:S(2)}, u32[]{:S(2)}) collective-permute-start(bf16[128,2048]{1,0:T(8,128)(2,1)S(1)} %add_convert_fusion.3), channel_id=1, source_target_pairs={{0,2},{2,0},{4,6},{6,4},{1,3},{3,1},{5,7},{7,5},{8,10},{10,8},{12,... | collective-permute-start | bytes 1572872 | tf_op jit(solution)/shard_map/ppermute | solution.py:18
  588.4 15.1 %collective-permute-start.71 = (bf16[128,2048]{1,0:T(8,128)(2,1)}, bf16[128,2048]{1,0:T(8,128)(2,1)S(1)}, u32[]{:S(2)}, u32[]{:S(2)}) collective-permute-start(bf16[128,2048]{1,0:T(8,128)(2,1)} %add_convert_fusion.2), channel_id=1, source_target_pairs={{0,4},{2,6},{4,0},{6,2},{1,5},{3,7},{5,1},{7,3},{8,12},{10,14},{12... | collective-permute-start | bytes 1572872 | tf_op jit(solution)/shard_map/ppermute | solution.py:22
  590.6 35.7 %collective-permute-start.74 = (bf16[128,2176]{1,0:T(8,128)(2,1)}, bf16[128,2176]{1,0:T(8,128)(2,1)}, u32[]{:S(2)}, u32[]{:S(2)}) collective-permute-start(bf16[128,2176]{1,0:T(8,128)(2,1)} %get-tuple-element.364), channel_id=1, source_target_pairs={{0,2},{2,0},{4,6},{6,4},{1,3},{3,1},{5,7},{7,5},{8,10},{10,8},{12,... | collective-permute-start | bytes 1671176 | tf_op jit(solution)/shard_map/ppermute | solution.py:18
  591.3 35.0 %collective-permute-start.75 = (bf16[128,2176]{1,0:T(8,128)(2,1)}, bf16[128,2176]{1,0:T(8,128)(2,1)}, u32[]{:S(2)}, u32[]{:S(2)}) collective-permute-start(bf16[128,2176]{1,0:T(8,128)(2,1)} %get-tuple-element.365), channel_id=1, source_target_pairs={{0,4},{2,6},{4,0},{6,2},{1,5},{3,7},{5,1},{7,3},{8,12},{10,14},{12... | collective-permute-start | bytes 1671176 | tf_op jit(solution)/shard_map/ppermute | solution.py:22
  593.0 33.3 %collective-permute-start.76 = (bf16[128,2176]{1,0:T(8,128)(2,1)}, bf16[128,2176]{1,0:T(8,128)(2,1)}, u32[]{:S(2)}, u32[]{:S(2)}) collective-permute-start(bf16[128,2176]{1,0:T(8,128)(2,1)} %get-tuple-element.366), channel_id=1, source_target_pairs={{0,6},{2,4},{4,2},{6,0},{1,7},{3,5},{5,3},{7,1},{8,14},{10,12},{12... | collective-permute-start | bytes 1671176 | tf_op jit(solution)/shard_map/ppermute | solution.py:26
  618.8 33.4 %collective-permute-start.80 = (f32[256,2048]{1,0:T(8,128)}, f32[256,2048]{1,0:T(8,128)S(1)}, u32[]{:S(2)}, u32[]{:S(2)}) collective-permute-start(f32[256,2048]{1,0:T(8,128)} %bitcast.196), channel_id=1, source_target_pairs={{0,1},{1,0},{2,3},{3,2},{4,5},{5,4},{6,7},{7,6},{8,9},{9,8},{10,11... | collective-permute-start | bytes 6291464 | tf_op jit(solution)/shard_map/ppermute | solution.py:30
  (115 other events, 993.4 us)
Sparse Core Ops, SparseCore 0:
  28.5 46.3 all-gather.4
  76.4 44.6 all-gather.6
  123.3 105.4 all-gather.8
  231.0 63.5 all-gather.10
  352.6 59.1 reduce-scatter.4
  417.8 102.2 reduce-scatter.6
  523.1 43.7 reduce-scatter.10
  569.8 43.1 reduce-scatter.8

commit v3 on v2

--- a/solution.py
+++ b/solution.py
@@ -112,16 +112,20 @@
 
 
 def sum_all(v, count):
-    v = v + swap_x(v)
-    v = v + swap_y(v)
+    v = (v + swap_x(v)) + (swap_y(v) + swap_xy(v))
     step = 1
     while step < count:
-        v = v + lax.ppermute(v, "seq", [(i, i ^ step) for i in range(count)])
-        step *= 2
+        got = [
+            lax.ppermute(v, "seq", [(i, i ^ (k * step)) for i in range(count)])
+            for k in (1, 2, 3)
+            if k * step < count
+        ]
+        v = v + got[0] if len(got) < 3 else (v + got[0]) + (got[1] + got[2])
+        step *= 4
     return v
 
 
-def enter(product, last, count, back):
+def enter(product, last, count, back, hops):
     def shift(pair, k):
         hops = [(i, i + k) for i in range(count - k)]
         return lax.ppermute(pair, "seq", [(b, a) for a, b in hops] if back else hops)
@@ -131,6 +135,7 @@
 
     ends = jnp.stack([product, last])
     value = shift(ends, 1)
+    hops.append(value)
     step = 2
     while step < count:
         value = link(shift(link(value, ends), step), value)
@@ -155,7 +160,7 @@
         ],
         compiler_params=pltpu.CompilerParams(vmem_limit_bytes=VMEM_BYTES),
         cost_estimate=pl.CostEstimate(
-            flops=0, bytes_accessed=int(cost * 3.5e6), transcendentals=0
+            flops=int(cost * 1.1e9), bytes_accessed=0, transcendentals=0
         ),
     )(*arrays)
 
@@ -199,7 +204,7 @@
     wait_all(stores)
 
 
-def rows_dot(xs, ws, first, wide, cost=7):
+def rows_dot(xs, ws, first, wide, cost=0, behind=()):
     n, rows, depth = len(xs) // 2, xs[0].shape[0], ws[0].shape[0]
     return call(
         functools.partial(dot_kernel, n, first, wide),
@@ -214,6 +219,7 @@
             (2 * n,),
         ],
         cost,
+        behind,
     )[0]
 
 
@@ -255,7 +261,7 @@
         [*xs, w],
         outs,
         [*outs, ((n, 2 * rows, depth), LOW), (w.shape, LOW), (2 * n + 1,), (n, 3)],
-        12,
+        0,
     )
 
 
@@ -507,6 +513,8 @@
     def spec(shape, skip=0):
         if shape[1] == 1:
             return pl.BlockSpec(shape, lambda i: (0, 0))
+        if skip == shape[1] // 128 - 1:
+            return pl.BlockSpec((shape[0], 128), lambda i: (0, skip))
         return pl.BlockSpec((shape[0], 128), lambda i: (0, i + skip))
 
     skips = [v[1] if isinstance(v, tuple) else 0 for v in arrays]
@@ -521,7 +529,7 @@
         scratch_shapes=[pltpu.VMEM(*v) for v in scratch],
         compiler_params=pltpu.CompilerParams(vmem_limit_bytes=VMEM_BYTES),
         cost_estimate=pl.CostEstimate(
-            flops=0, bytes_accessed=int(cost * 3.5e6), transcendentals=0
+            flops=int(cost * 1.1e9), bytes_accessed=0, transcendentals=0
         ),
     )(*arrays)
 
@@ -590,8 +598,9 @@
 
 
 def gate_back_kernel(
-    seg, wide, d_gated, gate, state, gain, inverse, dot, decay, gated, d_gate, gain_sum, local, product, held
+    seg, wide, d_gated, gate, state, gain, inverse, *refs
 ):
+    dots, (decay, gated, d_gate, gain_sum, local, product, held) = refs[:8], refs[8:]
     rows = gain.shape[0]
     for k in range(rows):
         at, one = pl.ds(k * seg, seg), pl.ds(k, 1)
@@ -601,7 +610,9 @@
         gated[at, :] = (normed * scale * act).astype(LOW)
         d_gate[at, :] = (up * normed * scale * sig * (1.0 + g * (1.0 - sig))).astype(LOW)
         gain_sum[one, :] = jnp.sum(up * normed * act, axis=0, keepdims=True)
-        shrink = inv * inv * inv * (dot[at, :] * (1.0 / wide))
+        dot = jnp.concatenate([dots[k // 2 * 2 + p][...].astype(FULL) for p in range(2)])
+        dot = jnp.sum(dot, axis=1, keepdims=True)
+        shrink = inv * inv * inv * (dot * (1.0 / wide))
         held[at, :] = inv * (up * scale * act) - h * shrink
     backward_scan(seg, rows, decay, held, local, product)
 
@@ -628,7 +639,7 @@
 STEP = 32
 
 
-def token_call(kernel, arrays, outs, seg, wide, cost=5):
+def token_call(kernel, arrays, outs, seg, wide, cost=0):
     half = seg // 2
 
     def spec(shape):
@@ -650,7 +661,7 @@
         out_shape=[jax.ShapeDtypeStruct(folded(shape), kind) for shape, kind in outs],
         compiler_params=pltpu.CompilerParams(vmem_limit_bytes=VMEM_BYTES),
         cost_estimate=pl.CostEstimate(
-            flops=0, bytes_accessed=int(cost * 3.5e6), transcendentals=0
+            flops=int(cost * 1.1e9), bytes_accessed=0, transcendentals=0
         ),
     )(*arrays)
     return [v.reshape(shape) for v, (shape, _) in zip(got, outs)]
@@ -886,9 +897,10 @@
         [((8 * seg, 128), FULL)],
     )
     w_gates = own_other(after(w_gates, local_state))
-    carry_in = enter(by_row(cum_decay)[:, -1], by_row(local_state)[:, -1], segments, False)
+    hops = []
+    carry_in = enter(by_row(cum_decay)[:, -1], by_row(local_state)[:, -1], segments, False, hops)
     cot_pieces = [cot_own[: seg // 2], cot_own[seg // 2 :]]
-    proj_gate = rows_dot(normed_in, w_gates, 0, chan, 0)
+    proj_gate = rows_dot(normed_in, w_gates, 0, chan, 0, (hops[0].reshape(-1, chan),))
     carry_in = after(carry_in, proj_gate)
     state, gated_raw, squares = channel_call(
         functools.partial(state_kernel, seg),
@@ -900,7 +912,7 @@
     inv_own = inv_all[0][:, None]
     gated_raw = after(gated_raw, square_total)
 
-    def two_step(parts, cost=5, behind=False):
+    def two_step(parts, cost=0, behind=False):
         diag = rows_terms(parts, (3,), seg, cost=cost)
         first = settled(*diag) if behind else diag[0]
         rest = rows_terms(parts, (1, 2, 0), seg, (first,))
@@ -926,8 +938,8 @@
     def hidden_pieces(h):
         return [(hidden[h], r * seg, seg) for r in range(4)]
 
-    (grad_other,) = rows_grad(cot_all, [[hidden_pieces(1)]], 7)
-    (grad_down,) = rows_grad(cot_all, [[hidden_pieces(0)]], 8, swap_core(grad_other))
+    (grad_other,) = rows_grad(cot_all, [[hidden_pieces(1)]], 0)
+    (grad_down,) = rows_grad(cot_all, [[hidden_pieces(0)]], 0, swap_core(grad_other))
     w_down = gather_width(after(down, normed_mlp[2]))
     w_down = own_other(after(w_down, *hidden))
     w_down[0] = after(w_down[0], grad_down)
@@ -939,7 +951,7 @@
         d_acts[picked], *terms = rows_back(cot_all, gate_act, up_act, downs, w_mlp, picked, seg, cost)
         return terms
 
-    diag = back_terms((3,), 13)
+    diag = back_terms((3,), 0)
     sides = back_terms((1, 2), 0, diag[0])
     mine = back_terms((0,), 0, sides[0])
     mlp_sums, sent = scatter_rows([*mine, *sides, *diag], tuple(mine))
@@ -951,7 +963,8 @@
 
     normed_mlp[0] = after(normed_mlp[0], *sent)
     (grad_other,) = rows_grad(normed_mlp, [[d_act_pieces(1)]], 0)
-    mlp_sums[0] = after(mlp_sums[0], grad_other)
+    (grad_mlp,) = rows_grad(normed_mlp, [[d_act_pieces(0)]], 0, swap_core(grad_other))
+    mlp_sums[0] = after(mlp_sums[0], grad_mlp)
 
     d_resid, *d_low, gain_two_sum = token_call(
         d_mlp_kernel,
@@ -959,19 +972,16 @@
         [(whole, FULL), (wider, LOW), (wider, LOW), ((1, width), FULL)],
         seg,
         width,
+        14,
     )
     hidden = [after(hidden[0], *d_low), hidden[1]]
     out_terms = two_step([(hidden[h], (1, 0), w_down[h], 0) for h in range(2)], 0)
     d_resid_all = gather_rows(d_low)
-    normed_mlp[0] = after(normed_mlp[0], *d_low)
-    (grad_mlp,) = rows_grad(normed_mlp, [[d_act_pieces(0)]], 0, swap_core(grad_other))
     d_resid_all[6] = after(d_resid_all[6], grad_mlp, *out_terms)
     grad_mlp = scatter_width(grad_mlp)
     out_terms = list(lax.optimization_barrier((*out_terms, d_resid_all[6]))[:-1])
     out_sums, sent = scatter_rows(out_terms)
-    dot_total = jnp.stack([v[:, width : width + 128] for v in d_resid_all]).astype(FULL)
-    dot_total = jnp.sum(dot_total, axis=-1).reshape(4, seg)
-    d_gated = rows_dot(d_resid_all, w_gates, chan, chan)
+    d_gated = rows_dot(d_resid_all, w_gates, chan, chan, 21)
     gated, d_proj_gate, gain_three_grad, back_local, back_prod = channel_call(
         functools.partial(gate_back_kernel, seg, width),
         [
@@ -980,11 +990,12 @@
             state,
             gain_three,
             columns(inv_all),
-            columns(dot_total),
+            *[(v, width // 128) for v in d_resid_all],
             after(decay, grad_down),
         ],
         [((8 * seg, chan), LOW)] * 2 + [((8, chan), FULL)] + [channel] * 2,
         [((8 * seg, 128), FULL)],
+        34,
     )
     both = [
         rows_grad(xs, [[block_pieces(v, h, seg)] for h in range(2)], 0, None, width)
@@ -997,6 +1008,7 @@
         first_decay * by_row(back_local)[:, 0],
         segments,
         True,
+        [],
     )
 
     def chip_sum(own, other):
@@ -1020,6 +1032,8 @@
             keep_mask,
         ],
         [((8 * seg, chan), LOW), ((8 * seg, chan), LOW), ((8, chan), FULL)],
+        (),
+        0,
     )
     grad_scan = rows_grad(
         normed_in, [[block_pieces(v, h, seg) for v in d_scan] for h in range(2)], 0
@@ -1029,8 +1043,7 @@
     grad_scan = scatter_width(grad_scan)
     in_parts = [(d_scan[k], (2, h), w_scan[h], k * chan) for h in range(2) for k in range(2)]
     in_parts += [(d_proj_gate, (2, h), w_gates[h], 0) for h in range(2)]
-    in_sums, sent = scatter_rows(two_step(in_parts, 5, True), (grad_gates,))
-    in_sums[0] = after(in_sums[0], grad_scan)
+    in_sums, sent = scatter_rows(two_step(in_parts, 20, True), (grad_gates,))
     behind = settled(*sent)
     mlp = exchange(list(lax.optimization_barrier((*mlp_places, behind))[:4]))
     grad_own, gain_one_sum = token_call(
@@ -1064,7 +1077,7 @@
     small = jnp.concatenate([gains_keep, channels[0]]) + swap_core(
         jnp.concatenate([gains_send, channels[1]])
     )
-    small = sum_all(after(small, *mlp), segments)
+    small = sum_all(after(small, *mlp, *mixer), segments)
     soft = jax.nn.softmax(bound_param, axis=0)
     grad_table = small[3] * soft * (used - jnp.sum(soft * used, axis=0))
     *grads, grad_tokens = final(

time: 677 us -> 674 us (level)
    reduce_scatter x4, waiting for transfers between devices: 9.55 us -> 0.04 us  [scatter_width(): return lax.psum_scatter(grad, 'seq', scatter_dimension=0, tiled=True)]
    ppermute x4 -> x5, waiting for transfers between devices: 14.6 us -> 12.4 us  [swap_xy(): return lax.ppermute(v, 'batch', [(i, i ^ 3) for i in range(4)])]
    unnamed x189 -> x196, local copies, waits for them, and re-layouts: 19.8 us -> 18.7 us
  transfers between devices with their start and end apart: 94 -> 96, of which waited for: 54 -> 52; matrix products, arithmetic and copies ran while one was open for 9% -> 9% of each run, Pallas kernels for 36% -> 37%
where the time goes in v3:
time: 674 us; the launch traced here: 665 us
  Pallas kernels  263 us (39%)
  waiting for transfers between devices  213 us (32%)
  starting transfers between devices  94.5 us (14%)
  local copies, waits for them, and re-layouts  51.3 us (8%)
  other arithmetic  26 us (4%)
  between operations  16.9 us (3%)
    pallas_call x21, Pallas kernels, call(): pl.pallas_call(body, in_specs=[ANYWHERE] * len(arrays), out_specs=[ANYWHE...  194 us
    ppermute x31, waiting for transfers between devices, swap_x(): return lax.ppermute(v, 'batch', [(i, i ^ 1) for i in range(4)])  106 us
    ppermute x31, waiting for transfers between devices, swap_y(): return lax.ppermute(v, 'batch', [(i, i ^ 2) for i in range(4)])  54.3 us
    pallas_call x4, Pallas kernels, channel_call(): pl.pallas_call(kernel, grid=(2,), in_specs=[spec(v.shape, skip) for v, sk...  35.9 us
    ppermute x31, starting transfers between devices, swap_y(): return lax.ppermute(v, 'batch', [(i, i ^ 2) for i in range(4)])  33.1 us
    ppermute x31, starting transfers between devices, swap_x(): return lax.ppermute(v, 'batch', [(i, i ^ 1) for i in range(4)])  31.4 us
    pallas_call x5, Pallas kernels, token_call(): pl.pallas_call(kernel, grid=(half // STEP,), in_specs=[spec(v.shape) for...  26.2 us
    unnamed x196, local copies, waits for them, and re-layouts  18.7 us
  transfers between devices with their start and end apart: 96, of which 52 were waited for; matrix products, arithmetic and copies ran while one was open for 9% of the time, Pallas kernels for 37%

profile of v3, /device:TPU:0, one launch (start us, length us, event | category | flops | bytes accessed | tf_op | source)
XLA Modules:
  0.0 664.9 jit_solution(1339859083510469762)
XLA Ops:
  10.8 4.0 collective-permute-start.2
  15.4 6.5 collective-permute-done.2
  21.9 4.7 collective-permute-done.1
  42.6 3.6 shard_map.246
  48.3 4.8 collective-permute-done.10
  53.1 8.7 %collective-permute-done.9 = bf16[128,2112]{0,1:T(8,128)(2,1)S(1)} collective-permute-done((bf16[128,2112]{0,1:T(8,128)(2,1)S(1)}, bf16[128,2112]{0,1:T(8,128)(2,1)S(1)}, u32[]{:S(2)}, u32[]{:S(2)}) %collective-permute-start.9) | collective-permute-done | bytes 540704 | tf_op jit(solution)/shard_map/ppermute | solution.py:22
  61.8 2.9 collective-permute-done.8
  77.2 6.6 collective-permute-done.11.refs_3_
  86.2 11.8 %collective-permute-done.13.refs_6_ = bf16[128,2048]{1,0:T(8,128)(2,1)S(1)} collective-permute-done((bf16[128,2048]{1,0:T(8,128)(2,1)S(1)}, bf16[128,2048]{1,0:T(8,128)(2,1)S(1)}, u32[]{:S(2)}, u32[]{:S(2)}) %collective-permute-start.13) | collective-permute-done | bytes 524320 | tf_op jit(solution)/shard_map/ppermute | solution.py:22
  103.4 8.8 %shard_map.247.proj_in.proj_forget = f32[2048,512]{1,0:T(8,128)} custom-call(bf16[128,2048]{1,0:T(8,128)(2,1)} %get-tuple-element.210.refs_0_, bf16[128,2048]{1,0:T(8,128)(2,1)} %get-tuple-element.209.refs_1_, bf16[128,2048]{1,0:T(8,128)(2,1)} %copy-done.6, bf16[128,2048]{1,0:T(8,128)(2,1)} %copy-done.8, bf16[128,2048]{1,0:T(8,128)(2,1)} %copy-done.9, ...), custom_call_target="tpu_custom_call" | custom-call | tf_op jit(solution)/shard_map/pallas_call | solution.py:153
  112.2 10.2 %shard_map.248 = (f32[2048,256]{1,0:T(8,128)}, f32[2048,256]{1,0:T(8,128)}, f32[2048,256]{1,0:T(8,128)}) custom-call(f32[2048,512]{1,0:T(8,128)} %shard_map.247.proj_in.proj_forget, f32[2048,512]{1,0:T(8,128)} %shard_map.247.proj_in.proj_forget, f32[8,256]{1,0:T(8,128)} %tile.20.bound, f32[2048,1]{1,0:T(8,128)} %reshape_reshape.8.keep), custom_call_target="tpu_custom_call" | custom-call | tf_op jit(solution)/shard_map/pallas_call | solution.py:523
  124.5 3.5 collective-permute-start.16
  129.4 5.4 collective-permute-start.17
  138.1 6.7 %shard_map.249.gate = f32[2048,256]{1,0:T(8,128)} custom-call(bf16[128,2048]{1,0:T(8,128)(2,1)} %get-tuple-element.210.refs_0_, bf16[128,2048]{1,0:T(8,128)(2,1)} %get-tuple-element.209.refs_1_, bf16[128,2048]{1,0:T(8,128)(2,1)} %copy-done.6, bf16[128,2048]{1,0:T(8,128)(2,1)} %copy-done.8, bf16[128,2048]{1,0:T(8,128)(2,1)} %copy-done.9, ...), custom_call_target="tpu_custom_call" | custom-call | tf_op jit(solution)/shard_map/pallas_call | solution.py:153
  144.8 4.7 shard_map.250
  152.2 2.7 collective-permute-done.19
  155.9 2.7 collective-permute-done.20
  158.6 3.4 shard_map.251
  164.0 5.6 shard_map.252
  171.8 4.3 collective-permute-done.22
  177.8 6.6 collective-permute-done.23.refs_1_
  189.9 6.2 collective-permute-done.25.refs_2_
  197.9 5.8 shard_map.253
  207.8 10.6 %collective-permute-done.29.refs_3_ = bf16[128,2048]{1,0:T(8,128)(2,1)S(1)} collective-permute-done((bf16[128,2048]{1,0:T(8,128)(2,1)}, bf16[128,2048]{1,0:T(8,128)(2,1)S(1)}, u32[]{:S(2)}, u32[]{:S(2)}) %collective-permute-start.29) | collective-permute-done | bytes 524320 | tf_op jit(solution)/shard_map/ppermute | solution.py:18
  219.1 4.9 collective-permute-done.27.refs_2_
  224.7 4.1 all-gather.9.cloned.1.call-done.refs_8_.refs_10_
  235.5 10.0 %collective-permute-done.32.refs_7_ = bf16[128,2048]{1,0:T(8,128)(2,1)S(1)} collective-permute-done((bf16[128,2048]{1,0:T(8,128)(2,1)S(1)}, bf16[128,2048]{1,0:T(8,128)(2,1)S(1)}, u32[]{:S(2)}, u32[]{:S(2)}) %collective-permute-start.32) | collective-permute-done | bytes 524320 | tf_op jit(solution)/shard_map/ppermute | solution.py:18
  250.8 11.9 %shard_map.255 = (f32[1024,704]{1,0:T(8,128)}, f32[1024,704]{1,0:T(8,128)}, bf16[1024,768]{1,0:T(8,128)(2,1)}) custom-call(bf16[128,2048]{1,0:T(8,128)(2,1)} %get-tuple-element.280.refs_0_, bf16[128,2048]{1,0:T(8,128)(2,1)} %get-tuple-element.240.refs_1_, bf16[128,2048]{1,0:T(8,128)(2,1)} %copy-done.14, bf16[128,2048]{1,0:T(8,128)(2,1)} %copy-done.12, ...), custom_call_target="tpu_custom_call" | custom-call | tf_op jit(solution)/shard_map/pallas_call | solution.py:153
  262.7 8.5 %collective-permute-done.34.refs_2_.refs_0_ = bf16[128,2048]{1,0:T(8,128)(2,1)S(1)} collective-permute-done((bf16[128,2048]{1,0:T(8,128)(2,1)S(1)}, bf16[128,2048]{1,0:T(8,128)(2,1)S(1)}, u32[]{:S(2)}, u32[]{:S(2)}) %collective-permute-start.34) | collective-permute-done | bytes 524320 | tf_op jit(solution)/shard_map/ppermute | solution.py:18
  274.5 12.2 %shard_map.254 = (f32[1024,704]{1,0:T(8,128)}, f32[1024,704]{1,0:T(8,128)}, bf16[1024,768]{1,0:T(8,128)(2,1)}) custom-call(bf16[128,2048]{1,0:T(8,128)(2,1)} %get-tuple-element.280.refs_0_, bf16[128,2048]{1,0:T(8,128)(2,1)} %get-tuple-element.240.refs_1_, bf16[128,2048]{1,0:T(8,128)(2,1)} %copy-done.14, bf16[128,2048]{1,0:T(8,128)(2,1)} %copy-done.12, ...), custom_call_target="tpu_custom_call" | custom-call | tf_op jit(solution)/shard_map/pallas_call | solution.py:153
  288.4 7.0 %shard_map.256 = bf16[2048,768]{1,0:T(8,128)(2,1)} custom-call(bf16[128,2048]{1,0:T(8,128)(2,1)} %copy-done.5, bf16[128,2048]{1,0:T(8,128)(2,1)} %copy-done.4, bf16[128,2048]{1,0:T(8,128)(2,1)} %copy-done.25, bf16[128,2048]{1,0:T(8,128)(2,1)} %copy-done.23, bf16[128,2048]{1,0:T(8,128)(2,1)} %copy-done.24, bf16[128,2048]{1,0:T(8,128)(2,1)} %copy-done.26, ...), custom_call_target="tpu_custom_call" | custom-call | tf_op jit(solution)/shard_map/pallas_call | solution.py:153
  297.4 4.1 collective-permute-done.40.refs_9_
  301.5 8.1 %shard_map.257 = bf16[2048,768]{1,0:T(8,128)(2,1)} custom-call(bf16[128,2048]{1,0:T(8,128)(2,1)} %copy-done.5, bf16[128,2048]{1,0:T(8,128)(2,1)} %copy-done.4, bf16[128,2048]{1,0:T(8,128)(2,1)} %copy-done.25, bf16[128,2048]{1,0:T(8,128)(2,1)} %copy-done.23, bf16[128,2048]{1,0:T(8,128)(2,1)} %copy-done.24, bf16[128,2048]{1,0:T(8,128)(2,1)} %copy-done.26, ...), custom_call_target="tpu_custom_call" | custom-call | tf_op jit(solution)/shard_map/pallas_call | solution.py:153
  311.2 14.0 %shard_map.258 = (bf16[512,1408]{1,0:T(8,128)(2,1)}, bf16[128,2048]{1,0:T(8,128)(2,1)}, bf16[128,2048]{1,0:T(8,128)(2,1)}) custom-call(bf16[128,2048]{1,0:T(8,128)(2,1)} %copy-done.27, bf16[128,2048]{1,0:T(8,128)(2,1)} %copy-done.28, f32[1024,704]{1,0:T(8,128)} %get-tuple-element.253.refs_2_.refs_4_, f32[1024,704]{1,0:T(8,128)} %get-tuple-element.254.refs_3_.refs_5_, ...), custom_call_target="tpu_custom_call" | custom-call | tf_op jit(solution)/shard_map/pallas_call | solution.py:153
  326.5 19.9 %shard_map.259 = (bf16[1024,1408]{1,0:T(8,128)(2,1)}, bf16[128,2048]{1,0:T(8,128)(2,1)}, f32[128,2048]{1,0:T(8,128)}, f32[128,2048]{1,0:T(8,128)}, bf16[128,2048]{1,0:T(8,128)(2,1)}) custom-call(bf16[128,2048]{1,0:T(8,128)(2,1)} %copy-done.25, bf16[128,2048]{1,0:T(8,128)(2,1)} %copy-done.23, bf16[128,2048]{1,0:T(8,128)(2,1)} %copy-done.24, ...), custom_call_target="tpu_custom_call" | custom-call | tf_op jit(solution)/shard_map/pallas_call | solution.py:153
  349.8 14.0 %shard_map.260 = (bf16[512,1408]{1,0:T(8,128)(2,1)}, f32[256,2048]{1,0:T(8,128)}) custom-call(bf16[128,2048]{1,0:T(8,128)(2,1)} %copy-done.5, bf16[128,2048]{1,0:T(8,128)(2,1)} %copy-done.4, f32[1024,704]{1,0:T(8,128)} %get-tuple-element.253.refs_2_.refs_4_, f32[1024,704]{1,0:T(8,128)} %get-tuple-element.254.refs_3_.refs_5_, ...), custom_call_target="tpu_custom_call" | custom-call | tf_op jit(solution)/shard_map/pallas_call | solution.py:153
  365.5 10.9 %shard_map.261 = bf16[2048,1408]{1,0:T(8,128)(2,1)} custom-call(bf16[128,2048]{1,0:T(8,128)(2,1)} %get-tuple-element.280.refs_0_, bf16[128,2048]{1,0:T(8,128)(2,1)} %get-tuple-element.240.refs_1_, bf16[128,2048]{1,0:T(8,128)(2,1)} %copy-done.14, bf16[128,2048]{1,0:T(8,128)(2,1)} %copy-done.12, bf16[128,2048]{1,0:T(8,128)(2,1)} %copy-done.13, ...), custom_call_target="tpu_custom_call" | custom-call | tf_op jit(solution)/shard_map/pallas_call | solution.py:153
  377.8 8.3 %collective-permute-done.46.refs_11_ = bf16[2048,1408]{1,0:T(8,128)(2,1)S(1)} collective-permute-done((bf16[2048,1408]{1,0:T(8,128)(2,1)}, bf16[2048,1408]{1,0:T(8,128)(2,1)S(1)}, u32[]{:S(2)}, u32[]{:S(2)}) %collective-permute-start.46) | collective-permute-done | bytes 5767200 | tf_op jit(solution)/shard_map/ppermute | solution.py:30
  386.1 2.6 copy-done.18
  388.7 12.8 %shard_map.262 = bf16[2048,1408]{1,0:T(8,128)(2,1)} custom-call(bf16[128,2048]{1,0:T(8,128)(2,1)} %get-tuple-element.280.refs_0_, bf16[128,2048]{1,0:T(8,128)(2,1)} %get-tuple-element.240.refs_1_, bf16[128,2048]{1,0:T(8,128)(2,1)} %copy-done.14, bf16[128,2048]{1,0:T(8,128)(2,1)} %copy-done.12, bf16[128,2048]{1,0:T(8,128)(2,1)} %copy-done.13, ...), custom_call_target="tpu_custom_call" | custom-call | tf_op jit(solution)/shard_map/pallas_call | solution.py:153
  402.6 6.7 %shard_map.263 = (f32[2,128,2048]{2,1,0:T(8,128)}, bf16[128,2176]{1,0:T(8,128)(2,1)}, bf16[128,2176]{1,0:T(8,128)(2,1)}, f32[1,2048]{1,0:T(1,128)}) custom-call(f32[2,128,2048]{2,1,0:T(8,128)} %bitcast.215, bf16[128,2048]{1,0:T(8,128)(2,1)} %copy-done.88, bf16[128,2048]{1,0:T(8,128)(2,1)} %copy-done.90, bf16[128,2048]{1,0:T(8,128)(2,1)} %copy-done.91, ...), custom_call_target="tpu_custom_call" | custom-call | flops 15399999488 | tf_op jit(solution)/shard_map/pallas_call | solution.py:656
  413.4 11.6 %collective-permute-done.51.refs_3_ = bf16[128,2176]{1,0:T(8,128)(2,1)S(1)} collective-permute-done((bf16[128,2176]{1,0:T(8,128)(2,1)}, bf16[128,2176]{1,0:T(8,128)(2,1)S(1)}, u32[]{:S(2)}, u32[]{:S(2)}) %collective-permute-start.51) | collective-permute-done | bytes 557088 | tf_op jit(solution)/shard_map/ppermute | solution.py:18
  425.8 10.4 %collective-permute-done.49.refs_2_ = bf16[128,2176]{1,0:T(8,128)(2,1)S(1)} collective-permute-done((bf16[128,2176]{1,0:T(8,128)(2,1)}, bf16[128,2176]{1,0:T(8,128)(2,1)S(1)}, u32[]{:S(2)}, u32[]{:S(2)}) %collective-permute-start.49) | collective-permute-done | bytes 557088 | tf_op jit(solution)/shard_map/ppermute | solution.py:18
  440.5 5.9 shard_map.264
  446.4 11.0 %shard_map.265 = (bf16[128,2048]{1,0:T(8,128)(2,1)}, f32[128,2048]{1,0:T(8,128)}, f32[128,2048]{1,0:T(8,128)}, bf16[128,2048]{1,0:T(8,128)(2,1)}, f32[256,2048]{1,0:T(8,128)}) custom-call(bf16[1024,768]{1,0:T(8,128)(2,1)} %get-tuple-element.294.refs_8_.refs_0_, bf16[2048,768]{1,0:T(8,128)(2,1)} %all-gather.11.cloned.1.call-done.refs_6_.refs_8_.refs_1_, ...), custom_call_target="tpu_custom_call" | custom-call | tf_op jit(solution)/shard_map/pallas_call | solution.py:153
  461.6 6.8 %shard_map.266.d_gated = f32[2048,256]{1,0:T(8,128)} custom-call(bf16[128,2176]{1,0:T(8,128)(2,1)} %get-tuple-element.303.refs_0_, bf16[128,2176]{1,0:T(8,128)(2,1)} %get-tuple-element.302.refs_1_, bf16[128,2176]{1,0:T(8,128)(2,1)} %copy-done.49, bf16[128,2176]{1,0:T(8,128)(2,1)} %copy-done.47, bf16[128,2176]{1,0:T(8,128)(2,1)} %copy-done.48, ...), custom_call_target="tpu_custom_call" | custom-call | flops 23100000256 | tf_op jit(solution)/shard_map/pallas_call | solution.py:153
  468.4 13.8 %shard_map.267 = (bf16[2048,256]{1,0:T(8,128)(2,1)}, bf16[2048,256]{1,0:T(8,128)(2,1)}, f32[8,256]{1,0:T(8,128)}, f32[2048,256]{1,0:T(8,128)}, f32[2048,256]{1,0:T(8,128)}) custom-call(f32[2048,256]{1,0:T(8,128)} %shard_map.266.d_gated, f32[2048,256]{1,0:T(8,128)} %shard_map.249.gate, f32[2048,256]{1,0:T(8,128)} %get-tuple-element.324.state, ...), custom_call_target="tpu_custom_call" | custom-call | flops 37399998464 | tf_op jit(solution)/shard_map/pallas_call | solution.py:523
  482.2 5.8 shard_map.269
  488.0 5.9 shard_map.268
  505.7 12.0 %collective-permute-done.62 = f32[2,8,256]{2,1,0:T(8,128)S(1)} collective-permute-done((f32[2,8,256]{2,1,0:T(8,128)S(1)}, f32[2,8,256]{2,1,0:T(8,128)S(1)}, u32[]{:S(2)}, u32[]{:S(2)}) %collective-permute-start.62) | collective-permute-done | bytes 16416 | tf_op jit(solution)/shard_map/ppermute | solution.py:131
  524.0 7.2 %shard_map.270 = (bf16[2048,256]{1,0:T(8,128)(2,1)}, bf16[2048,256]{1,0:T(8,128)(2,1)}, f32[8,256]{1,0:T(8,128)}) custom-call(f32[2048,256]{1,0:T(8,128)} %get-tuple-element.327.local, f32[2048,256]{1,0:T(8,128)} %get-tuple-element.328.product, f32[8,256]{1,0:T(8,128)} %fusion.21.returned, f32[2048,256]{1,0:T(8,128)} %get-tuple-element.324.state, ...), custom_call_target="tpu_custom_call" | custom-call | tf_op jit(solution)/shard_map/pallas_call | solution.py:523
  531.3 8.5 %shard_map.271 = (bf16[2048,512]{1,0:T(8,128)(2,1)}, bf16[2048,512]{1,0:T(8,128)(2,1)}) custom-call(bf16[128,2048]{1,0:T(8,128)(2,1)} %get-tuple-element.210.refs_0_, bf16[128,2048]{1,0:T(8,128)(2,1)} %get-tuple-element.209.refs_1_, bf16[128,2048]{1,0:T(8,128)(2,1)} %copy-done.6, bf16[128,2048]{1,0:T(8,128)(2,1)} %copy-done.8, bf16[128,2048]{1,0:T(8,128)(2,1)} %copy-done.9, ...), custom_call_target="tpu_custom_call" | custom-call | tf_op jit(solution)/shard_map/pallas_call | solution.py:153
  539.9 4.3 collective-permute-done.64
  544.2 3.6 add_convert_fusion
  547.8 4.8 shard_map.272
  556.5 10.4 %shard_map.273 = (bf16[128,2048]{1,0:T(8,128)(2,1)}, f32[128,2048]{1,0:T(8,128)}, f32[128,2048]{1,0:T(8,128)}, bf16[128,2048]{1,0:T(8,128)(2,1)}, f32[256,2048]{1,0:T(8,128)}) custom-call(bf16[2048,256]{1,0:T(8,128)(2,1)} %get-tuple-element.340.refs_8_.refs_0_, bf16[2048,512]{1,0:T(8,128)(2,1)} %all-gather.5.cloned.1.call-done.refs_8_.refs_1_, ...), custom_call_target="tpu_custom_call" | custom-call | tf_op jit(solution)/shard_map/pallas_call | solution.py:153
  568.9 12.0 %collective-permute-done.68.refs_1_ = bf16[128,2048]{1,0:T(8,128)(2,1)S(1)} collective-permute-done((bf16[128,2048]{1,0:T(8,128)(2,1)}, bf16[128,2048]{1,0:T(8,128)(2,1)S(1)}, u32[]{:S(2)}, u32[]{:S(2)}) %collective-permute-start.68) | collective-permute-done | bytes 524320 | tf_op jit(solution)/shard_map/ppermute | solution.py:18
  590.9 7.0 %collective-permute-done.70.refs_2_ = bf16[128,2048]{1,0:T(8,128)(2,1)S(1)} collective-permute-done((bf16[128,2048]{1,0:T(8,128)(2,1)S(1)}, bf16[128,2048]{1,0:T(8,128)(2,1)S(1)}, u32[]{:S(2)}, u32[]{:S(2)}) %collective-permute-start.70) | collective-permute-done | bytes 524320 | tf_op jit(solution)/shard_map/ppermute | solution.py:18
  601.1 5.7 shard_map.274
  608.3 4.4 shard_map.275
  620.0 7.9 %collective-permute-done.75.refs_2_ = bf16[128,2176]{1,0:T(8,128)(2,1)} collective-permute-done((bf16[128,2176]{1,0:T(8,128)(2,1)}, bf16[128,2176]{1,0:T(8,128)(2,1)}, u32[]{:S(2)}, u32[]{:S(2)}) %collective-permute-start.75) | collective-permute-done | bytes 557088 | tf_op jit(solution)/shard_map/ppermute | solution.py:22
  629.4 3.6 collective-permute-done.78.refs_6_
  640.6 6.3 collective-permute-start.87
  650.0 6.4 shard_map.276
  (485 shorter events, 172.0 us)
Async XLA Ops:
  7.2 91.6 %all-gather.5.cloned.1.call-start = ((), (), s32[]{:S(2)}) async-start(), calls=%async_computation.4 | async-start | bytes 2621440 | tf_op jit(solution)/shard_map/all_gather | solution.py:70
  28.4 94.0 %all-gather.7.cloned.1.call-start = ((), (), s32[]{:S(2)}) async-start(), calls=%async_computation.5 | async-start | bytes 2621440 | tf_op jit(solution)/shard_map/all_gather | solution.py:70
  36.2 192.6 %all-gather.9.cloned.1.call-start = ((), (), s32[]{:S(2)}) async-start(), calls=%async_computation.6 | async-start | bytes 7208960 | tf_op jit(solution)/shard_map/all_gather | solution.py:70
  36.9 16.2 %collective-permute-start.10 = (bf16[128,2112]{0,1:T(8,128)(2,1)S(1)}, bf16[128,2112]{0,1:T(8,128)(2,1)S(1)}, u32[]{:S(2)}, u32[]{:S(2)}) collective-permute-start(bf16[128,2112]{0,1:T(8,128)(2,1)S(1)} %get-tuple-element.390), channel_id=1, source_target_pairs={{0,6},{2,4},{4,2},{6,0},{1,7},{3,5},{5,3},{7,1},{8,14},{10,12},{12... | collective-permute-start | bytes 1622024 | tf_op jit(solution)/shard_map/ppermute | solution.py:26
  38.5 23.3 %collective-permute-start.9 = (bf16[128,2112]{0,1:T(8,128)(2,1)S(1)}, bf16[128,2112]{0,1:T(8,128)(2,1)S(1)}, u32[]{:S(2)}, u32[]{:S(2)}) collective-permute-start(bf16[128,2112]{0,1:T(8,128)(2,1)S(1)} %get-tuple-element.391), channel_id=1, source_target_pairs={{0,4},{2,6},{4,0},{6,2},{1,5},{3,7},{5,1},{7,3},{8,12},{10,14},{12... | collective-permute-start | bytes 1622024 | tf_op jit(solution)/shard_map/ppermute | solution.py:22
  39.9 24.7 %collective-permute-start.8 = (bf16[128,2112]{0,1:T(8,128)(2,1)S(1)}, bf16[128,2112]{0,1:T(8,128)(2,1)S(1)}, u32[]{:S(2)}, u32[]{:S(2)}) collective-permute-start(bf16[128,2112]{0,1:T(8,128)(2,1)S(1)} %get-tuple-element.392), channel_id=1, source_target_pairs={{0,2},{2,0},{4,6},{6,4},{1,3},{3,1},{5,7},{7,5},{8,10},{10,8},{12,... | collective-permute-start | bytes 1622024 | tf_op jit(solution)/shard_map/ppermute | solution.py:18
  46.2 31.0 %collective-permute-start.3 = (bf16[128,2048]{1,0:T(8,128)(2,1)}, bf16[128,2048]{1,0:T(8,128)(2,1)S(1)}, u32[]{:S(2)}, u32[]{:S(2)}) collective-permute-start(bf16[128,2048]{1,0:T(8,128)(2,1)} %get-tuple-element.210.refs_0_), channel_id=1, source_target_pairs={{0,2},{2,0},{4,6},{6,4},{1,3},{3,1},{5,7},{7,5},{8,10},{10,8},{12,... | collective-permute-start | bytes 1572872 | tf_op jit(solution)/shard_map/ppermute | solution.py:18
  47.7 29.6 %collective-permute-start.4 = (bf16[128,2048]{1,0:T(8,128)(2,1)}, bf16[128,2048]{1,0:T(8,128)(2,1)S(1)}, u32[]{:S(2)}, u32[]{:S(2)}) collective-permute-start(bf16[128,2048]{1,0:T(8,128)(2,1)} %get-tuple-element.209.refs_1_), channel_id=1, source_target_pairs={{0,4},{2,6},{4,0},{6,2},{1,5},{3,7},{5,1},{7,3},{8,12},{10,14},{12... | collective-permute-start | bytes 1572872 | tf_op jit(solution)/shard_map/ppermute | solution.py:22
  64.6 19.2 %collective-permute-start.11 = (bf16[128,2048]{1,0:T(8,128)(2,1)}, bf16[128,2048]{1,0:T(8,128)(2,1)S(1)}, u32[]{:S(2)}, u32[]{:S(2)}) collective-permute-start(bf16[128,2048]{1,0:T(8,128)(2,1)} %get-tuple-element.209.refs_1_), channel_id=1, source_target_pairs={{0,2},{2,0},{4,6},{6,4},{1,3},{3,1},{5,7},{7,5},{8,10},{10,8},{12,... | collective-permute-start | bytes 1572872 | tf_op jit(solution)/shard_map/ppermute | solution.py:18
  65.3 18.9 %collective-permute-start.12 = (bf16[128,2048]{1,0:T(8,128)(2,1)}, bf16[128,2048]{1,0:T(8,128)(2,1)S(1)}, u32[]{:S(2)}, u32[]{:S(2)}) collective-permute-start(bf16[128,2048]{1,0:T(8,128)(2,1)} %get-tuple-element.210.refs_0_), channel_id=1, source_target_pairs={{0,4},{2,6},{4,0},{6,2},{1,5},{3,7},{5,1},{7,3},{8,12},{10,14},{12... | collective-permute-start | bytes 1572872 | tf_op jit(solution)/shard_map/ppermute | solution.py:22
  77.2 220.2 %all-gather.11.cloned.1.call-start = ((), (), s32[]{:S(2)}) async-start(), calls=%async_computation.7 | async-start | bytes 3932160 | tf_op jit(solution)/shard_map/all_gather | solution.py:70
  84.1 13.8 %collective-permute-start.13 = (bf16[128,2048]{1,0:T(8,128)(2,1)S(1)}, bf16[128,2048]{1,0:T(8,128)(2,1)S(1)}, u32[]{:S(2)}, u32[]{:S(2)}) collective-permute-start(bf16[128,2048]{1,0:T(8,128)(2,1)S(1)} %collective-permute-done.3.refs_2_), channel_id=1, source_target_pairs={{0,4},{2,6},{4,0},{6,2},{1,5},{3,7},{5,1},{7,3},{8,12},{10,14},{12... | collective-permute-start | bytes 1572872 | tf_op jit(solution)/shard_map/ppermute | solution.py:22
  122.4 14.4 %collective-permute-start.18 = (bf16[2048,512]{1,0:T(8,128)(2,1)}, bf16[2048,512]{1,0:T(8,128)(2,1)S(1)}, u32[]{:S(2)}, u32[]{:S(2)}) collective-permute-start(bf16[2048,512]{1,0:T(8,128)(2,1)} %all-gather.7.cloned.1.call-done.refs_8_.refs_1_.refs_5_), channel_id=1, source_target_pairs={{0,1},{1,0},{2,3},{3,2},{4,5},{5,4},{6,7},{7,6},{8,9},{9,8},{10,11... | collective-permute-start | bytes 6291464 | tf_op jit(solution)/shard_map/ppermute | solution.py:30
  161.9 14.1 %collective-permute-start.22 = (bf16[128,2048]{1,0:T(8,128)(2,1)}, bf16[128,2048]{1,0:T(8,128)(2,1)S(1)}, u32[]{:S(2)}, u32[]{:S(2)}) collective-permute-start(bf16[128,2048]{1,0:T(8,128)(2,1)} %get-tuple-element.227), channel_id=1, source_target_pairs={{0,4},{2,6},{4,0},{6,2},{1,5},{3,7},{5,1},{7,3},{8,12},{10,14},{12... | collective-permute-start | bytes 1572872 | tf_op jit(solution)/shard_map/ppermute | solution.py:22
  162.9 14.9 %collective-permute-start.21 = (bf16[128,2048]{1,0:T(8,128)(2,1)}, bf16[128,2048]{1,0:T(8,128)(2,1)S(1)}, u32[]{:S(2)}, u32[]{:S(2)}) collective-permute-start(bf16[128,2048]{1,0:T(8,128)(2,1)} %get-tuple-element.225.refs_3_), channel_id=1, source_target_pairs={{0,2},{2,0},{4,6},{6,4},{1,3},{3,1},{5,7},{7,5},{8,10},{10,8},{12,... | collective-permute-start | bytes 1572872 | tf_op jit(solution)/shard_map/ppermute | solution.py:18
  169.7 14.8 %collective-permute-start.23 = (bf16[128,2048]{1,0:T(8,128)(2,1)}, bf16[128,2048]{1,0:T(8,128)(2,1)S(1)}, u32[]{:S(2)}, u32[]{:S(2)}) collective-permute-start(bf16[128,2048]{1,0:T(8,128)(2,1)} %get-tuple-element.228), channel_id=1, source_target_pairs={{0,2},{2,0},{4,6},{6,4},{1,3},{3,1},{5,7},{7,5},{8,10},{10,8},{12,... | collective-permute-start | bytes 1572872 | tf_op jit(solution)/shard_map/ppermute | solution.py:18
  170.7 13.7 %collective-permute-start.24 = (bf16[128,2048]{1,0:T(8,128)(2,1)}, bf16[128,2048]{1,0:T(8,128)(2,1)S(1)}, u32[]{:S(2)}, u32[]{:S(2)}) collective-permute-start(bf16[128,2048]{1,0:T(8,128)(2,1)} %get-tuple-element.229), channel_id=1, source_target_pairs={{0,4},{2,6},{4,0},{6,2},{1,5},{3,7},{5,1},{7,3},{8,12},{10,14},{12... | collective-permute-start | bytes 1572872 | tf_op jit(solution)/shard_map/ppermute | solution.py:22
  203.7 14.7 %collective-permute-start.29 = (bf16[128,2048]{1,0:T(8,128)(2,1)}, bf16[128,2048]{1,0:T(8,128)(2,1)S(1)}, u32[]{:S(2)}, u32[]{:S(2)}) collective-permute-start(bf16[128,2048]{1,0:T(8,128)(2,1)} %get-tuple-element.240.refs_1_), channel_id=1, source_target_pairs={{0,2},{2,0},{4,6},{6,4},{1,3},{3,1},{5,7},{7,5},{8,10},{10,8},{12,... | collective-permute-start | bytes 1572872 | tf_op jit(solution)/shard_map/ppermute | solution.py:18
  204.7 14.4 %collective-permute-start.30 = (bf16[128,2048]{1,0:T(8,128)(2,1)}, bf16[128,2048]{1,0:T(8,128)(2,1)S(1)}, u32[]{:S(2)}, u32[]{:S(2)}) collective-permute-start(bf16[128,2048]{1,0:T(8,128)(2,1)} %get-tuple-element.280.refs_0_), channel_id=1, source_target_pairs={{0,4},{2,6},{4,0},{6,2},{1,5},{3,7},{5,1},{7,3},{8,12},{10,14},{12... | collective-permute-start | bytes 1572872 | tf_op jit(solution)/shard_map/ppermute | solution.py:22
  205.9 18.1 %collective-permute-start.27 = (bf16[128,2048]{1,0:T(8,128)(2,1)}, bf16[128,2048]{1,0:T(8,128)(2,1)S(1)}, u32[]{:S(2)}, u32[]{:S(2)}) collective-permute-start(bf16[128,2048]{1,0:T(8,128)(2,1)} %get-tuple-element.280.refs_0_), channel_id=1, source_target_pairs={{0,2},{2,0},{4,6},{6,4},{1,3},{3,1},{5,7},{7,5},{8,10},{10,8},{12,... | collective-permute-start | bytes 1572872 | tf_op jit(solution)/shard_map/ppermute | solution.py:18
  206.7 17.9 %collective-permute-start.28 = (bf16[128,2048]{1,0:T(8,128)(2,1)}, bf16[128,2048]{1,0:T(8,128)(2,1)S(1)}, u32[]{:S(2)}, u32[]{:S(2)}) collective-permute-start(bf16[128,2048]{1,0:T(8,128)(2,1)} %get-tuple-element.240.refs_1_), channel_id=1, source_target_pairs={{0,4},{2,6},{4,0},{6,2},{1,5},{3,7},{5,1},{7,3},{8,12},{10,14},{12... | collective-permute-start | bytes 1572872 | tf_op jit(solution)/shard_map/ppermute | solution.py:22
  228.8 22.0 %collective-permute-start.33 = (bf16[2048,1408]{1,0:T(8,128)(2,1)}, bf16[2048,1408]{1,0:T(8,128)(2,1)}, u32[]{:S(2)}, u32[]{:S(2)}) collective-permute-start(bf16[2048,1408]{1,0:T(8,128)(2,1)} %all-gather.9.cloned.1.call-done.refs_8_.refs_10_), channel_id=1, source_target_pairs={{0,1},{1,0},{2,3},{3,2},{4,5},{5,4},{6,7},{7,6},{8,9},{9,8},{10,11... | collective-permute-start | bytes 17301512 | tf_op jit(solution)/shard_map/ppermute | solution.py:30
  230.9 209.6 %reduce-scatter.5.cloned.1.call-start = ((), (), s32[]{:S(2)}) async-start(), calls=%async_computation.8 | async-start | bytes 3932160 | tf_op jit(solution)/shard_map/reduce_scatter | solution.py:78
  231.1 14.3 %collective-permute-start.32 = (bf16[128,2048]{1,0:T(8,128)(2,1)S(1)}, bf16[128,2048]{1,0:T(8,128)(2,1)S(1)}, u32[]{:S(2)}, u32[]{:S(2)}) collective-permute-start(bf16[128,2048]{1,0:T(8,128)(2,1)S(1)} %collective-permute-done.28.refs_5_), channel_id=1, source_target_pairs={{0,2},{2,0},{4,6},{6,4},{1,3},{3,1},{5,7},{7,5},{8,10},{10,8},{12,... | collective-permute-start | bytes 1572872 | tf_op jit(solution)/shard_map/ppermute | solution.py:18
  232.7 14.0 %collective-permute-start.31 = (bf16[128,2048]{1,0:T(8,128)(2,1)S(1)}, bf16[128,2048]{1,0:T(8,128)(2,1)S(1)}, u32[]{:S(2)}, u32[]{:S(2)}) collective-permute-start(bf16[128,2048]{1,0:T(8,128)(2,1)S(1)} %collective-permute-done.27.refs_2_), channel_id=1, source_target_pairs={{0,4},{2,6},{4,0},{6,2},{1,5},{3,7},{5,1},{7,3},{8,12},{10,14},{12... | collective-permute-start | bytes 1572872 | tf_op jit(solution)/shard_map/ppermute | solution.py:22
  246.7 16.0 %collective-permute-start.36 = (bf16[128,2048]{1,0:T(8,128)(2,1)S(1)}, bf16[128,2048]{1,0:T(8,128)(2,1)S(1)}, u32[]{:S(2)}, u32[]{:S(2)}) collective-permute-start(bf16[128,2048]{1,0:T(8,128)(2,1)S(1)} %get-tuple-element.260.refs_1_.refs_8_), channel_id=1, source_target_pairs={{0,2},{2,0},{4,6},{6,4},{1,3},{3,1},{5,7},{7,5},{8,10},{10,8},{12,... | collective-permute-start | bytes 1572872 | tf_op jit(solution)/shard_map/ppermute | solution.py:18
  247.2 15.5 %collective-permute-start.37 = (bf16[128,2048]{1,0:T(8,128)(2,1)S(1)}, bf16[128,2048]{1,0:T(8,128)(2,1)S(1)}, u32[]{:S(2)}, u32[]{:S(2)}) collective-permute-start(bf16[128,2048]{1,0:T(8,128)(2,1)S(1)} %get-tuple-element.261.refs_0_.refs_7_), channel_id=1, source_target_pairs={{0,4},{2,6},{4,0},{6,2},{1,5},{3,7},{5,1},{7,3},{8,12},{10,14},{12... | collective-permute-start | bytes 1572872 | tf_op jit(solution)/shard_map/ppermute | solution.py:22
  248.7 22.5 %collective-permute-start.34 = (bf16[128,2048]{1,0:T(8,128)(2,1)S(1)}, bf16[128,2048]{1,0:T(8,128)(2,1)S(1)}, u32[]{:S(2)}, u32[]{:S(2)}) collective-permute-start(bf16[128,2048]{1,0:T(8,128)(2,1)S(1)} %get-tuple-element.261.refs_0_.refs_7_), channel_id=1, source_target_pairs={{0,2},{2,0},{4,6},{6,4},{1,3},{3,1},{5,7},{7,5},{8,10},{10,8},{12,... | collective-permute-start | bytes 1572872 | tf_op jit(solution)/shard_map/ppermute | solution.py:18
  250.2 21.4 %collective-permute-start.35 = (bf16[128,2048]{1,0:T(8,128)(2,1)S(1)}, bf16[128,2048]{1,0:T(8,128)(2,1)S(1)}, u32[]{:S(2)}, u32[]{:S(2)}) collective-permute-start(bf16[128,2048]{1,0:T(8,128)(2,1)S(1)} %get-tuple-element.260.refs_1_.refs_8_), channel_id=1, source_target_pairs={{0,4},{2,6},{4,0},{6,2},{1,5},{3,7},{5,1},{7,3},{8,12},{10,14},{12... | collective-permute-start | bytes 1572872 | tf_op jit(solution)/shard_map/ppermute | solution.py:22
  271.7 15.1 %collective-permute-start.38 = (bf16[128,2048]{1,0:T(8,128)(2,1)S(1)}, bf16[128,2048]{1,0:T(8,128)(2,1)S(1)}, u32[]{:S(2)}, u32[]{:S(2)}) collective-permute-start(bf16[128,2048]{1,0:T(8,128)(2,1)S(1)} %collective-permute-done.34.refs_2_.refs_0_), channel_id=1, source_target_pairs={{0,4},{2,6},{4,0},{6,2},{1,5},{3,7},{5,1},{7,3},{8,12},{10,14},{12... | collective-permute-start | bytes 1572872 | tf_op jit(solution)/shard_map/ppermute | solution.py:22
  325.2 38.6 %collective-permute-start.42 = (bf16[128,2048]{1,0:T(8,128)(2,1)}, bf16[128,2048]{1,0:T(8,128)(2,1)S(1)}, u32[]{:S(2)}, u32[]{:S(2)}) collective-permute-start(bf16[128,2048]{1,0:T(8,128)(2,1)} %get-tuple-element.269), channel_id=1, source_target_pairs={{0,2},{2,0},{4,6},{6,4},{1,3},{3,1},{5,7},{7,5},{8,10},{10,8},{12,... | collective-permute-start | bytes 1572872 | tf_op jit(solution)/shard_map/ppermute | solution.py:18
  325.9 37.9 %collective-permute-start.43 = (bf16[128,2048]{1,0:T(8,128)(2,1)}, bf16[128,2048]{1,0:T(8,128)(2,1)S(1)}, u32[]{:S(2)}, u32[]{:S(2)}) collective-permute-start(bf16[128,2048]{1,0:T(8,128)(2,1)} %get-tuple-element.275), channel_id=1, source_target_pairs={{0,4},{2,6},{4,0},{6,2},{1,5},{3,7},{5,1},{7,3},{8,12},{10,14},{12... | collective-permute-start | bytes 1572872 | tf_op jit(solution)/shard_map/ppermute | solution.py:22
  346.4 17.4 %collective-permute-start.45 = (bf16[128,2048]{1,0:T(8,128)(2,1)}, bf16[128,2048]{1,0:T(8,128)(2,1)S(1)}, u32[]{:S(2)}, u32[]{:S(2)}) collective-permute-start(bf16[128,2048]{1,0:T(8,128)(2,1)} %get-tuple-element.276), channel_id=1, source_target_pairs={{0,4},{2,6},{4,0},{6,2},{1,5},{3,7},{5,1},{7,3},{8,12},{10,14},{12... | collective-permute-start | bytes 1572872 | tf_op jit(solution)/shard_map/ppermute | solution.py:22
  347.9 15.9 %collective-permute-start.44 = (bf16[128,2048]{1,0:T(8,128)(2,1)}, bf16[128,2048]{1,0:T(8,128)(2,1)S(1)}, u32[]{:S(2)}, u32[]{:S(2)}) collective-permute-start(bf16[128,2048]{1,0:T(8,128)(2,1)} %get-tuple-element.271), channel_id=1, source_target_pairs={{0,2},{2,0},{4,6},{6,4},{1,3},{3,1},{5,7},{7,5},{8,10},{10,8},{12,... | collective-permute-start | bytes 1572872 | tf_op jit(solution)/shard_map/ppermute | solution.py:18
  349.3 171.1 %reduce-scatter.7.cloned.1.call-start = ((), (), s32[]{:S(2)}) async-start(), calls=%async_computation.9 | async-start | bytes 7208960 | tf_op jit(solution)/shard_map/reduce_scatter | solution.py:78
  376.5 25.1 %collective-permute-start.47 = (bf16[128,2048]{1,0:T(8,128)(2,1)S(1)}, bf16[128,2048]{1,0:T(8,128)(2,1)S(1)}, u32[]{:S(2)}, u32[]{:S(2)}) collective-permute-start(bf16[128,2048]{1,0:T(8,128)(2,1)S(1)} %add_convert_fusion.7), channel_id=1, source_target_pairs={{0,2},{2,0},{4,6},{6,4},{1,3},{3,1},{5,7},{7,5},{8,10},{10,8},{12,... | collective-permute-start | bytes 1572872 | tf_op jit(solution)/shard_map/ppermute | solution.py:18
  377.2 24.4 %collective-permute-start.48 = (bf16[128,2048]{1,0:T(8,128)(2,1)S(1)}, bf16[128,2048]{1,0:T(8,128)(2,1)S(1)}, u32[]{:S(2)}, u32[]{:S(2)}) collective-permute-start(bf16[128,2048]{1,0:T(8,128)(2,1)S(1)} %add_convert_fusion.6), channel_id=1, source_target_pairs={{0,4},{2,6},{4,0},{6,2},{1,5},{3,7},{5,1},{7,3},{8,12},{10,14},{12... | collective-permute-start | bytes 1572872 | tf_op jit(solution)/shard_map/ppermute | solution.py:22
  401.5 167.1 %reduce-scatter.9.cloned.1.call-start = ((), (), s32[]{:S(2)}) async-start(), calls=%async_computation.10 | async-start | bytes 2621440 | tf_op jit(solution)/shard_map/reduce_scatter | solution.py:78
  409.3 15.8 %collective-permute-start.51 = (bf16[128,2176]{1,0:T(8,128)(2,1)}, bf16[128,2176]{1,0:T(8,128)(2,1)S(1)}, u32[]{:S(2)}, u32[]{:S(2)}) collective-permute-start(bf16[128,2176]{1,0:T(8,128)(2,1)} %get-tuple-element.302.refs_1_), channel_id=1, source_target_pairs={{0,2},{2,0},{4,6},{6,4},{1,3},{3,1},{5,7},{7,5},{8,10},{10,8},{12,... | collective-permute-start | bytes 1671176 | tf_op jit(solution)/shard_map/ppermute | solution.py:18
  410.1 15.7 %collective-permute-start.52 = (bf16[128,2176]{1,0:T(8,128)(2,1)}, bf16[128,2176]{1,0:T(8,128)(2,1)S(1)}, u32[]{:S(2)}, u32[]{:S(2)}) collective-permute-start(bf16[128,2176]{1,0:T(8,128)(2,1)} %get-tuple-element.303.refs_0_), channel_id=1, source_target_pairs={{0,4},{2,6},{4,0},{6,2},{1,5},{3,7},{5,1},{7,3},{8,12},{10,14},{12... | collective-permute-start | bytes 1671176 | tf_op jit(solution)/shard_map/ppermute | solution.py:22
  410.6 25.6 %collective-permute-start.49 = (bf16[128,2176]{1,0:T(8,128)(2,1)}, bf16[128,2176]{1,0:T(8,128)(2,1)S(1)}, u32[]{:S(2)}, u32[]{:S(2)}) collective-permute-start(bf16[128,2176]{1,0:T(8,128)(2,1)} %get-tuple-element.303.refs_0_), channel_id=1, source_target_pairs={{0,2},{2,0},{4,6},{6,4},{1,3},{3,1},{5,7},{7,5},{8,10},{10,8},{12,... | collective-permute-start | bytes 1671176 | tf_op jit(solution)/shard_map/ppermute | solution.py:18
  412.0 24.6 %collective-permute-start.50 = (bf16[128,2176]{1,0:T(8,128)(2,1)}, bf16[128,2176]{1,0:T(8,128)(2,1)S(1)}, u32[]{:S(2)}, u32[]{:S(2)}) collective-permute-start(bf16[128,2176]{1,0:T(8,128)(2,1)} %get-tuple-element.302.refs_1_), channel_id=1, source_target_pairs={{0,4},{2,6},{4,0},{6,2},{1,5},{3,7},{5,1},{7,3},{8,12},{10,14},{12... | collective-permute-start | bytes 1671176 | tf_op jit(solution)/shard_map/ppermute | solution.py:22
  436.6 20.8 %collective-permute-start.53 = (bf16[128,2176]{1,0:T(8,128)(2,1)S(1)}, bf16[128,2176]{1,0:T(8,128)(2,1)S(1)}, u32[]{:S(2)}, u32[]{:S(2)}) collective-permute-start(bf16[128,2176]{1,0:T(8,128)(2,1)S(1)} %collective-permute-done.49.refs_2_), channel_id=1, source_target_pairs={{0,4},{2,6},{4,0},{6,2},{1,5},{3,7},{5,1},{7,3},{8,12},{10,14},{12... | collective-permute-start | bytes 1671176 | tf_op jit(solution)/shard_map/ppermute | solution.py:22
  437.2 20.3 %collective-permute-start.54 = (bf16[128,2176]{1,0:T(8,128)(2,1)S(1)}, bf16[128,2176]{1,0:T(8,128)(2,1)S(1)}, u32[]{:S(2)}, u32[]{:S(2)}) collective-permute-start(bf16[128,2176]{1,0:T(8,128)(2,1)S(1)} %collective-permute-done.50.refs_5_), channel_id=1, source_target_pairs={{0,2},{2,0},{4,6},{6,4},{1,3},{3,1},{5,7},{7,5},{8,10},{10,8},{12,... | collective-permute-start | bytes 1671176 | tf_op jit(solution)/shard_map/ppermute | solution.py:18
  457.5 40.7 %collective-permute-start.55 = (bf16[128,2048]{1,0:T(8,128)(2,1)S(1)}, bf16[128,2048]{1,0:T(8,128)(2,1)S(1)}, u32[]{:S(2)}, u32[]{:S(2)}) collective-permute-start(bf16[128,2048]{1,0:T(8,128)(2,1)S(1)} %copy-done.61), channel_id=1, source_target_pairs={{0,2},{2,0},{4,6},{6,4},{1,3},{3,1},{5,7},{7,5},{8,10},{10,8},{12,... | collective-permute-start | bytes 1572872 | tf_op jit(solution)/shard_map/ppermute | solution.py:18
  458.1 41.5 %collective-permute-start.56 = (bf16[128,2048]{1,0:T(8,128)(2,1)S(1)}, bf16[128,2048]{1,0:T(8,128)(2,1)S(1)}, u32[]{:S(2)}, u32[]{:S(2)}) collective-permute-start(bf16[128,2048]{1,0:T(8,128)(2,1)S(1)} %copy-done.89), channel_id=1, source_target_pairs={{0,4},{2,6},{4,0},{6,2},{1,5},{3,7},{5,1},{7,3},{8,12},{10,14},{12... | collective-permute-start | bytes 1572872 | tf_op jit(solution)/shard_map/ppermute | solution.py:22
  459.6 40.0 %collective-permute-start.57 = (bf16[128,2048]{1,0:T(8,128)(2,1)}, bf16[128,2048]{1,0:T(8,128)(2,1)S(1)}, u32[]{:S(2)}, u32[]{:S(2)}) collective-permute-start(bf16[128,2048]{1,0:T(8,128)(2,1)} %get-tuple-element.311), channel_id=1, source_target_pairs={{0,2},{2,0},{4,6},{6,4},{1,3},{3,1},{5,7},{7,5},{8,10},{10,8},{12,... | collective-permute-start | bytes 1572872 | tf_op jit(solution)/shard_map/ppermute | solution.py:18
  461.0 38.7 %collective-permute-start.58 = (bf16[128,2048]{1,0:T(8,128)(2,1)}, bf16[128,2048]{1,0:T(8,128)(2,1)S(1)}, u32[]{:S(2)}, u32[]{:S(2)}) collective-permute-start(bf16[128,2048]{1,0:T(8,128)(2,1)} %get-tuple-element.312), channel_id=1, source_target_pairs={{0,4},{2,6},{4,0},{6,2},{1,5},{3,7},{5,1},{7,3},{8,12},{10,14},{12... | collective-permute-start | bytes 1572872 | tf_op jit(solution)/shard_map/ppermute | solution.py:22
  495.4 22.9 %collective-permute-start.63 = (bf16[2048,512]{1,0:T(8,128)(2,1)S(1)}, bf16[2048,512]{1,0:T(8,128)(2,1)S(1)}, u32[]{:S(2)}, u32[]{:S(2)}) collective-permute-start(bf16[2048,512]{1,0:T(8,128)(2,1)S(1)} %pad_maximum_fusion.4), channel_id=1, source_target_pairs={{0,1},{1,0},{2,3},{3,2},{4,5},{5,4},{6,7},{7,6},{8,9},{9,8},{10,11... | collective-permute-start | bytes 6291464 | tf_op jit(solution)/shard_map/ppermute | solution.py:30
  499.8 18.6 %collective-permute-start.59 = (bf16[128,2048]{1,0:T(8,128)(2,1)S(1)}, bf16[128,2048]{1,0:T(8,128)(2,1)S(1)}, u32[]{:S(2)}, u32[]{:S(2)}) collective-permute-start(bf16[128,2048]{1,0:T(8,128)(2,1)S(1)} %add_convert_fusion.5), channel_id=1, source_target_pairs={{0,2},{2,0},{4,6},{6,4},{1,3},{3,1},{5,7},{7,5},{8,10},{10,8},{12,... | collective-permute-start | bytes 1572872 | tf_op jit(solution)/shard_map/ppermute | solution.py:18
  500.6 17.7 %collective-permute-start.60 = (bf16[128,2048]{1,0:T(8,128)(2,1)S(1)}, bf16[128,2048]{1,0:T(8,128)(2,1)S(1)}, u32[]{:S(2)}, u32[]{:S(2)}) collective-permute-start(bf16[128,2048]{1,0:T(8,128)(2,1)S(1)} %add_convert_fusion.4), channel_id=1, source_target_pairs={{0,4},{2,6},{4,0},{6,2},{1,5},{3,7},{5,1},{7,3},{8,12},{10,14},{12... | collective-permute-start | bytes 1572872 | tf_op jit(solution)/shard_map/ppermute | solution.py:22
  520.4 94.4 %reduce-scatter.11.cloned.1.call-start = ((), (), s32[]{:S(2)}) async-start(), calls=%async_computation.11 | async-start | bytes 2621440 | tf_op jit(solution)/shard_map/reduce_scatter | solution.py:78
  553.5 15.4 %collective-permute-start.66 = (bf16[128,2048]{1,0:T(8,128)(2,1)}, bf16[128,2048]{1,0:T(8,128)(2,1)S(1)}, u32[]{:S(2)}, u32[]{:S(2)}) collective-permute-start(bf16[128,2048]{1,0:T(8,128)(2,1)} %get-tuple-element.341), channel_id=1, source_target_pairs={{0,2},{2,0},{4,6},{6,4},{1,3},{3,1},{5,7},{7,5},{8,10},{10,8},{12,... | collective-permute-start | bytes 1572872 | tf_op jit(solution)/shard_map/ppermute | solution.py:18
  554.8 14.1 %collective-permute-start.67 = (bf16[128,2048]{1,0:T(8,128)(2,1)}, bf16[128,2048]{1,0:T(8,128)(2,1)S(1)}, u32[]{:S(2)}, u32[]{:S(2)}) collective-permute-start(bf16[128,2048]{1,0:T(8,128)(2,1)} %get-tuple-element.343), channel_id=1, source_target_pairs={{0,4},{2,6},{4,0},{6,2},{1,5},{3,7},{5,1},{7,3},{8,12},{10,14},{12... | collective-permute-start | bytes 1572872 | tf_op jit(solution)/shard_map/ppermute | solution.py:22
  566.9 14.0 %collective-permute-start.68 = (bf16[128,2048]{1,0:T(8,128)(2,1)}, bf16[128,2048]{1,0:T(8,128)(2,1)S(1)}, u32[]{:S(2)}, u32[]{:S(2)}) collective-permute-start(bf16[128,2048]{1,0:T(8,128)(2,1)} %get-tuple-element.344), channel_id=1, source_target_pairs={{0,2},{2,0},{4,6},{6,4},{1,3},{3,1},{5,7},{7,5},{8,10},{10,8},{12,... | collective-permute-start | bytes 1572872 | tf_op jit(solution)/shard_map/ppermute | solution.py:18
  583.0 14.9 %collective-permute-start.70 = (bf16[128,2048]{1,0:T(8,128)(2,1)S(1)}, bf16[128,2048]{1,0:T(8,128)(2,1)S(1)}, u32[]{:S(2)}, u32[]{:S(2)}) collective-permute-start(bf16[128,2048]{1,0:T(8,128)(2,1)S(1)} %add_convert_fusion.3), channel_id=1, source_target_pairs={{0,2},{2,0},{4,6},{6,4},{1,3},{3,1},{5,7},{7,5},{8,10},{10,8},{12,... | collective-permute-start | bytes 1572872 | tf_op jit(solution)/shard_map/ppermute | solution.py:18
  585.2 15.1 %collective-permute-start.71 = (bf16[128,2048]{1,0:T(8,128)(2,1)}, bf16[128,2048]{1,0:T(8,128)(2,1)S(1)}, u32[]{:S(2)}, u32[]{:S(2)}) collective-permute-start(bf16[128,2048]{1,0:T(8,128)(2,1)} %add_convert_fusion.2), channel_id=1, source_target_pairs={{0,4},{2,6},{4,0},{6,2},{1,5},{3,7},{5,1},{7,3},{8,12},{10,14},{12... | collective-permute-start | bytes 1572872 | tf_op jit(solution)/shard_map/ppermute | solution.py:22
  587.4 31.3 %collective-permute-start.74 = (bf16[128,2176]{1,0:T(8,128)(2,1)}, bf16[128,2176]{1,0:T(8,128)(2,1)}, u32[]{:S(2)}, u32[]{:S(2)}) collective-permute-start(bf16[128,2176]{1,0:T(8,128)(2,1)} %get-tuple-element.360), channel_id=1, source_target_pairs={{0,2},{2,0},{4,6},{6,4},{1,3},{3,1},{5,7},{7,5},{8,10},{10,8},{12,... | collective-permute-start | bytes 1671176 | tf_op jit(solution)/shard_map/ppermute | solution.py:18
  588.2 39.7 %collective-permute-start.75 = (bf16[128,2176]{1,0:T(8,128)(2,1)}, bf16[128,2176]{1,0:T(8,128)(2,1)}, u32[]{:S(2)}, u32[]{:S(2)}) collective-permute-start(bf16[128,2176]{1,0:T(8,128)(2,1)} %get-tuple-element.361), channel_id=1, source_target_pairs={{0,4},{2,6},{4,0},{6,2},{1,5},{3,7},{5,1},{7,3},{8,12},{10,14},{12... | collective-permute-start | bytes 1671176 | tf_op jit(solution)/shard_map/ppermute | solution.py:22
  589.4 39.9 %collective-permute-start.76 = (bf16[128,2176]{1,0:T(8,128)(2,1)}, bf16[128,2176]{1,0:T(8,128)(2,1)}, u32[]{:S(2)}, u32[]{:S(2)}) collective-permute-start(bf16[128,2176]{1,0:T(8,128)(2,1)} %get-tuple-element.362), channel_id=1, source_target_pairs={{0,6},{2,4},{4,2},{6,0},{1,7},{3,5},{5,3},{7,1},{8,14},{10,12},{12... | collective-permute-start | bytes 1671176 | tf_op jit(solution)/shard_map/ppermute | solution.py:26
  606.8 41.9 %collective-permute-start.80 = (f32[256,2048]{1,0:T(8,128)}, f32[256,2048]{1,0:T(8,128)S(1)}, u32[]{:S(2)}, u32[]{:S(2)}) collective-permute-start(f32[256,2048]{1,0:T(8,128)} %bitcast.180), channel_id=1, source_target_pairs={{0,1},{1,0},{2,3},{3,2},{4,5},{5,4},{6,7},{7,6},{8,9},{9,8},{10,11... | collective-permute-start | bytes 6291464 | tf_op jit(solution)/shard_map/ppermute | solution.py:30
  618.7 14.3 %collective-permute-start.78 = (bf16[128,1024]{1,0:T(8,128)(2,1)S(1)}, bf16[128,1024]{1,0:T(8,128)(2,1)}, u32[]{:S(2)}, u32[]{:S(2)}) collective-permute-start(bf16[128,1024]{1,0:T(8,128)(2,1)S(1)} %get-tuple-element.395), channel_id=1, source_target_pairs={{0,4},{2,6},{4,0},{6,2},{1,5},{3,7},{5,1},{7,3},{8,12},{10,14},{12... | collective-permute-start | bytes 786440 | tf_op jit(solution)/shard_map/ppermute | solution.py:22
  629.3 18.3 %collective-permute-start.72 = (bf16[256,1024]{1,0:T(8,128)(2,1)}, bf16[256,1024]{1,0:T(8,128)(2,1)S(1)}, u32[]{:S(2)}, u32[]{:S(2)}) collective-permute-start(bf16[256,1024]{1,0:T(8,128)(2,1)} %get-tuple-element.403), channel_id=1, source_target_pairs={{0,1},{1,0},{2,3},{3,2},{4,5},{5,4},{6,7},{7,6},{8,9},{9,8},{10,11... | collective-permute-start | bytes 1572872 | tf_op jit(solution)/shard_map/ppermute | solution.py:30
  640.6 15.8 %collective-permute-start.87 = (f32[4,1024]{1,0:T(4,128)S(1)}, f32[4,1024]{1,0:T(4,128)S(1)}, u32[]{:S(2)}, u32[]{:S(2)}) collective-permute-start(f32[4,1024]{1,0:T(4,128)S(1)} %add_add_fusion.1), channel_id=1, source_target_pairs={{0,24},{8,16},{16,8},{24,0},{1,25},{9,17},{17,9},{25,1},{2,26},{10... | collective-permute-start | bytes 49160 | tf_op jit(solution)/shard_map/ppermute | solution.py:119
  (124 other events, 1133.0 us)
Sparse Core Ops, SparseCore 0:
  28.5 46.3 all-gather.4
  76.5 44.6 all-gather.6
  123.3 105.4 all-gather.8
  231.0 66.3 all-gather.10
  349.4 65.2 reduce-scatter.4
  416.9 102.9 reduce-scatter.6
  522.2 44.3 reduce-scatter.8
  569.6 43.1 reduce-scatter.10

commit v4 on v3

--- a/solution.py
+++ b/solution.py
@@ -942,7 +942,7 @@
     (grad_down,) = rows_grad(cot_all, [[hidden_pieces(0)]], 0, swap_core(grad_other))
     w_down = gather_width(after(down, normed_mlp[2]))
     w_down = own_other(after(w_down, *hidden))
-    w_down[0] = after(w_down[0], grad_down)
+    w_down[0] = after(w_down[0], grad_other)
     grad_down = scatter_width(grad_down)
     d_acts = {}
 

time: 674 us -> 710 us (1.053)
  waiting for transfers between devices: 213 us -> 247 us
    all_gather x4, waiting for transfers between devices: 5.97 us -> 28.2 us  [gather_width(): return lax.all_gather(shard, 'seq', axis=0, tiled=True)]
    ppermute x31, waiting for transfers between devices: 54.3 us -> 74.5 us  [swap_y(): return lax.ppermute(v, 'batch', [(i, i ^ 2) for i in range(4)])]
    ppermute x4, waiting for transfers between devices: 16.7 us -> 7.89 us  [shift(): lax.ppermute(pair, 'seq', [(b, a) for a, b in hops] if back else hops)]
    unnamed x196 -> x200, local copies, waits for them, and re-layouts: 18.7 us -> 20.7 us
  transfers between devices with their start and end apart: 96 -> 96, of which waited for: 52 -> 56; matrix products, arithmetic and copies ran while one was open for 9% -> 8% of each run, Pallas kernels for 37% -> 38%
where the time goes in v4:
time: 710 us; the launch traced here: 701 us
  Pallas kernels  263 us (37%)
  waiting for transfers between devices  247 us (35%)
  starting transfers between devices  93.4 us (13%)
  local copies, waits for them, and re-layouts  53.2 us (7%)
  other arithmetic  27.5 us (4%)
  between operations  16.9 us (2%)
    pallas_call x21, Pallas kernels, call(): pl.pallas_call(body, in_specs=[ANYWHERE] * len(arrays), out_specs=[ANYWHE...  194 us
    ppermute x31, waiting for transfers between devices, swap_x(): return lax.ppermute(v, 'batch', [(i, i ^ 1) for i in range(4)])  111 us
    ppermute x31, waiting for transfers between devices, swap_y(): return lax.ppermute(v, 'batch', [(i, i ^ 2) for i in range(4)])  74.5 us
    pallas_call x4, Pallas kernels, channel_call(): pl.pallas_call(kernel, grid=(2,), in_specs=[spec(v.shape, skip) for v, sk...  35.9 us
    ppermute x31, starting transfers between devices, swap_x(): return lax.ppermute(v, 'batch', [(i, i ^ 1) for i in range(4)])  35.3 us
    ppermute x31, starting transfers between devices, swap_y(): return lax.ppermute(v, 'batch', [(i, i ^ 2) for i in range(4)])  33.3 us
    all_gather x4, waiting for transfers between devices, gather_width(): return lax.all_gather(shard, 'seq', axis=0, tiled=True)  28.2 us
    pallas_call x5, Pallas kernels, token_call(): pl.pallas_call(kernel, grid=(half // STEP,), in_specs=[spec(v.shape) for...  26.2 us
  transfers between devices with their start and end apart: 96, of which 56 were waited for; matrix products, arithmetic and copies ran while one was open for 8% of the time, Pallas kernels for 38%

profile of v4, /device:TPU:0, one launch (start us, length us, event | category | flops | bytes accessed | tf_op | source)
XLA Modules:
  0.0 700.7 jit_solution(7273080295205576218)
XLA Ops:
  10.8 3.0 collective-permute-start
  15.3 5.6 collective-permute-done
  20.9 6.2 collective-permute-done.1
  42.8 3.6 shard_map.246
  48.4 4.9 collective-permute-done.10
  53.3 11.6 %collective-permute-done.8 = bf16[128,2112]{0,1:T(8,128)(2,1)S(1)} collective-permute-done((bf16[128,2112]{0,1:T(8,128)(2,1)S(1)}, bf16[128,2112]{0,1:T(8,128)(2,1)S(1)}, u32[]{:S(2)}, u32[]{:S(2)}) %collective-permute-start.8) | collective-permute-done | bytes 540704 | tf_op jit(solution)/shard_map/ppermute | solution.py:18
  77.2 5.0 collective-permute-done.11.refs_3_
  84.9 12.1 %collective-permute-done.13.refs_6_ = bf16[128,2048]{1,0:T(8,128)(2,1)S(1)} collective-permute-done((bf16[128,2048]{1,0:T(8,128)(2,1)S(1)}, bf16[128,2048]{1,0:T(8,128)(2,1)S(1)}, u32[]{:S(2)}, u32[]{:S(2)}) %collective-permute-start.13) | collective-permute-done | bytes 524320 | tf_op jit(solution)/shard_map/ppermute | solution.py:22
  101.8 8.8 %shard_map.247.proj_in.proj_forget = f32[2048,512]{1,0:T(8,128)} custom-call(bf16[128,2048]{1,0:T(8,128)(2,1)} %get-tuple-element.210.refs_0_, bf16[128,2048]{1,0:T(8,128)(2,1)} %get-tuple-element.209.refs_1_, bf16[128,2048]{1,0:T(8,128)(2,1)} %copy-done.6, bf16[128,2048]{1,0:T(8,128)(2,1)} %copy-done.8, bf16[128,2048]{1,0:T(8,128)(2,1)} %copy-done.9, ...), custom_call_target="tpu_custom_call" | custom-call | tf_op jit(solution)/shard_map/pallas_call | solution.py:153
  110.6 10.2 %shard_map.248 = (f32[2048,256]{1,0:T(8,128)}, f32[2048,256]{1,0:T(8,128)}, f32[2048,256]{1,0:T(8,128)}) custom-call(f32[2048,512]{1,0:T(8,128)} %shard_map.247.proj_in.proj_forget, f32[2048,512]{1,0:T(8,128)} %shard_map.247.proj_in.proj_forget, f32[8,256]{1,0:T(8,128)} %tile.20.bound, f32[2048,1]{1,0:T(8,128)} %reshape_reshape.8.keep), custom_call_target="tpu_custom_call" | custom-call | tf_op jit(solution)/shard_map/pallas_call | solution.py:523
  123.0 3.4 collective-permute-start.16
  127.8 5.4 collective-permute-start.17
  136.6 6.7 shard_map.249.gate
  143.2 4.7 shard_map.250
  150.7 2.5 collective-permute-done.19
  157.0 3.3 shard_map.251
  161.5 5.7 shard_map.252
  170.2 12.0 %collective-permute-done.23.refs_1_ = bf16[128,2048]{1,0:T(8,128)(2,1)S(1)} collective-permute-done((bf16[128,2048]{1,0:T(8,128)(2,1)}, bf16[128,2048]{1,0:T(8,128)(2,1)S(1)}, u32[]{:S(2)}, u32[]{:S(2)}) %collective-permute-start.23) | collective-permute-done | bytes 524320 | tf_op jit(solution)/shard_map/ppermute | solution.py:18
  183.3 6.9 collective-permute-done.22
  195.8 5.1 collective-permute-done.26.refs_3_
  203.3 5.7 shard_map.253
  213.1 8.9 %collective-permute-done.29.refs_3_ = bf16[128,2048]{1,0:T(8,128)(2,1)S(1)} collective-permute-done((bf16[128,2048]{1,0:T(8,128)(2,1)}, bf16[128,2048]{1,0:T(8,128)(2,1)S(1)}, u32[]{:S(2)}, u32[]{:S(2)}) %collective-permute-start.29) | collective-permute-done | bytes 524320 | tf_op jit(solution)/shard_map/ppermute | solution.py:18
  222.8 4.8 collective-permute-done.27.refs_2_
  235.8 10.0 %collective-permute-done.31.refs_6_ = bf16[128,2048]{1,0:T(8,128)(2,1)S(1)} collective-permute-done((bf16[128,2048]{1,0:T(8,128)(2,1)S(1)}, bf16[128,2048]{1,0:T(8,128)(2,1)S(1)}, u32[]{:S(2)}, u32[]{:S(2)}) %collective-permute-start.31) | collective-permute-done | bytes 524320 | tf_op jit(solution)/shard_map/ppermute | solution.py:22
  251.0 11.8 %shard_map.254 = (f32[1024,704]{1,0:T(8,128)}, f32[1024,704]{1,0:T(8,128)}, bf16[1024,768]{1,0:T(8,128)(2,1)}) custom-call(bf16[128,2048]{1,0:T(8,128)(2,1)} %get-tuple-element.280.refs_0_, bf16[128,2048]{1,0:T(8,128)(2,1)} %get-tuple-element.240.refs_1_, bf16[128,2048]{1,0:T(8,128)(2,1)} %copy-done.14, bf16[128,2048]{1,0:T(8,128)(2,1)} %copy-done.12, ...), custom_call_target="tpu_custom_call" | custom-call | tf_op jit(solution)/shard_map/pallas_call | solution.py:153
  262.9 12.1 %shard_map.255 = (f32[1024,704]{1,0:T(8,128)}, f32[1024,704]{1,0:T(8,128)}, bf16[1024,768]{1,0:T(8,128)(2,1)}) custom-call(bf16[128,2048]{1,0:T(8,128)(2,1)} %get-tuple-element.280.refs_0_, bf16[128,2048]{1,0:T(8,128)(2,1)} %get-tuple-element.240.refs_1_, bf16[128,2048]{1,0:T(8,128)(2,1)} %copy-done.14, bf16[128,2048]{1,0:T(8,128)(2,1)} %copy-done.12, ...), custom_call_target="tpu_custom_call" | custom-call | tf_op jit(solution)/shard_map/pallas_call | solution.py:153
  275.1 27.4 %all-gather.11.cloned.1.call-done.refs_6_.refs_8_.refs_1_ = bf16[2048,768]{1,0:T(8,128)(2,1)} async-done(((bf16[512,768]{1,0:T(8,128)(2,1)}), bf16[2048,768]{1,0:T(8,128)(2,1)}) %all-gather.11.cloned.1.call-update) | async-done | bytes 3145744 | tf_op jit(solution)/shard_map/all_gather | solution.py:70
  305.4 11.4 %collective-permute-done.38.refs_6_.refs_0_ = bf16[128,2048]{1,0:T(8,128)(2,1)S(1)} collective-permute-done((bf16[128,2048]{1,0:T(8,128)(2,1)S(1)}, bf16[128,2048]{1,0:T(8,128)(2,1)S(1)}, u32[]{:S(2)}, u32[]{:S(2)}) %collective-permute-start.38) | collective-permute-done | bytes 524320 | tf_op jit(solution)/shard_map/ppermute | solution.py:22
  318.8 7.0 %shard_map.256 = bf16[2048,768]{1,0:T(8,128)(2,1)} custom-call(bf16[128,2048]{1,0:T(8,128)(2,1)} %copy-done.5, bf16[128,2048]{1,0:T(8,128)(2,1)} %copy-done.4, bf16[128,2048]{1,0:T(8,128)(2,1)} %copy-done.25, bf16[128,2048]{1,0:T(8,128)(2,1)} %copy-done.23, bf16[128,2048]{1,0:T(8,128)(2,1)} %copy-done.24, bf16[128,2048]{1,0:T(8,128)(2,1)} %copy-done.26, ...), custom_call_target="tpu_custom_call" | custom-call | tf_op jit(solution)/shard_map/pallas_call | solution.py:153
  327.6 13.6 %shard_map.257 = (bf16[512,1408]{1,0:T(8,128)(2,1)}, bf16[128,2048]{1,0:T(8,128)(2,1)}, bf16[128,2048]{1,0:T(8,128)(2,1)}) custom-call(bf16[128,2048]{1,0:T(8,128)(2,1)} %copy-done.27, bf16[128,2048]{1,0:T(8,128)(2,1)} %copy-done.28, f32[1024,704]{1,0:T(8,128)} %get-tuple-element.253.refs_2_.refs_4_, f32[1024,704]{1,0:T(8,128)} %get-tuple-element.254.refs_3_.refs_5_, ...), custom_call_target="tpu_custom_call" | custom-call | tf_op jit(solution)/shard_map/pallas_call | solution.py:153
  342.7 19.9 %shard_map.258 = (bf16[1024,1408]{1,0:T(8,128)(2,1)}, bf16[128,2048]{1,0:T(8,128)(2,1)}, f32[128,2048]{1,0:T(8,128)}, f32[128,2048]{1,0:T(8,128)}, bf16[128,2048]{1,0:T(8,128)(2,1)}) custom-call(bf16[128,2048]{1,0:T(8,128)(2,1)} %copy-done.25, bf16[128,2048]{1,0:T(8,128)(2,1)} %copy-done.23, bf16[128,2048]{1,0:T(8,128)(2,1)} %copy-done.24, ...), custom_call_target="tpu_custom_call" | custom-call | tf_op jit(solution)/shard_map/pallas_call | solution.py:153
  365.3 14.2 %shard_map.259 = (bf16[512,1408]{1,0:T(8,128)(2,1)}, f32[256,2048]{1,0:T(8,128)}) custom-call(bf16[128,2048]{1,0:T(8,128)(2,1)} %copy-done.5, bf16[128,2048]{1,0:T(8,128)(2,1)} %copy-done.4, f32[1024,704]{1,0:T(8,128)} %get-tuple-element.253.refs_2_.refs_4_, f32[1024,704]{1,0:T(8,128)} %get-tuple-element.254.refs_3_.refs_5_, ...), custom_call_target="tpu_custom_call" | custom-call | tf_op jit(solution)/shard_map/pallas_call | solution.py:153
  381.2 8.1 %shard_map.266 = bf16[2048,768]{1,0:T(8,128)(2,1)} custom-call(bf16[128,2048]{1,0:T(8,128)(2,1)} %copy-done.5, bf16[128,2048]{1,0:T(8,128)(2,1)} %copy-done.4, bf16[128,2048]{1,0:T(8,128)(2,1)} %copy-done.25, bf16[128,2048]{1,0:T(8,128)(2,1)} %copy-done.23, bf16[128,2048]{1,0:T(8,128)(2,1)} %copy-done.24, bf16[128,2048]{1,0:T(8,128)(2,1)} %copy-done.26, ...), custom_call_target="tpu_custom_call" | custom-call | tf_op jit(solution)/shard_map/pallas_call | solution.py:153
  391.6 11.5 %shard_map.260 = bf16[2048,1408]{1,0:T(8,128)(2,1)} custom-call(bf16[128,2048]{1,0:T(8,128)(2,1)} %get-tuple-element.280.refs_0_, bf16[128,2048]{1,0:T(8,128)(2,1)} %get-tuple-element.240.refs_1_, bf16[128,2048]{1,0:T(8,128)(2,1)} %copy-done.14, bf16[128,2048]{1,0:T(8,128)(2,1)} %copy-done.12, bf16[128,2048]{1,0:T(8,128)(2,1)} %copy-done.13, ...), custom_call_target="tpu_custom_call" | custom-call | tf_op jit(solution)/shard_map/pallas_call | solution.py:153
  405.4 7.4 %collective-permute-done.45.refs_11_ = bf16[2048,1408]{1,0:T(8,128)(2,1)S(1)} collective-permute-done((bf16[2048,1408]{1,0:T(8,128)(2,1)}, bf16[2048,1408]{1,0:T(8,128)(2,1)S(1)}, u32[]{:S(2)}, u32[]{:S(2)}) %collective-permute-start.45) | collective-permute-done | bytes 5767200 | tf_op jit(solution)/shard_map/ppermute | solution.py:30
  412.7 2.6 copy-done.18
  415.3 12.6 %shard_map.261 = bf16[2048,1408]{1,0:T(8,128)(2,1)} custom-call(bf16[128,2048]{1,0:T(8,128)(2,1)} %get-tuple-element.280.refs_0_, bf16[128,2048]{1,0:T(8,128)(2,1)} %get-tuple-element.240.refs_1_, bf16[128,2048]{1,0:T(8,128)(2,1)} %copy-done.14, bf16[128,2048]{1,0:T(8,128)(2,1)} %copy-done.12, bf16[128,2048]{1,0:T(8,128)(2,1)} %copy-done.13, ...), custom_call_target="tpu_custom_call" | custom-call | tf_op jit(solution)/shard_map/pallas_call | solution.py:153
  429.4 6.7 shard_map.262
  440.2 11.6 %collective-permute-done.50.refs_3_ = bf16[128,2176]{1,0:T(8,128)(2,1)S(1)} collective-permute-done((bf16[128,2176]{1,0:T(8,128)(2,1)}, bf16[128,2176]{1,0:T(8,128)(2,1)S(1)}, u32[]{:S(2)}, u32[]{:S(2)}) %collective-permute-start.50) | collective-permute-done | bytes 557088 | tf_op jit(solution)/shard_map/ppermute | solution.py:18
  453.3 9.6 %collective-permute-done.48.refs_2_ = bf16[128,2176]{1,0:T(8,128)(2,1)S(1)} collective-permute-done((bf16[128,2176]{1,0:T(8,128)(2,1)}, bf16[128,2176]{1,0:T(8,128)(2,1)S(1)}, u32[]{:S(2)}, u32[]{:S(2)}) %collective-permute-start.48) | collective-permute-done | bytes 557088 | tf_op jit(solution)/shard_map/ppermute | solution.py:18
  467.3 5.9 shard_map.263
  473.2 11.0 %shard_map.264 = (bf16[128,2048]{1,0:T(8,128)(2,1)}, f32[128,2048]{1,0:T(8,128)}, f32[128,2048]{1,0:T(8,128)}, bf16[128,2048]{1,0:T(8,128)(2,1)}, f32[256,2048]{1,0:T(8,128)}) custom-call(bf16[1024,768]{1,0:T(8,128)(2,1)} %get-tuple-element.294.refs_0_.refs_8_, bf16[2048,768]{1,0:T(8,128)(2,1)} %all-gather.11.cloned.1.call-done.refs_6_.refs_8_.refs_1_, ...), custom_call_target="tpu_custom_call" | custom-call | tf_op jit(solution)/shard_map/pallas_call | solution.py:153
  485.3 6.7 shard_map.265.d_gated
  492.0 13.4 %shard_map.267 = (bf16[2048,256]{1,0:T(8,128)(2,1)}, bf16[2048,256]{1,0:T(8,128)(2,1)}, f32[8,256]{1,0:T(8,128)}, f32[2048,256]{1,0:T(8,128)}, f32[2048,256]{1,0:T(8,128)}) custom-call(f32[2048,256]{1,0:T(8,128)} %shard_map.265.d_gated, f32[2048,256]{1,0:T(8,128)} %shard_map.249.gate, f32[2048,256]{1,0:T(8,128)} %get-tuple-element.324.state, ...), custom_call_target="tpu_custom_call" | custom-call | flops 37399998464 | tf_op jit(solution)/shard_map/pallas_call | solution.py:523
  505.4 5.8 shard_map.268
  511.3 5.9 shard_map.269
  525.6 6.6 collective-permute-done.54
  533.7 7.4 %collective-permute-done.56.refs_1_ = bf16[128,2048]{1,0:T(8,128)(2,1)S(1)} collective-permute-done((bf16[128,2048]{1,0:T(8,128)(2,1)S(1)}, bf16[128,2048]{1,0:T(8,128)(2,1)S(1)}, u32[]{:S(2)}, u32[]{:S(2)}) %collective-permute-start.56) | collective-permute-done | bytes 524320 | tf_op jit(solution)/shard_map/ppermute | solution.py:18
  545.8 5.7 collective-permute-done.62
  561.1 7.6 %shard_map.270 = (bf16[2048,256]{1,0:T(8,128)(2,1)}, bf16[2048,256]{1,0:T(8,128)(2,1)}, f32[8,256]{1,0:T(8,128)}) custom-call(f32[2048,256]{1,0:T(8,128)} %get-tuple-element.327.local, f32[2048,256]{1,0:T(8,128)} %get-tuple-element.328.product, f32[8,256]{1,0:T(8,128)} %fusion.21.returned, f32[2048,256]{1,0:T(8,128)} %get-tuple-element.324.state, ...), custom_call_target="tpu_custom_call" | custom-call | tf_op jit(solution)/shard_map/pallas_call | solution.py:523
  568.7 8.5 %shard_map.271 = (bf16[2048,512]{1,0:T(8,128)(2,1)}, bf16[2048,512]{1,0:T(8,128)(2,1)}) custom-call(bf16[128,2048]{1,0:T(8,128)(2,1)} %get-tuple-element.210.refs_0_, bf16[128,2048]{1,0:T(8,128)(2,1)} %get-tuple-element.209.refs_1_, bf16[128,2048]{1,0:T(8,128)(2,1)} %copy-done.6, bf16[128,2048]{1,0:T(8,128)(2,1)} %copy-done.8, bf16[128,2048]{1,0:T(8,128)(2,1)} %copy-done.9, ...), custom_call_target="tpu_custom_call" | custom-call | tf_op jit(solution)/shard_map/pallas_call | solution.py:153
  577.3 4.4 collective-permute-done.64
  581.6 3.6 add_convert_fusion
  585.3 4.8 shard_map.272
  593.5 10.4 %shard_map.273 = (bf16[128,2048]{1,0:T(8,128)(2,1)}, f32[128,2048]{1,0:T(8,128)}, f32[128,2048]{1,0:T(8,128)}, bf16[128,2048]{1,0:T(8,128)(2,1)}, f32[256,2048]{1,0:T(8,128)}) custom-call(bf16[2048,256]{1,0:T(8,128)(2,1)} %get-tuple-element.340.refs_8_.refs_0_, bf16[2048,512]{1,0:T(8,128)(2,1)} %all-gather.5.cloned.1.call-done.refs_8_.refs_1_, ...), custom_call_target="tpu_custom_call" | custom-call | tf_op jit(solution)/shard_map/pallas_call | solution.py:153
  606.2 11.5 %collective-permute-done.68.refs_1_ = bf16[128,2048]{1,0:T(8,128)(2,1)S(1)} collective-permute-done((bf16[128,2048]{1,0:T(8,128)(2,1)}, bf16[128,2048]{1,0:T(8,128)(2,1)S(1)}, u32[]{:S(2)}, u32[]{:S(2)}) %collective-permute-start.68) | collective-permute-done | bytes 524320 | tf_op jit(solution)/shard_map/ppermute | solution.py:18
  618.7 2.4 add_convert_fusion.2
  629.1 7.0 %collective-permute-done.71.refs_3_ = bf16[128,2048]{1,0:T(8,128)(2,1)S(1)} collective-permute-done((bf16[128,2048]{1,0:T(8,128)(2,1)}, bf16[128,2048]{1,0:T(8,128)(2,1)S(1)}, u32[]{:S(2)}, u32[]{:S(2)}) %collective-permute-start.71) | collective-permute-done | bytes 524320 | tf_op jit(solution)/shard_map/ppermute | solution.py:22
  639.0 5.8 shard_map.274
  646.3 4.4 shard_map.275
  661.2 5.1 collective-permute-done.77.refs_5_
  666.9 4.4 collective-permute-done.79.refs_7_
  679.8 3.6 collective-permute-start.87
  685.8 6.4 shard_map.276
  (489 shorter events, 181.8 us)
Async XLA Ops:
  7.2 90.0 %all-gather.5.cloned.1.call-start = ((), (), s32[]{:S(2)}) async-start(), calls=%async_computation.4 | async-start | bytes 2621440 | tf_op jit(solution)/shard_map/all_gather | solution.py:70
  28.6 92.7 %all-gather.7.cloned.1.call-start = ((), (), s32[]{:S(2)}) async-start(), calls=%async_computation.5 | async-start | bytes 2621440 | tf_op jit(solution)/shard_map/all_gather | solution.py:70
  36.4 192.5 %all-gather.9.cloned.1.call-start = ((), (), s32[]{:S(2)}) async-start(), calls=%async_computation.6 | async-start | bytes 7208960 | tf_op jit(solution)/shard_map/all_gather | solution.py:70
  37.1 16.2 %collective-permute-start.10 = (bf16[128,2112]{0,1:T(8,128)(2,1)S(1)}, bf16[128,2112]{0,1:T(8,128)(2,1)S(1)}, u32[]{:S(2)}, u32[]{:S(2)}) collective-permute-start(bf16[128,2112]{0,1:T(8,128)(2,1)S(1)} %get-tuple-element.390), channel_id=1, source_target_pairs={{0,6},{2,4},{4,2},{6,0},{1,7},{3,5},{5,3},{7,1},{8,14},{10,12},{12... | collective-permute-start | bytes 1622024 | tf_op jit(solution)/shard_map/ppermute | solution.py:26
  38.6 26.3 %collective-permute-start.8 = (bf16[128,2112]{0,1:T(8,128)(2,1)S(1)}, bf16[128,2112]{0,1:T(8,128)(2,1)S(1)}, u32[]{:S(2)}, u32[]{:S(2)}) collective-permute-start(bf16[128,2112]{0,1:T(8,128)(2,1)S(1)} %get-tuple-element.392), channel_id=1, source_target_pairs={{0,2},{2,0},{4,6},{6,4},{1,3},{3,1},{5,7},{7,5},{8,10},{10,8},{12,... | collective-permute-start | bytes 1622024 | tf_op jit(solution)/shard_map/ppermute | solution.py:18
  40.1 24.8 %collective-permute-start.9 = (bf16[128,2112]{0,1:T(8,128)(2,1)S(1)}, bf16[128,2112]{0,1:T(8,128)(2,1)S(1)}, u32[]{:S(2)}, u32[]{:S(2)}) collective-permute-start(bf16[128,2112]{0,1:T(8,128)(2,1)S(1)} %get-tuple-element.391), channel_id=1, source_target_pairs={{0,4},{2,6},{4,0},{6,2},{1,5},{3,7},{5,1},{7,3},{8,12},{10,14},{12... | collective-permute-start | bytes 1622024 | tf_op jit(solution)/shard_map/ppermute | solution.py:22
  46.3 30.8 %collective-permute-start.3 = (bf16[128,2048]{1,0:T(8,128)(2,1)}, bf16[128,2048]{1,0:T(8,128)(2,1)S(1)}, u32[]{:S(2)}, u32[]{:S(2)}) collective-permute-start(bf16[128,2048]{1,0:T(8,128)(2,1)} %get-tuple-element.210.refs_0_), channel_id=1, source_target_pairs={{0,2},{2,0},{4,6},{6,4},{1,3},{3,1},{5,7},{7,5},{8,10},{10,8},{12,... | collective-permute-start | bytes 1572872 | tf_op jit(solution)/shard_map/ppermute | solution.py:18
  47.6 29.6 %collective-permute-start.4 = (bf16[128,2048]{1,0:T(8,128)(2,1)}, bf16[128,2048]{1,0:T(8,128)(2,1)S(1)}, u32[]{:S(2)}, u32[]{:S(2)}) collective-permute-start(bf16[128,2048]{1,0:T(8,128)(2,1)} %get-tuple-element.209.refs_1_), channel_id=1, source_target_pairs={{0,4},{2,6},{4,0},{6,2},{1,5},{3,7},{5,1},{7,3},{8,12},{10,14},{12... | collective-permute-start | bytes 1572872 | tf_op jit(solution)/shard_map/ppermute | solution.py:22
  64.9 17.3 %collective-permute-start.11 = (bf16[128,2048]{1,0:T(8,128)(2,1)}, bf16[128,2048]{1,0:T(8,128)(2,1)S(1)}, u32[]{:S(2)}, u32[]{:S(2)}) collective-permute-start(bf16[128,2048]{1,0:T(8,128)(2,1)} %get-tuple-element.209.refs_1_), channel_id=1, source_target_pairs={{0,2},{2,0},{4,6},{6,4},{1,3},{3,1},{5,7},{7,5},{8,10},{10,8},{12,... | collective-permute-start | bytes 1572872 | tf_op jit(solution)/shard_map/ppermute | solution.py:18
  65.4 17.7 %collective-permute-start.12 = (bf16[128,2048]{1,0:T(8,128)(2,1)}, bf16[128,2048]{1,0:T(8,128)(2,1)S(1)}, u32[]{:S(2)}, u32[]{:S(2)}) collective-permute-start(bf16[128,2048]{1,0:T(8,128)(2,1)} %get-tuple-element.210.refs_0_), channel_id=1, source_target_pairs={{0,4},{2,6},{4,0},{6,2},{1,5},{3,7},{5,1},{7,3},{8,12},{10,14},{12... | collective-permute-start | bytes 1572872 | tf_op jit(solution)/shard_map/ppermute | solution.py:22
  77.1 225.3 %all-gather.11.cloned.1.call-start = ((), (), s32[]{:S(2)}) async-start(), calls=%async_computation.7 | async-start | bytes 3932160 | tf_op jit(solution)/shard_map/all_gather | solution.py:70
  83.1 13.8 %collective-permute-start.13 = (bf16[128,2048]{1,0:T(8,128)(2,1)S(1)}, bf16[128,2048]{1,0:T(8,128)(2,1)S(1)}, u32[]{:S(2)}, u32[]{:S(2)}) collective-permute-start(bf16[128,2048]{1,0:T(8,128)(2,1)S(1)} %collective-permute-done.3.refs_2_), channel_id=1, source_target_pairs={{0,4},{2,6},{4,0},{6,2},{1,5},{3,7},{5,1},{7,3},{8,12},{10,14},{12... | collective-permute-start | bytes 1572872 | tf_op jit(solution)/shard_map/ppermute | solution.py:22
  83.8 13.4 %collective-permute-start.14 = (bf16[128,2048]{1,0:T(8,128)(2,1)S(1)}, bf16[128,2048]{1,0:T(8,128)(2,1)S(1)}, u32[]{:S(2)}, u32[]{:S(2)}) collective-permute-start(bf16[128,2048]{1,0:T(8,128)(2,1)S(1)} %collective-permute-done.4.refs_5_), channel_id=1, source_target_pairs={{0,2},{2,0},{4,6},{6,4},{1,3},{3,1},{5,7},{7,5},{8,10},{10,8},{12,... | collective-permute-start | bytes 1572872 | tf_op jit(solution)/shard_map/ppermute | solution.py:18
  121.2 14.0 %collective-permute-start.18 = (bf16[2048,512]{1,0:T(8,128)(2,1)}, bf16[2048,512]{1,0:T(8,128)(2,1)S(1)}, u32[]{:S(2)}, u32[]{:S(2)}) collective-permute-start(bf16[2048,512]{1,0:T(8,128)(2,1)} %all-gather.7.cloned.1.call-done.refs_8_.refs_1_.refs_5_), channel_id=1, source_target_pairs={{0,1},{1,0},{2,3},{3,2},{4,5},{5,4},{6,7},{7,6},{8,9},{9,8},{10,11... | collective-permute-start | bytes 6291464 | tf_op jit(solution)/shard_map/ppermute | solution.py:30
  160.3 22.9 %collective-permute-start.21 = (bf16[128,2048]{1,0:T(8,128)(2,1)}, bf16[128,2048]{1,0:T(8,128)(2,1)S(1)}, u32[]{:S(2)}, u32[]{:S(2)}) collective-permute-start(bf16[128,2048]{1,0:T(8,128)(2,1)} %get-tuple-element.225.refs_3_), channel_id=1, source_target_pairs={{0,2},{2,0},{4,6},{6,4},{1,3},{3,1},{5,7},{7,5},{8,10},{10,8},{12,... | collective-permute-start | bytes 1572872 | tf_op jit(solution)/shard_map/ppermute | solution.py:18
  167.2 15.0 %collective-permute-start.23 = (bf16[128,2048]{1,0:T(8,128)(2,1)}, bf16[128,2048]{1,0:T(8,128)(2,1)S(1)}, u32[]{:S(2)}, u32[]{:S(2)}) collective-permute-start(bf16[128,2048]{1,0:T(8,128)(2,1)} %get-tuple-element.228), channel_id=1, source_target_pairs={{0,2},{2,0},{4,6},{6,4},{1,3},{3,1},{5,7},{7,5},{8,10},{10,8},{12,... | collective-permute-start | bytes 1572872 | tf_op jit(solution)/shard_map/ppermute | solution.py:18
  168.2 15.1 %collective-permute-start.24 = (bf16[128,2048]{1,0:T(8,128)(2,1)}, bf16[128,2048]{1,0:T(8,128)(2,1)S(1)}, u32[]{:S(2)}, u32[]{:S(2)}) collective-permute-start(bf16[128,2048]{1,0:T(8,128)(2,1)} %get-tuple-element.229), channel_id=1, source_target_pairs={{0,4},{2,6},{4,0},{6,2},{1,5},{3,7},{5,1},{7,3},{8,12},{10,14},{12... | collective-permute-start | bytes 1572872 | tf_op jit(solution)/shard_map/ppermute | solution.py:22
  169.7 20.5 %collective-permute-start.22 = (bf16[128,2048]{1,0:T(8,128)(2,1)S(1)}, bf16[128,2048]{1,0:T(8,128)(2,1)S(1)}, u32[]{:S(2)}, u32[]{:S(2)}) collective-permute-start(bf16[128,2048]{1,0:T(8,128)(2,1)S(1)} %copy-done.93), channel_id=1, source_target_pairs={{0,4},{2,6},{4,0},{6,2},{1,5},{3,7},{5,1},{7,3},{8,12},{10,14},{12... | collective-permute-start | bytes 1572872 | tf_op jit(solution)/shard_map/ppermute | solution.py:22
  210.7 16.9 %collective-permute-start.27 = (bf16[128,2048]{1,0:T(8,128)(2,1)}, bf16[128,2048]{1,0:T(8,128)(2,1)S(1)}, u32[]{:S(2)}, u32[]{:S(2)}) collective-permute-start(bf16[128,2048]{1,0:T(8,128)(2,1)} %get-tuple-element.280.refs_0_), channel_id=1, source_target_pairs={{0,2},{2,0},{4,6},{6,4},{1,3},{3,1},{5,7},{7,5},{8,10},{10,8},{12,... | collective-permute-start | bytes 1572872 | tf_op jit(solution)/shard_map/ppermute | solution.py:18
  211.7 16.7 %collective-permute-start.28 = (bf16[128,2048]{1,0:T(8,128)(2,1)}, bf16[128,2048]{1,0:T(8,128)(2,1)S(1)}, u32[]{:S(2)}, u32[]{:S(2)}) collective-permute-start(bf16[128,2048]{1,0:T(8,128)(2,1)} %get-tuple-element.240.refs_1_), channel_id=1, source_target_pairs={{0,4},{2,6},{4,0},{6,2},{1,5},{3,7},{5,1},{7,3},{8,12},{10,14},{12... | collective-permute-start | bytes 1572872 | tf_op jit(solution)/shard_map/ppermute | solution.py:22
  228.9 34.1 %collective-permute-start.33 = (bf16[2048,1408]{1,0:T(8,128)(2,1)}, bf16[2048,1408]{1,0:T(8,128)(2,1)}, u32[]{:S(2)}, u32[]{:S(2)}) collective-permute-start(bf16[2048,1408]{1,0:T(8,128)(2,1)} %all-gather.9.cloned.1.call-done.refs_8_.refs_10_), channel_id=1, source_target_pairs={{0,1},{1,0},{2,3},{3,2},{4,5},{5,4},{6,7},{7,6},{8,9},{9,8},{10,11... | collective-permute-start | bytes 17301512 | tf_op jit(solution)/shard_map/ppermute | solution.py:30
  230.9 253.3 %reduce-scatter.5.cloned.1.call-start = ((), (), s32[]{:S(2)}) async-start(), calls=%async_computation.8 | async-start | bytes 3932160 | tf_op jit(solution)/shard_map/reduce_scatter | solution.py:78
  231.4 14.3 %collective-permute-start.31 = (bf16[128,2048]{1,0:T(8,128)(2,1)S(1)}, bf16[128,2048]{1,0:T(8,128)(2,1)S(1)}, u32[]{:S(2)}, u32[]{:S(2)}) collective-permute-start(bf16[128,2048]{1,0:T(8,128)(2,1)S(1)} %collective-permute-done.27.refs_2_), channel_id=1, source_target_pairs={{0,4},{2,6},{4,0},{6,2},{1,5},{3,7},{5,1},{7,3},{8,12},{10,14},{12... | collective-permute-start | bytes 1572872 | tf_op jit(solution)/shard_map/ppermute | solution.py:22
  232.9 14.0 %collective-permute-start.32 = (bf16[128,2048]{1,0:T(8,128)(2,1)S(1)}, bf16[128,2048]{1,0:T(8,128)(2,1)S(1)}, u32[]{:S(2)}, u32[]{:S(2)}) collective-permute-start(bf16[128,2048]{1,0:T(8,128)(2,1)S(1)} %collective-permute-done.28.refs_5_), channel_id=1, source_target_pairs={{0,2},{2,0},{4,6},{6,4},{1,3},{3,1},{5,7},{7,5},{8,10},{10,8},{12,... | collective-permute-start | bytes 1572872 | tf_op jit(solution)/shard_map/ppermute | solution.py:18
  247.0 28.0 %collective-permute-start.36 = (bf16[128,2048]{1,0:T(8,128)(2,1)S(1)}, bf16[128,2048]{1,0:T(8,128)(2,1)S(1)}, u32[]{:S(2)}, u32[]{:S(2)}) collective-permute-start(bf16[128,2048]{1,0:T(8,128)(2,1)S(1)} %get-tuple-element.260.refs_1_.refs_8_), channel_id=1, source_target_pairs={{0,2},{2,0},{4,6},{6,4},{1,3},{3,1},{5,7},{7,5},{8,10},{10,8},{12,... | collective-permute-start | bytes 1572872 | tf_op jit(solution)/shard_map/ppermute | solution.py:18
  248.4 26.6 %collective-permute-start.37 = (bf16[128,2048]{1,0:T(8,128)(2,1)S(1)}, bf16[128,2048]{1,0:T(8,128)(2,1)S(1)}, u32[]{:S(2)}, u32[]{:S(2)}) collective-permute-start(bf16[128,2048]{1,0:T(8,128)(2,1)S(1)} %get-tuple-element.261.refs_0_.refs_7_), channel_id=1, source_target_pairs={{0,4},{2,6},{4,0},{6,2},{1,5},{3,7},{5,1},{7,3},{8,12},{10,14},{12... | collective-permute-start | bytes 1572872 | tf_op jit(solution)/shard_map/ppermute | solution.py:22
  249.0 26.1 %collective-permute-start.34 = (bf16[128,2048]{1,0:T(8,128)(2,1)S(1)}, bf16[128,2048]{1,0:T(8,128)(2,1)S(1)}, u32[]{:S(2)}, u32[]{:S(2)}) collective-permute-start(bf16[128,2048]{1,0:T(8,128)(2,1)S(1)} %get-tuple-element.261.refs_0_.refs_7_), channel_id=1, source_target_pairs={{0,2},{2,0},{4,6},{6,4},{1,3},{3,1},{5,7},{7,5},{8,10},{10,8},{12,... | collective-permute-start | bytes 1572872 | tf_op jit(solution)/shard_map/ppermute | solution.py:18
  249.5 25.5 %collective-permute-start.35 = (bf16[128,2048]{1,0:T(8,128)(2,1)S(1)}, bf16[128,2048]{1,0:T(8,128)(2,1)S(1)}, u32[]{:S(2)}, u32[]{:S(2)}) collective-permute-start(bf16[128,2048]{1,0:T(8,128)(2,1)S(1)} %get-tuple-element.260.refs_1_.refs_8_), channel_id=1, source_target_pairs={{0,4},{2,6},{4,0},{6,2},{1,5},{3,7},{5,1},{7,3},{8,12},{10,14},{12... | collective-permute-start | bytes 1572872 | tf_op jit(solution)/shard_map/ppermute | solution.py:22
  302.4 23.5 %collective-permute-start.40 = (bf16[2048,768]{1,0:T(8,128)(2,1)}, bf16[2048,768]{1,0:T(8,128)(2,1)S(1)}, u32[]{:S(2)}, u32[]{:S(2)}) collective-permute-start(bf16[2048,768]{1,0:T(8,128)(2,1)} %all-gather.11.cloned.1.call-done.refs_6_.refs_8_.refs_1_), channel_id=1, source_target_pairs={{0,1},{1,0},{2,3},{3,2},{4,5},{5,4},{6,7},{7,6},{8,9},{9,8},{10,11... | collective-permute-start | bytes 9437192 | tf_op jit(solution)/shard_map/ppermute | solution.py:30
  302.4 14.3 %collective-permute-start.38 = (bf16[128,2048]{1,0:T(8,128)(2,1)S(1)}, bf16[128,2048]{1,0:T(8,128)(2,1)S(1)}, u32[]{:S(2)}, u32[]{:S(2)}) collective-permute-start(bf16[128,2048]{1,0:T(8,128)(2,1)S(1)} %collective-permute-done.34.refs_2_.refs_0_), channel_id=1, source_target_pairs={{0,4},{2,6},{4,0},{6,2},{1,5},{3,7},{5,1},{7,3},{8,12},{10,14},{12... | collective-permute-start | bytes 1572872 | tf_op jit(solution)/shard_map/ppermute | solution.py:22
  303.9 14.1 %collective-permute-start.39 = (bf16[128,2048]{1,0:T(8,128)(2,1)S(1)}, bf16[128,2048]{1,0:T(8,128)(2,1)S(1)}, u32[]{:S(2)}, u32[]{:S(2)}) collective-permute-start(bf16[128,2048]{1,0:T(8,128)(2,1)S(1)} %collective-permute-done.35.refs_5_.refs_3_), channel_id=1, source_target_pairs={{0,2},{2,0},{4,6},{6,4},{1,3},{3,1},{5,7},{7,5},{8,10},{10,8},{12,... | collective-permute-start | bytes 1572872 | tf_op jit(solution)/shard_map/ppermute | solution.py:18
  325.8 53.7 %collective-permute-start.60 = (bf16[2048,768]{1,0:T(8,128)(2,1)}, bf16[2048,768]{1,0:T(8,128)(2,1)S(1)}, u32[]{:S(2)}, u32[]{:S(2)}) collective-permute-start(bf16[2048,768]{1,0:T(8,128)(2,1)} %shard_map.256), channel_id=1, source_target_pairs={{0,1},{1,0},{2,3},{3,2},{4,5},{5,4},{6,7},{7,6},{8,9},{9,8},{10,11... | collective-permute-start | bytes 9437192 | tf_op jit(solution)/shard_map/ppermute | solution.py:30
  341.2 48.2 %collective-permute-start.41 = (bf16[128,2048]{1,0:T(8,128)(2,1)}, bf16[128,2048]{1,0:T(8,128)(2,1)S(1)}, u32[]{:S(2)}, u32[]{:S(2)}) collective-permute-start(bf16[128,2048]{1,0:T(8,128)(2,1)} %get-tuple-element.269), channel_id=1, source_target_pairs={{0,2},{2,0},{4,6},{6,4},{1,3},{3,1},{5,7},{7,5},{8,10},{10,8},{12,... | collective-permute-start | bytes 1572872 | tf_op jit(solution)/shard_map/ppermute | solution.py:18
  362.7 26.7 %collective-permute-start.43 = (bf16[128,2048]{1,0:T(8,128)(2,1)}, bf16[128,2048]{1,0:T(8,128)(2,1)}, u32[]{:S(2)}, u32[]{:S(2)}) collective-permute-start(bf16[128,2048]{1,0:T(8,128)(2,1)} %get-tuple-element.271), channel_id=1, source_target_pairs={{0,2},{2,0},{4,6},{6,4},{1,3},{3,1},{5,7},{7,5},{8,10},{10,8},{12,... | collective-permute-start | bytes 1572872 | tf_op jit(solution)/shard_map/ppermute | solution.py:18
  363.3 26.1 %collective-permute-start.44 = (bf16[128,2048]{1,0:T(8,128)(2,1)}, bf16[128,2048]{1,0:T(8,128)(2,1)}, u32[]{:S(2)}, u32[]{:S(2)}) collective-permute-start(bf16[128,2048]{1,0:T(8,128)(2,1)} %get-tuple-element.276), channel_id=1, source_target_pairs={{0,4},{2,6},{4,0},{6,2},{1,5},{3,7},{5,1},{7,3},{8,12},{10,14},{12... | collective-permute-start | bytes 1572872 | tf_op jit(solution)/shard_map/ppermute | solution.py:22
  364.3 25.1 %collective-permute-start.42 = (bf16[128,2048]{1,0:T(8,128)(2,1)}, bf16[128,2048]{1,0:T(8,128)(2,1)S(1)}, u32[]{:S(2)}, u32[]{:S(2)}) collective-permute-start(bf16[128,2048]{1,0:T(8,128)(2,1)} %get-tuple-element.275), channel_id=1, source_target_pairs={{0,4},{2,6},{4,0},{6,2},{1,5},{3,7},{5,1},{7,3},{8,12},{10,14},{12... | collective-permute-start | bytes 1572872 | tf_op jit(solution)/shard_map/ppermute | solution.py:22
  389.3 168.2 %reduce-scatter.7.cloned.1.call-start = ((), (), s32[]{:S(2)}) async-start(), calls=%async_computation.9 | async-start | bytes 7208960 | tf_op jit(solution)/shard_map/reduce_scatter | solution.py:78
  403.1 25.3 %collective-permute-start.47 = (bf16[128,2048]{1,0:T(8,128)(2,1)S(1)}, bf16[128,2048]{1,0:T(8,128)(2,1)S(1)}, u32[]{:S(2)}, u32[]{:S(2)}) collective-permute-start(bf16[128,2048]{1,0:T(8,128)(2,1)S(1)} %copy-done.67), channel_id=1, source_target_pairs={{0,4},{2,6},{4,0},{6,2},{1,5},{3,7},{5,1},{7,3},{8,12},{10,14},{12... | collective-permute-start | bytes 1572872 | tf_op jit(solution)/shard_map/ppermute | solution.py:22
  403.9 24.6 %collective-permute-start.46 = (bf16[128,2048]{1,0:T(8,128)(2,1)S(1)}, bf16[128,2048]{1,0:T(8,128)(2,1)S(1)}, u32[]{:S(2)}, u32[]{:S(2)}) collective-permute-start(bf16[128,2048]{1,0:T(8,128)(2,1)S(1)} %add_convert_fusion.7), channel_id=1, source_target_pairs={{0,2},{2,0},{4,6},{6,4},{1,3},{3,1},{5,7},{7,5},{8,10},{10,8},{12,... | collective-permute-start | bytes 1572872 | tf_op jit(solution)/shard_map/ppermute | solution.py:18
  427.9 178.3 %reduce-scatter.9.cloned.1.call-start = ((), (), s32[]{:S(2)}) async-start(), calls=%async_computation.10 | async-start | bytes 2621440 | tf_op jit(solution)/shard_map/reduce_scatter | solution.py:78
  436.1 15.7 %collective-permute-start.50 = (bf16[128,2176]{1,0:T(8,128)(2,1)}, bf16[128,2176]{1,0:T(8,128)(2,1)S(1)}, u32[]{:S(2)}, u32[]{:S(2)}) collective-permute-start(bf16[128,2176]{1,0:T(8,128)(2,1)} %get-tuple-element.302.refs_1_), channel_id=1, source_target_pairs={{0,2},{2,0},{4,6},{6,4},{1,3},{3,1},{5,7},{7,5},{8,10},{10,8},{12,... | collective-permute-start | bytes 1671176 | tf_op jit(solution)/shard_map/ppermute | solution.py:18
  437.6 15.7 %collective-permute-start.51 = (bf16[128,2176]{1,0:T(8,128)(2,1)}, bf16[128,2176]{1,0:T(8,128)(2,1)S(1)}, u32[]{:S(2)}, u32[]{:S(2)}) collective-permute-start(bf16[128,2176]{1,0:T(8,128)(2,1)} %get-tuple-element.303.refs_0_), channel_id=1, source_target_pairs={{0,4},{2,6},{4,0},{6,2},{1,5},{3,7},{5,1},{7,3},{8,12},{10,14},{12... | collective-permute-start | bytes 1671176 | tf_op jit(solution)/shard_map/ppermute | solution.py:22
  438.3 24.6 %collective-permute-start.48 = (bf16[128,2176]{1,0:T(8,128)(2,1)}, bf16[128,2176]{1,0:T(8,128)(2,1)S(1)}, u32[]{:S(2)}, u32[]{:S(2)}) collective-permute-start(bf16[128,2176]{1,0:T(8,128)(2,1)} %get-tuple-element.303.refs_0_), channel_id=1, source_target_pairs={{0,2},{2,0},{4,6},{6,4},{1,3},{3,1},{5,7},{7,5},{8,10},{10,8},{12,... | collective-permute-start | bytes 1671176 | tf_op jit(solution)/shard_map/ppermute | solution.py:18
  438.9 25.2 %collective-permute-start.49 = (bf16[128,2176]{1,0:T(8,128)(2,1)}, bf16[128,2176]{1,0:T(8,128)(2,1)S(1)}, u32[]{:S(2)}, u32[]{:S(2)}) collective-permute-start(bf16[128,2176]{1,0:T(8,128)(2,1)} %get-tuple-element.302.refs_1_), channel_id=1, source_target_pairs={{0,4},{2,6},{4,0},{6,2},{1,5},{3,7},{5,1},{7,3},{8,12},{10,14},{12... | collective-permute-start | bytes 1671176 | tf_op jit(solution)/shard_map/ppermute | solution.py:22
  464.1 20.2 %collective-permute-start.52 = (bf16[128,2176]{1,0:T(8,128)(2,1)S(1)}, bf16[128,2176]{1,0:T(8,128)(2,1)S(1)}, u32[]{:S(2)}, u32[]{:S(2)}) collective-permute-start(bf16[128,2176]{1,0:T(8,128)(2,1)S(1)} %collective-permute-done.48.refs_2_), channel_id=1, source_target_pairs={{0,4},{2,6},{4,0},{6,2},{1,5},{3,7},{5,1},{7,3},{8,12},{10,14},{12... | collective-permute-start | bytes 1671176 | tf_op jit(solution)/shard_map/ppermute | solution.py:22
  464.8 19.5 %collective-permute-start.53 = (bf16[128,2176]{1,0:T(8,128)(2,1)S(1)}, bf16[128,2176]{1,0:T(8,128)(2,1)S(1)}, u32[]{:S(2)}, u32[]{:S(2)}) collective-permute-start(bf16[128,2176]{1,0:T(8,128)(2,1)S(1)} %collective-permute-done.49.refs_5_), channel_id=1, source_target_pairs={{0,2},{2,0},{4,6},{6,4},{1,3},{3,1},{5,7},{7,5},{8,10},{10,8},{12,... | collective-permute-start | bytes 1671176 | tf_op jit(solution)/shard_map/ppermute | solution.py:18
  517.2 14.9 %collective-permute-start.54 = (bf16[128,2048]{1,0:T(8,128)(2,1)S(1)}, bf16[128,2048]{1,0:T(8,128)(2,1)S(1)}, u32[]{:S(2)}, u32[]{:S(2)}) collective-permute-start(bf16[128,2048]{1,0:T(8,128)(2,1)S(1)} %copy-done.62), channel_id=1, source_target_pairs={{0,2},{2,0},{4,6},{6,4},{1,3},{3,1},{5,7},{7,5},{8,10},{10,8},{12,... | collective-permute-start | bytes 1572872 | tf_op jit(solution)/shard_map/ppermute | solution.py:18
  518.8 14.9 %collective-permute-start.55 = (bf16[128,2048]{1,0:T(8,128)(2,1)S(1)}, bf16[128,2048]{1,0:T(8,128)(2,1)S(1)}, u32[]{:S(2)}, u32[]{:S(2)}) collective-permute-start(bf16[128,2048]{1,0:T(8,128)(2,1)S(1)} %copy-done.90), channel_id=1, source_target_pairs={{0,4},{2,6},{4,0},{6,2},{1,5},{3,7},{5,1},{7,3},{8,12},{10,14},{12... | collective-permute-start | bytes 1572872 | tf_op jit(solution)/shard_map/ppermute | solution.py:22
  520.1 20.9 %collective-permute-start.56 = (bf16[128,2048]{1,0:T(8,128)(2,1)S(1)}, bf16[128,2048]{1,0:T(8,128)(2,1)S(1)}, u32[]{:S(2)}, u32[]{:S(2)}) collective-permute-start(bf16[128,2048]{1,0:T(8,128)(2,1)S(1)} %copy-done.89), channel_id=1, source_target_pairs={{0,2},{2,0},{4,6},{6,4},{1,3},{3,1},{5,7},{7,5},{8,10},{10,8},{12,... | collective-permute-start | bytes 1572872 | tf_op jit(solution)/shard_map/ppermute | solution.py:18
  520.7 21.4 %collective-permute-start.57 = (bf16[128,2048]{1,0:T(8,128)(2,1)S(1)}, bf16[128,2048]{1,0:T(8,128)(2,1)S(1)}, u32[]{:S(2)}, u32[]{:S(2)}) collective-permute-start(bf16[128,2048]{1,0:T(8,128)(2,1)S(1)} %copy-done.88), channel_id=1, source_target_pairs={{0,4},{2,6},{4,0},{6,2},{1,5},{3,7},{5,1},{7,3},{8,12},{10,14},{12... | collective-permute-start | bytes 1572872 | tf_op jit(solution)/shard_map/ppermute | solution.py:22
  522.8 31.9 %collective-permute-start.63 = (bf16[2048,512]{1,0:T(8,128)(2,1)S(1)}, bf16[2048,512]{1,0:T(8,128)(2,1)S(1)}, u32[]{:S(2)}, u32[]{:S(2)}) collective-permute-start(bf16[2048,512]{1,0:T(8,128)(2,1)S(1)} %pad_maximum_fusion.4), channel_id=1, source_target_pairs={{0,1},{1,0},{2,3},{3,2},{4,5},{5,4},{6,7},{7,6},{8,9},{9,8},{10,11... | collective-permute-start | bytes 6291464 | tf_op jit(solution)/shard_map/ppermute | solution.py:30
  557.5 95.3 %reduce-scatter.11.cloned.1.call-start = ((), (), s32[]{:S(2)}) async-start(), calls=%async_computation.11 | async-start | bytes 2621440 | tf_op jit(solution)/shard_map/reduce_scatter | solution.py:78
  591.0 15.2 %collective-permute-start.66 = (bf16[128,2048]{1,0:T(8,128)(2,1)}, bf16[128,2048]{1,0:T(8,128)(2,1)S(1)}, u32[]{:S(2)}, u32[]{:S(2)}) collective-permute-start(bf16[128,2048]{1,0:T(8,128)(2,1)} %get-tuple-element.341), channel_id=1, source_target_pairs={{0,2},{2,0},{4,6},{6,4},{1,3},{3,1},{5,7},{7,5},{8,10},{10,8},{12,... | collective-permute-start | bytes 1572872 | tf_op jit(solution)/shard_map/ppermute | solution.py:18
  591.9 14.3 %collective-permute-start.67 = (bf16[128,2048]{1,0:T(8,128)(2,1)}, bf16[128,2048]{1,0:T(8,128)(2,1)S(1)}, u32[]{:S(2)}, u32[]{:S(2)}) collective-permute-start(bf16[128,2048]{1,0:T(8,128)(2,1)} %get-tuple-element.343), channel_id=1, source_target_pairs={{0,4},{2,6},{4,0},{6,2},{1,5},{3,7},{5,1},{7,3},{8,12},{10,14},{12... | collective-permute-start | bytes 1572872 | tf_op jit(solution)/shard_map/ppermute | solution.py:22
  603.9 13.9 %collective-permute-start.68 = (bf16[128,2048]{1,0:T(8,128)(2,1)}, bf16[128,2048]{1,0:T(8,128)(2,1)S(1)}, u32[]{:S(2)}, u32[]{:S(2)}) collective-permute-start(bf16[128,2048]{1,0:T(8,128)(2,1)} %get-tuple-element.344), channel_id=1, source_target_pairs={{0,2},{2,0},{4,6},{6,4},{1,3},{3,1},{5,7},{7,5},{8,10},{10,8},{12,... | collective-permute-start | bytes 1572872 | tf_op jit(solution)/shard_map/ppermute | solution.py:18
  605.2 13.5 %collective-permute-start.69 = (bf16[128,2048]{1,0:T(8,128)(2,1)}, bf16[128,2048]{1,0:T(8,128)(2,1)S(1)}, u32[]{:S(2)}, u32[]{:S(2)}) collective-permute-start(bf16[128,2048]{1,0:T(8,128)(2,1)} %get-tuple-element.345), channel_id=1, source_target_pairs={{0,4},{2,6},{4,0},{6,2},{1,5},{3,7},{5,1},{7,3},{8,12},{10,14},{12... | collective-permute-start | bytes 1572872 | tf_op jit(solution)/shard_map/ppermute | solution.py:22
  621.1 15.1 %collective-permute-start.71 = (bf16[128,2048]{1,0:T(8,128)(2,1)}, bf16[128,2048]{1,0:T(8,128)(2,1)S(1)}, u32[]{:S(2)}, u32[]{:S(2)}) collective-permute-start(bf16[128,2048]{1,0:T(8,128)(2,1)} %add_convert_fusion.2), channel_id=1, source_target_pairs={{0,4},{2,6},{4,0},{6,2},{1,5},{3,7},{5,1},{7,3},{8,12},{10,14},{12... | collective-permute-start | bytes 1572872 | tf_op jit(solution)/shard_map/ppermute | solution.py:22
  623.3 14.9 %collective-permute-start.70 = (bf16[128,2048]{1,0:T(8,128)(2,1)S(1)}, bf16[128,2048]{1,0:T(8,128)(2,1)S(1)}, u32[]{:S(2)}, u32[]{:S(2)}) collective-permute-start(bf16[128,2048]{1,0:T(8,128)(2,1)S(1)} %add_convert_fusion.3), channel_id=1, source_target_pairs={{0,2},{2,0},{4,6},{6,4},{1,3},{3,1},{5,7},{7,5},{8,10},{10,8},{12,... | collective-permute-start | bytes 1572872 | tf_op jit(solution)/shard_map/ppermute | solution.py:18
  625.6 30.9 %collective-permute-start.74 = (bf16[128,2176]{1,0:T(8,128)(2,1)}, bf16[128,2176]{1,0:T(8,128)(2,1)}, u32[]{:S(2)}, u32[]{:S(2)}) collective-permute-start(bf16[128,2176]{1,0:T(8,128)(2,1)} %get-tuple-element.360), channel_id=1, source_target_pairs={{0,2},{2,0},{4,6},{6,4},{1,3},{3,1},{5,7},{7,5},{8,10},{10,8},{12,... | collective-permute-start | bytes 1671176 | tf_op jit(solution)/shard_map/ppermute | solution.py:18
  626.8 30.7 %collective-permute-start.75 = (bf16[128,2176]{1,0:T(8,128)(2,1)}, bf16[128,2176]{1,0:T(8,128)(2,1)}, u32[]{:S(2)}, u32[]{:S(2)}) collective-permute-start(bf16[128,2176]{1,0:T(8,128)(2,1)} %get-tuple-element.361), channel_id=1, source_target_pairs={{0,4},{2,6},{4,0},{6,2},{1,5},{3,7},{5,1},{7,3},{8,12},{10,14},{12... | collective-permute-start | bytes 1671176 | tf_op jit(solution)/shard_map/ppermute | solution.py:22
  627.8 33.4 %collective-permute-start.76 = (bf16[128,2176]{1,0:T(8,128)(2,1)}, bf16[128,2176]{1,0:T(8,128)(2,1)}, u32[]{:S(2)}, u32[]{:S(2)}) collective-permute-start(bf16[128,2176]{1,0:T(8,128)(2,1)} %get-tuple-element.362), channel_id=1, source_target_pairs={{0,6},{2,4},{4,2},{6,0},{1,7},{3,5},{5,3},{7,1},{8,14},{10,12},{12... | collective-permute-start | bytes 1671176 | tf_op jit(solution)/shard_map/ppermute | solution.py:26
  645.6 38.9 %collective-permute-start.80 = (f32[256,2048]{1,0:T(8,128)}, f32[256,2048]{1,0:T(8,128)S(1)}, u32[]{:S(2)}, u32[]{:S(2)}) collective-permute-start(f32[256,2048]{1,0:T(8,128)} %bitcast.180), channel_id=1, source_target_pairs={{0,1},{1,0},{2,3},{3,2},{4,5},{5,4},{6,7},{7,6},{8,9},{9,8},{10,11... | collective-permute-start | bytes 6291464 | tf_op jit(solution)/shard_map/ppermute | solution.py:30
  657.5 13.8 %collective-permute-start.79 = (bf16[128,1024]{1,0:T(8,128)(2,1)S(1)}, bf16[128,1024]{1,0:T(8,128)(2,1)}, u32[]{:S(2)}, u32[]{:S(2)}) collective-permute-start(bf16[128,1024]{1,0:T(8,128)(2,1)S(1)} %get-tuple-element.394), channel_id=1, source_target_pairs={{0,6},{2,4},{4,2},{6,0},{1,7},{3,5},{5,3},{7,1},{8,14},{10,12},{12... | collective-permute-start | bytes 786440 | tf_op jit(solution)/shard_map/ppermute | solution.py:26
  661.2 22.1 %collective-permute-start.72 = (bf16[256,1024]{1,0:T(8,128)(2,1)}, bf16[256,1024]{1,0:T(8,128)(2,1)S(1)}, u32[]{:S(2)}, u32[]{:S(2)}) collective-permute-start(bf16[256,1024]{1,0:T(8,128)(2,1)} %get-tuple-element.403), channel_id=1, source_target_pairs={{0,1},{1,0},{2,3},{3,2},{4,5},{5,4},{6,7},{7,6},{8,9},{9,8},{10,11... | collective-permute-start | bytes 1572872 | tf_op jit(solution)/shard_map/ppermute | solution.py:30
  (126 other events, 1278.6 us)
Sparse Core Ops, SparseCore 0:
  28.7 46.2 all-gather.4
  76.5 44.6 all-gather.6
  123.4 105.4 all-gather.8
  231.1 71.3 all-gather.10
  389.5 58.4 reduce-scatter.4
  450.1 102.9 reduce-scatter.6
  557.6 42.1 reduce-scatter.8
  602.8 43.1 reduce-scatter.10
